TPU v7x, 256 devices: a whole 4x4x8 slice. The times are simulated.
256 devices in a mesh: ctx: 32 (over x, z), tp: 8 (over y, core).
Axes of the slice: x: 4, y: 4, z: 8, core: 2. Of those that a mesh axis runs over, the one named last changes fastest.
Arguments:
- queries: bfloat16 [8192, 8192], P('ctx', 'tp'), may hold values from -12 to 12
- keys: bfloat16 [8192, 1024], P('ctx', 'tp'), may hold values from -12 to 12
- values: bfloat16 [8192, 1024], P('ctx', 'tp'), may hold values from -6 to 6
- lengths: int32 [4], replicated, may hold values from 1 to 6144, 8192 in all
- out_weight: bfloat16 [8192, 4096], P('tp'), may hold values from -0.59765625 to 0.59765625
Outputs:
- mixed: bfloat16 [8192, 4096], P('ctx', 'tp')
Inputs may be any that keep to these rules, and one draw needn't show every extreme that they name: The 4 lengths sum to 8192; the longest is exactly 6144.
All inputs are finite; a program needn't handle non-finite values.
Results may differ from a plain program's by a relative error of at most 0.014.
Values may be sent and summed in bfloat16 or wider, within the bound.
No kernel may reach another device: no remote copies, remote signals or barrier semaphores. Data moves between devices by JAX's collectives and lax.ppermute only.
A program may use at most 192 MiB of HBM per device.

v0:
```python
import jax
import jax.numpy as jnp
from jax import lax
from jax.sharding import PartitionSpec as P

QH = 64
KVH = 8
HD = 128


def on_device(queries, keys, values, lengths, out_weight):
    devices = lax.axis_size("ctx")
    own_index = lax.axis_index("ctx")
    rows_dev = queries.shape[0]
    half_rows = rows_dev // 2
    group_size = QH // KVH
    kv_local = keys.shape[1] // HD
    score_scale = HD ** (-0.5)
    doc_ends = jnp.cumsum(lengths)

    def placed(rows):
        device = rows // rows_dev
        offset = rows % rows_dev
        return jnp.where(
            offset < half_rows,
            device * half_rows + offset,
            (2 * devices - 1 - device) * half_rows + offset - half_rows,
        )

    def doc_of(places):
        return jnp.sum((places[:, None] >= doc_ends[None, :]).astype(jnp.int32), axis=1)

    local_rows = own_index * rows_dev + jnp.arange(rows_dev, dtype=jnp.int32)
    q_place = placed(local_rows)
    q_doc = doc_of(q_place)
    query_heads = queries.reshape(rows_dev, kv_local, group_size, HD)
    key_piece = lax.all_gather(keys, "ctx", axis=0, tiled=True)
    piece_rows = key_piece.shape[0]
    k_place = placed(jnp.arange(piece_rows, dtype=jnp.int32))
    k_doc = doc_of(k_place)
    allowed = (k_doc[None, :] == q_doc[:, None]) & (k_place[None, :] <= q_place[:, None])
    row_max = jnp.full((rows_dev, kv_local, group_size), -1e30, jnp.float32)
    piece_rows = key_piece.shape[0]
    key_heads = key_piece.reshape(piece_rows, kv_local, HD)
    value_heads = lax.all_gather(values, "ctx", axis=0, tiled=True).reshape(
        piece_rows, kv_local, HD
    )
    scores = (
        jnp.einsum("tkgd,pkd->tkgp", query_heads, key_heads, preferred_element_type=jnp.float32)
        * score_scale
    )
    key_mask = allowed[:, None, None, :]
    scores = jnp.where(key_mask, scores, -1e30)
    new_max = jnp.maximum(row_max, jnp.max(scores, axis=3))
    weights = jnp.where(key_mask, jnp.exp(scores - new_max[..., None]), 0.0)
    totals = jnp.sum(weights, axis=3)
    weighted = jnp.einsum(
        "tkgp,pkd->tkgd",
        weights.astype(jnp.bfloat16),
        value_heads,
        preferred_element_type=jnp.float32,
    )
    final = (new_max, totals, weighted)
    row_max, totals, weighted = final
    attended = (
        (weighted / totals[..., None])
        .reshape(rows_dev, kv_local * group_size * HD)
        .astype(jnp.bfloat16)
    )
    terms = jnp.dot(attended, out_weight, preferred_element_type=jnp.float32)
    return lax.psum_scatter(terms.astype(jnp.bfloat16), "tp", scatter_dimension=1, tiled=True)


def solution(mesh):
    return jax.shard_map(
        on_device,
        mesh=mesh,
        in_specs=(P("ctx", "tp"), P("ctx", "tp"), P("ctx", "tp"), P(), P("tp", None)),
        out_specs=P("ctx", "tp"),
        check_vma=False,
    )
```

profile of v0, /device:TPU:6, one launch (start us, length us, event | category | flops | bytes accessed | tf_op | source)
XLA Modules:
  0.0 239.3 jit_solution(11941522823952205930)
XLA Ops:
  6.5 0.0 copy-start
  6.5 0.0 all-gather.3.cloned.1.call-start
  6.5 0.7 all-gather.3.cloned.1.call-update
  7.3 0.0 all-gather.5.cloned.1.call-start
  7.3 1.6 copy.10
  8.9 0.0 all-gather.5.cloned.1.call-update
  8.9 0.0 reduce-scatter.2.cloned.1.call-start
  9.0 0.8 reduce-window.8
  9.8 0.2 convert_reduce_fusion
  10.0 0.1 convert_reduce_fusion.1
  10.1 5.6 %compare_and_fusion = pred[256,8192]{0,1:T(8,128)(4,1)S(1)} fusion(s32[256]{0:T(256)S(1)} %compare_select_fusion, s32[256]{0:T(256)S(1)} %convert_reduce_fusion.1, s32[8192]{0:T(1024)S(1)} %fusion.30, s32[8192]{0:T(1024)S(1)} %convert_reduce_fusion), kind=kLoop, calls=%fused_computation.8 | loop fusion | flops 6291456 | bytes 2164736 | tf_op jit(solution)/shard_map/and | solution.py:41
  15.7 73.7 %all-gather.3.cloned.1.call-done = bf16[8192,128]{1,0:T(8,128)(2,1)} async-done(((bf16[256,128]{1,0:T(8,128)(2,1)}), bf16[8192,128]{1,0:T(8,128)(2,1)}) %all-gather.3.cloned.1.call-update) | async-done | bytes 2097168 | tf_op jit(solution)/shard_map/all_gather | solution.py:37
  89.3 0.0 copy-done
  89.3 25.0 %fusion = (f32[256,8]{0,1:T(8,128)S(1)}, f32[8192,256,8]{1,0,2:T(8,128)}) fusion(pred[256,8192]{0,1:T(8,128)(4,1)S(1)} %compare_and_fusion, bf16[8192,128]{1,0:T(8,128)(2,1)} %all-gather.3.cloned.1.call-done, bf16[256,1024]{1,0:T(8,128)(2,1)S(1)} %copy-done), kind=kOutput, calls=%fused_computation.2 | convolution fusion | flops 4345296896 | bytes 71835648 | tf_op jit(solution)/shard_map/tkgd,pkd->tkgp/dot_general | solution.py:49
  114.3 21.7 %fusion.1 = f32[256,8]{0,1:T(8,128)S(1)} fusion(f32[8192,256,8]{1,0,2:T(8,128)} %get-tuple-element.6, f32[256,8]{0,1:T(8,128)S(1)} %broadcast_maximum_fusion, pred[256,8192]{0,1:T(8,128)(4,1)S(1)} %compare_and_fusion), kind=kLoop, calls=%fused_computation.3 | loop fusion | flops 83884032 | bytes 69222400 | tf_op jit(solution)/shard_map/reduce_sum | solution.py:56
  136.1 29.3 %all-gather.5.cloned.1.call-done = bf16[8192,128]{0,1:T(8,128)(2,1)} async-done(((bf16[256,128]{0,1:T(8,128)(2,1)}), bf16[8192,128]{0,1:T(8,128)(2,1)}) %all-gather.5.cloned.1.call-update) | async-done | bytes 2097168 | tf_op jit(solution)/shard_map/all_gather | solution.py:45
  165.4 24.7 %divide_convert_fusion = bf16[1,128,256,8]{2,1,3,0:T(8,128)(2,1)S(1)} fusion(f32[8192,256,8]{1,0,2:T(8,128)} %get-tuple-element.6, f32[256,8]{0,1:T(8,128)S(1)} %broadcast_maximum_fusion, pred[256,8192]{0,1:T(8,128)(4,1)S(1)} %compare_and_fusion, bf16[8192,128]{0,1:T(8,128)(2,1)} %all-gather.5.cloned.1.call-done, f32[256,8]{0,1:T(8,128)S(1)} %fusion.1), kind=kOutput, calls=%fused_computation.14 | convolution fusion | flops 4379377664 | bytes 71843840 | tf_op jit(solution)/shard_map/tkgp,pkd->tkgd/dot_general | solution.py:57
  190.1 7.1 %convolution_convert_fusion = bf16[256,4096]{1,0:T(8,128)(2,1)} fusion(bf16[256,1024]{0,1:T(8,128)(2,1)S(1)} %bitcast.60, bf16[1024,4096]{1,0:T(8,128)(2,1)} %param.9), kind=kOutput, calls=%fused_computation.9 | convolution fusion | flops 2148532224 | bytes 11010048 | tf_op jit(solution)/shard_map/dot_general | solution.py:70
  197.2 0.0 reduce-scatter.2.cloned.1.call-update
  197.2 35.5 %reduce-scatter.2.cloned.1.call-done = bf16[256,512]{1,0:T(8,128)(2,1)} async-done(((bf16[256,4096]{1,0:T(8,128)(2,1)}), bf16[256,512]{1,0:T(8,128)(2,1)}) %reduce-scatter.2.cloned.1.call-update) | async-done | bytes 262160 | tf_op jit(solution)/shard_map/reduce_scatter | solution.py:71
  (3 shorter events, 0.0 us)
Async XLA Ops:
  6.5 82.8 %copy-start = (bf16[256,1024]{1,0:T(8,128)(2,1)S(1)}, bf16[256,1024]{1,0:T(8,128)(2,1)}, u32[]{:S(2)}) copy-start(bf16[256,1024]{1,0:T(8,128)(2,1)} %param.5) | copy-start | bytes 1572868
  6.5 82.8 %all-gather.3.cloned.1.call-start = ((), (), s32[]{:S(2)}) async-start(), calls=%async_computation.1 | async-start | bytes 2162688 | tf_op jit(solution)/shard_map/all_gather | solution.py:37
  7.3 158.2 %all-gather.5.cloned.1.call-start = ((), (), s32[]{:S(2)}) async-start(), calls=%async_computation.2 | async-start | bytes 2162688 | tf_op jit(solution)/shard_map/all_gather | solution.py:45
  8.9 223.8 %reduce-scatter.2.cloned.1.call-start = ((), (), s32[]{:S(2)}) async-start(), calls=%async_computation.3 | async-start | bytes 2359296 | tf_op jit(solution)/shard_map/reduce_scatter | solution.py:71
Sparse Core Ops, SparseCore 0:
  10.0 79.3 all-gather.2
  91.8 73.5 all-gather.4
  197.4 35.3 reduce-scatter.1
where the time goes:
time: 240 us; the launch traced here: 239 us
  waiting for transfers between devices  139 us (58%)
  matrix products  56.8 us (24%)
  other arithmetic  28.4 us (12%)
  between operations  13.2 us (6%)
    all_gather x1, waiting for transfers between devices, on_device(): key_piece = lax.all_gather(keys, 'ctx', axis=0, tiled=True)  73.7 us
    reduce_scatter x1, waiting for transfers between devices, on_device(): lax.psum_scatter(terms.astype(jnp.bfloat16), 'tp', scatter_dimension=1, t...  35.5 us
    all_gather x1, waiting for transfers between devices, on_device(): lax.all_gather(values, 'ctx', axis=0, tiled=True)  29.3 us
    dot_general x1, matrix products, on_device(): jnp.einsum('tkgd,pkd->tkgp', query_heads, key_heads, preferred_element_ty...  25 us
    dot_general x1, matrix products, on_device(): jnp.einsum('tkgp,pkd->tkgd', weights.astype(jnp.bfloat16), value_heads, p...  24.7 us
    reduce_sum x1, other arithmetic, on_device(): totals = jnp.sum(weights, axis=3)  21.7 us
    dot_general x1, matrix products, on_device(): terms = jnp.dot(attended, out_weight, preferred_element_type=jnp.float32)  7.12 us
    and x1, other arithmetic, on_device(): (k_doc[None, :] == q_doc[:, None]) & (k_place[None, :] <= q_place[:, None])  5.59 us
  transfers between devices with their start and end apart: 3, of which 3 were waited for; matrix products, arithmetic and copies ran while one was open for 23% of the time, Pallas kernels for 0%

commit v1 on v0

v1 whole, which is shorter than its diff:
```python
import jax
import jax.numpy as jnp
from jax import lax
from jax.experimental import pallas as pl
from jax.experimental.pallas import tpu as pltpu
from jax.sharding import PartitionSpec as P

HD = 128
NX, NZ = 4, 8
NY = 4
CHUNK = 512
XROWS = 96
NEG = -1e30
SCALE2 = (HD ** -0.5) * 1.4426950408889634


def from_x(k):
    return [(((x + k) % NX) * NZ + z, x * NZ + z) for x in range(NX) for z in range(NZ)]


def from_z(k):
    return [(x * NZ + (z + k) % NZ, x * NZ + z) for x in range(NX) for z in range(NZ)]


def from_y(k):
    return [(((y + k) % NY) * 2 + c, y * 2 + c) for y in range(NY) for c in range(2)]


CORES = [(y * 2 + c, y * 2 + 1 - c) for y in range(NY) for c in range(2)]


def ctx(a, perm):
    return lax.ppermute(a, "ctx", perm)


def round_z(a):
    half = a.shape[0] // 2
    up1, up2 = ctx(a, from_z(1)), ctx(a, from_z(2))
    down1, down2 = ctx(a, from_z(-1)), ctx(a, from_z(-2))
    up3, down3 = ctx(up2, from_z(1)), ctx(down2, from_z(-1))
    mid = [ctx(up2[:half], from_z(2)), ctx(down2[half:], from_z(-2))]
    return [a], [up1], [up2], [up3], mid, [down3], [down2], [down1]


def attend_and_project(len_ref, q_ref, w_hbm, *rest):
    narrow, wide = rest[:9], rest[9:13]
    mine_ref, other_ref, kv, w, att, acc, top, kv_sem, w_sem = rest[13:]
    me = lax.axis_index("ctx")
    tp = lax.axis_index("tp")
    mx, mz = me // NZ, me % NZ
    my, mc = tp // 2, tp % 2
    blocks = 2 * NX * NZ
    half = kv.shape[0] // blocks

    def source(kx, kz):
        return ((mx + kx) % NX) * NZ + (mz + kz) % NZ

    def bring(src, start, rows, at):
        pltpu.make_async_copy(
            src.at[pl.ds(start, rows), :],
            kv.at[pl.ds(pl.multiple_of(at, 16), rows), :],
            kv_sem,
        ).start()

    low = half - XROWS
    for kz in range(NZ):
        for kx in range(NX):
            at = source(kx, kz) * half
            if kz < 4:
                bring(narrow[kz], kx * XROWS, XROWS, at)
            elif kz == 4:
                bring(narrow[4 + kx // 2], (kx % 2) * XROWS, XROWS, at)
            else:
                bring(narrow[kz + 1], kx * XROWS, XROWS, at)
            first = kz * (low + half)
            bring(wide[kx], first, low, at + XROWS)
            bring(wide[kx], first + low, half, (blocks - 1) * half - at)
    w_copy = pltpu.make_async_copy(w_hbm, w, w_sem)
    w_copy.start()

    ends = []
    total = 0
    for i in range(4):
        total = total + len_ref[i]
        ends.append(total)

    def begins(p):
        start = jnp.zeros_like(p)
        for e in ends:
            start = jnp.maximum(start, jnp.where(p >= e, e, 0))
        return start

    pltpu.make_async_copy(kv, kv, kv_sem).wait()
    ones = jnp.ones((CHUNK, HD), jnp.bfloat16)

    def rows_of(h, carry):
        block = jnp.where(h == 0, me, blocks - 1 - me)
        q0 = block * half
        last_start = begins(q0 + half - 1)
        acc[...] = jnp.zeros_like(acc)
        top[...] = jnp.full_like(top, NEG)
        q_rows = pl.ds(pl.multiple_of(h * half, half), half)

        def step(j, masked):
            k0 = pl.multiple_of(j * CHUNK, CHUNK)
            k = kv[pl.ds(k0, CHUNK), :HD]
            v = jnp.concatenate([kv[pl.ds(k0, CHUNK), HD:], ones], axis=1)
            if masked:
                kp = k0 + lax.broadcasted_iota(jnp.int32, (half, CHUNK), 1)
                qp = q0 + lax.broadcasted_iota(jnp.int32, (half, CHUNK), 0)
                ok = (kp <= qp) & (kp >= begins(qp))
            for g in range(8):
                rows = slice(g * half, (g + 1) * half)
                s = lax.dot_general(
                    q_ref[q_rows, g * HD : (g + 1) * HD],
                    k,
                    (((1,), (1,)), ((), ())),
                    preferred_element_type=jnp.float32,
                )
                if masked:
                    s = jnp.where(ok, s, NEG)
                old = top[rows, :]
                new = jnp.maximum(old, jnp.max(s, axis=1, keepdims=True))
                p = jnp.exp2((s - jnp.tile(new, (1, CHUNK // HD))) * SCALE2)
                o = jnp.dot(p.astype(jnp.bfloat16), v, preferred_element_type=jnp.float32)
                alpha = jnp.exp2((old - new) * SCALE2)
                acc[rows, :] = acc[rows, :] * jnp.tile(alpha, (1, 2)) + o
                top[rows, :] = new

        def one(j, c):
            whole = (j * CHUNK >= last_start) & (j * CHUNK + CHUNK - 1 <= q0)
            pl.when(whole)(lambda: step(j, False))
            pl.when(jnp.logical_not(whole))(lambda: step(j, True))
            return c

        lax.fori_loop(begins(q0) // CHUNK, (q0 + half - 1) // CHUNK + 1, one, 0)
        for g in range(8):
            rows = slice(g * half, (g + 1) * half)
            att[q_rows, g * HD : (g + 1) * HD] = (acc[rows, :HD] / acc[rows, HD:]).astype(
                jnp.bfloat16
            )
        return carry

    lax.fori_loop(0, 2, rows_of, 0)
    w_copy.wait()
    width = mine_ref.shape[2]
    for k in range(NY):
        for ref, parity in ((mine_ref, mc), (other_ref, 1 - mc)):
            col = pl.multiple_of((((my + k) % NY) * 2 + parity) * width, width)
            ref[k] = jnp.dot(
                att[...], w[:, pl.ds(col, width)], preferred_element_type=jnp.float32
            ).astype(jnp.bfloat16)


def on_device(queries, keys, values, lengths, out_weight):
    tokens = queries.shape[0]
    with jax.named_scope("gather_keys_values"):
        kv = jnp.concatenate([keys, values], axis=1)
        a, b = kv[:XROWS], kv[XROWS:]
        a4 = jnp.concatenate([a] + [ctx(a, from_x(k)) for k in (1, 2, 3)], axis=0)
        narrow = [p for part in round_z(a4) for p in part]
        b8 = jnp.concatenate([p for part in round_z(b) for p in part], axis=0)
        wide = [b8] + [ctx(b8, from_x(k)) for k in (1, 2, 3)]
    any_spec = pl.BlockSpec(memory_space=pl.ANY)
    vmem = pl.BlockSpec(memory_space=pltpu.VMEM)
    width = out_weight.shape[1] // (2 * NY)
    kv_rows = 32 * tokens
    with jax.named_scope("attend_and_project"):
        mine, other = pl.pallas_call(
            attend_and_project,
            out_shape=[jax.ShapeDtypeStruct((NY, tokens, width), jnp.bfloat16)] * 2,
            in_specs=[pl.BlockSpec(memory_space=pltpu.SMEM), vmem] + [any_spec] * 14,
            out_specs=[vmem, vmem],
            scratch_shapes=[
                pltpu.VMEM((kv_rows, 2 * HD), jnp.bfloat16),
                pltpu.VMEM(out_weight.shape, jnp.bfloat16),
                pltpu.VMEM((tokens, queries.shape[1]), jnp.bfloat16),
                pltpu.VMEM((8 * tokens // 2, 2 * HD), jnp.float32),
                pltpu.VMEM((8 * tokens // 2, HD), jnp.float32),
                pltpu.SemaphoreType.DMA,
                pltpu.SemaphoreType.DMA,
            ],
            compiler_params=pltpu.CompilerParams(vmem_limit_bytes=40 * 2**20),
            cost_estimate=pl.CostEstimate(
                flops=6_600_000_000, bytes_accessed=15 * 2**20, transcendentals=9_000_000
            ),
        )(lengths, queries, out_weight, *narrow, *wide)
    with jax.named_scope("sum_over_heads"):
        theirs = lax.ppermute(other, "tp", CORES)

        def pair(k):
            return (mine[k].astype(jnp.float32) + theirs[k].astype(jnp.float32)).astype(jnp.bfloat16)

        out = mine[0].astype(jnp.float32) + theirs[0].astype(jnp.float32)
        for k in (1, 2, 3):
            out = out + lax.ppermute(pair(k), "tp", from_y(-k)).astype(jnp.float32)
        return out.astype(jnp.bfloat16)


def solution(mesh):
    return jax.shard_map(
        on_device,
        mesh=mesh,
        in_specs=(P("ctx", "tp"), P("ctx", "tp"), P("ctx", "tp"), P(), P("tp", None)),
        out_specs=P("ctx", "tp"),
        check_vma=False,
    )
```

time: 240 us -> 116 us (0.48)
  waiting for transfers between devices: 139 us -> 41.2 us
  matrix products: 56.8 us -> 0 us
  starting transfers between devices: 0.08 us -> 45.4 us
  other arithmetic: 28.4 us -> 1.1 us
  Pallas kernels: 0 us -> 25.7 us
  between operations: 13.2 us -> 0.1 us
    all_gather x2 -> x0, waiting for transfers between devices: 103 us -> none  [the longest x1 73.7 us: on_device(): key_piece = lax.all_gather(keys, 'ctx', axis=0, tiled=True)]
    dot_general x3 -> x0, matrix products: 56.8 us -> none  [the longest x1 25 us: on_device(): jnp.einsum('tkgd,pkd->tkgp', query_heads, key_heads, preferred_element_ty...]
    ppermute x0 -> x26, starting transfers between devices: none -> 45.4 us  [the longest x22 40 us: ctx(): return lax.ppermute(a, 'ctx', perm)]
    ppermute x0 -> x26, waiting for transfers between devices: none -> 41.2 us  [the longest x22 27.3 us: ctx(): return lax.ppermute(a, 'ctx', perm)]
    reduce_scatter x1 -> x0, waiting for transfers between devices: 35.5 us -> none  [on_device(): lax.psum_scatter(terms.astype(jnp.bfloat16), 'tp', scatter_dimension=1, t...]
    pallas_call x0 -> x1, Pallas kernels: none -> 25.7 us  [on_device(): pl.pallas_call(attend_and_project, out_shape=[jax.ShapeDtypeStruct((NY, t...]
    reduce_sum x3 -> x0, other arithmetic: 22 us -> none  [the longest x1 21.7 us: on_device(): totals = jnp.sum(weights, axis=3)]
    and x1 -> x0, other arithmetic: 5.59 us -> none  [on_device(): (k_doc[None, :] == q_doc[:, None]) & (k_place[None, :] <= q_place[:, None])]
  transfers between devices with their start and end apart: 3 -> 26, of which waited for: 3 -> 13; matrix products, arithmetic and copies ran while one was open for 23% -> 0% of each run, Pallas kernels for 0% -> 0%
where the time goes in v1:
time: 116 us; the launch traced here: 117 us
  starting transfers between devices  45.4 us (39%)
  waiting for transfers between devices  41.2 us (36%)
  Pallas kernels  25.7 us (22%)
  local copies, waits for them, and re-layouts  3.49 us (3%)
    ppermute x22, starting transfers between devices, ctx(): return lax.ppermute(a, 'ctx', perm)  40 us
    ppermute x22, waiting for transfers between devices, ctx(): return lax.ppermute(a, 'ctx', perm)  27.3 us
    pallas_call x1, Pallas kernels, on_device(): pl.pallas_call(attend_and_project, out_shape=[jax.ShapeDtypeStruct((NY, t...  25.7 us
    ppermute x3, waiting for transfers between devices, on_device(): out = out + lax.ppermute(pair(k), 'tp', from_y(-k)).astype(jnp.float32)  11.2 us
    ppermute x3, starting transfers between devices, on_device(): out = out + lax.ppermute(pair(k), 'tp', from_y(-k)).astype(jnp.float32)  5.29 us
    ppermute x1, waiting for transfers between devices, on_device(): theirs = lax.ppermute(other, 'tp', CORES)  2.65 us
    unnamed x12, local copies, waits for them, and re-layouts  2.59 us
  transfers between devices with their start and end apart: 26, of which 13 were waited for; matrix products, arithmetic and copies ran while one was open for 0% of the time, Pallas kernels for 0%

profile of v1, /device:TPU:6, one launch (start us, length us, event | category | flops | bytes accessed | tf_op | source)
XLA Modules:
  0.0 117.0 jit_solution(9359406070910114331)
XLA Ops:
  1.7 2.3 %collective-permute-start.2 = (bf16[96,256]{1,0:T(8,128)(2,1)S(1)}, bf16[96,256]{1,0:T(8,128)(2,1)S(1)}, u32[]{:S(2)}, u32[]{:S(2)}) collective-permute-start(bf16[96,256]{1,0:T(8,128)(2,1)S(1)} %slice.56), channel_id=1, source_target_pairs={{192,0},{200,8},{208,16},{216,24},{224,32},{232,40},{240,48},{248,... | collective-permute-start | bytes 147464 | tf_op jit(solution)/shard_map/gather_keys_values/ppermute | solution.py:33
  6.7 3.3 %collective-permute-start.15 = (bf16[160,256]{1,0:T(8,128)(2,1)S(1)}, bf16[160,256]{1,0:T(8,128)(2,1)S(1)}, u32[]{:S(2)}, u32[]{:S(2)}) collective-permute-start(bf16[160,256]{1,0:T(8,128)(2,1)S(1)} %get-tuple-element.12), channel_id=1, source_target_pairs={{48,0},{56,8},{0,16},{8,24},{16,32},{24,40},{32,48},{40,56},{112,6... | collective-permute-start | bytes 245768 | tf_op jit(solution)/shard_map/gather_keys_values/ppermute | solution.py:33
  10.0 2.2 %collective-permute-start.12 = (bf16[160,256]{1,0:T(8,128)(2,1)S(1)}, bf16[160,256]{1,0:T(8,128)(2,1)S(1)}, u32[]{:S(2)}, u32[]{:S(2)}) collective-permute-start(bf16[160,256]{1,0:T(8,128)(2,1)S(1)} %get-tuple-element.12), channel_id=1, source_target_pairs={{16,0},{24,8},{32,16},{40,24},{48,32},{56,40},{0,48},{8,56},{80,64... | collective-permute-start | bytes 245768 | tf_op jit(solution)/shard_map/gather_keys_values/ppermute | solution.py:33
  14.8 2.0 %collective-permute-done.15 = bf16[160,256]{1,0:T(8,128)(2,1)S(1)} collective-permute-done((bf16[160,256]{1,0:T(8,128)(2,1)S(1)}, bf16[160,256]{1,0:T(8,128)(2,1)S(1)}, u32[]{:S(2)}, u32[]{:S(2)}) %collective-permute-start.15) | collective-permute-done | bytes 81952 | tf_op jit(solution)/shard_map/gather_keys_values/ppermute | solution.py:33
  18.1 2.8 %collective-permute-start.16 = (bf16[80,256]{1,0:T(8,128)(2,1)S(1)}, bf16[80,256]{1,0:T(8,128)(2,1)S(1)}, u32[]{:S(2)}, u32[]{:S(2)}) collective-permute-start(bf16[80,256]{1,0:T(8,128)(2,1)S(1)} %slice.61), channel_id=1, source_target_pairs={{48,0},{56,8},{0,16},{8,24},{16,32},{24,40},{32,48},{40,56},{112,6... | collective-permute-start | bytes 122888 | tf_op jit(solution)/shard_map/gather_keys_values/ppermute | solution.py:33
  22.8 5.3 %collective-permute-done.13 = bf16[160,256]{1,0:T(8,128)(2,1)S(1)} collective-permute-done((bf16[160,256]{1,0:T(8,128)(2,1)S(1)}, bf16[160,256]{1,0:T(8,128)(2,1)S(1)}, u32[]{:S(2)}, u32[]{:S(2)}) %collective-permute-start.13) | collective-permute-done | bytes 81952 | tf_op jit(solution)/shard_map/gather_keys_values/ppermute | solution.py:33
  28.1 2.9 %collective-permute-start.14 = (bf16[80,256]{1,0:T(8,128)(2,1)S(1)}, bf16[80,256]{1,0:T(8,128)(2,1)S(1)}, u32[]{:S(2)}, u32[]{:S(2)}) collective-permute-start(bf16[80,256]{1,0:T(8,128)(2,1)S(1)} %slice.60), channel_id=1, source_target_pairs={{16,0},{24,8},{32,16},{40,24},{48,32},{56,40},{0,48},{8,56},{80,64... | collective-permute-start | bytes 122888 | tf_op jit(solution)/shard_map/gather_keys_values/ppermute | solution.py:33
  31.1 2.0 %collective-permute-done.14 = bf16[80,256]{1,0:T(8,128)(2,1)S(1)} collective-permute-done((bf16[80,256]{1,0:T(8,128)(2,1)S(1)}, bf16[80,256]{1,0:T(8,128)(2,1)S(1)}, u32[]{:S(2)}, u32[]{:S(2)}) %collective-permute-start.14) | collective-permute-done | bytes 40992 | tf_op jit(solution)/shard_map/gather_keys_values/ppermute | solution.py:33
  35.0 4.0 %collective-permute-done.17 = bf16[160,256]{1,0:T(8,128)(2,1)S(1)} collective-permute-done((bf16[160,256]{1,0:T(8,128)(2,1)S(1)}, bf16[160,256]{1,0:T(8,128)(2,1)S(1)}, u32[]{:S(2)}, u32[]{:S(2)}) %collective-permute-start.17) | collective-permute-done | bytes 81952 | tf_op jit(solution)/shard_map/gather_keys_values/ppermute | solution.py:33
  39.1 2.9 %collective-permute-start.21 = (bf16[1280,256]{1,0:T(8,128)(2,1)S(1)}, bf16[1280,256]{1,0:T(8,128)(2,1)S(1)}, u32[]{:S(2)}, u32[]{:S(2)}) collective-permute-start(bf16[1280,256]{1,0:T(8,128)(2,1)S(1)} %constant_dynamic-update-slice_fusion.2.rest_9_), channel_id=1, source_target_pairs={{192,0},{200,8},{208,16},{216,24},{224,32},{232,40},{240,48},{248,... | collective-permute-start | bytes 1966088 | tf_op jit(solution)/shard_map/gather_keys_values/ppermute | solution.py:33
  44.0 2.6 %collective-permute-start.3 = (bf16[384,256]{1,0:T(8,128)(2,1)S(1)}, bf16[384,256]{1,0:T(8,128)(2,1)S(1)}, u32[]{:S(2)}, u32[]{:S(2)}) collective-permute-start(bf16[384,256]{1,0:T(8,128)(2,1)S(1)} %pad_maximum_fusion.rest_0_), channel_id=1, source_target_pairs={{8,0},{16,8},{24,16},{32,24},{40,32},{48,40},{56,48},{0,56},{72,64... | collective-permute-start | bytes 589832 | tf_op jit(solution)/shard_map/gather_keys_values/ppermute | solution.py:33
  46.7 4.7 %collective-permute-done.10.rest_8_ = bf16[384,256]{1,0:T(8,128)(2,1)S(1)} collective-permute-done((bf16[384,256]{1,0:T(8,128)(2,1)S(1)}, bf16[384,256]{1,0:T(8,128)(2,1)S(1)}, u32[]{:S(2)}, u32[]{:S(2)}) %collective-permute-start.10) | collective-permute-done | bytes 196640 | tf_op jit(solution)/shard_map/gather_keys_values/ppermute | solution.py:33
  51.4 2.1 %collective-permute-start.8 = (bf16[192,256]{1,0:T(8,128)(2,1)S(1)}, bf16[192,256]{1,0:T(8,128)(2,1)S(1)}, u32[]{:S(2)}, u32[]{:S(2)}) collective-permute-start(bf16[192,256]{1,0:T(8,128)(2,1)S(1)} %slice.58), channel_id=1, source_target_pairs={{48,0},{56,8},{0,16},{8,24},{16,32},{24,40},{32,48},{40,56},{112,6... | collective-permute-start | bytes 294920 | tf_op jit(solution)/shard_map/gather_keys_values/ppermute | solution.py:33
  53.5 2.1 %collective-permute-start.6 = (bf16[192,256]{1,0:T(8,128)(2,1)S(1)}, bf16[192,256]{1,0:T(8,128)(2,1)S(1)}, u32[]{:S(2)}, u32[]{:S(2)}) collective-permute-start(bf16[192,256]{1,0:T(8,128)(2,1)S(1)} %slice.57), channel_id=1, source_target_pairs={{16,0},{24,8},{32,16},{40,24},{48,32},{56,40},{0,48},{8,56},{80,64... | collective-permute-start | bytes 294920 | tf_op jit(solution)/shard_map/gather_keys_values/ppermute | solution.py:33
  55.6 2.9 %collective-permute-done.8.rest_5_ = bf16[192,256]{1,0:T(8,128)(2,1)S(1)} collective-permute-done((bf16[192,256]{1,0:T(8,128)(2,1)S(1)}, bf16[192,256]{1,0:T(8,128)(2,1)S(1)}, u32[]{:S(2)}, u32[]{:S(2)}) %collective-permute-start.8) | collective-permute-done | bytes 98336 | tf_op jit(solution)/shard_map/gather_keys_values/ppermute | solution.py:33
  58.5 2.1 %collective-permute-start.9 = (bf16[384,256]{1,0:T(8,128)(2,1)S(1)}, bf16[384,256]{1,0:T(8,128)(2,1)S(1)}, u32[]{:S(2)}, u32[]{:S(2)}) collective-permute-start(bf16[384,256]{1,0:T(8,128)(2,1)S(1)} %collective-permute-done.7.rest_7_), channel_id=1, source_target_pairs={{56,0},{0,8},{8,16},{16,24},{24,32},{32,40},{40,48},{48,56},{120,6... | collective-permute-start | bytes 589832 | tf_op jit(solution)/shard_map/gather_keys_values/ppermute | solution.py:33
  60.6 2.3 %collective-permute-start.5 = (bf16[384,256]{1,0:T(8,128)(2,1)S(1)}, bf16[384,256]{1,0:T(8,128)(2,1)S(1)}, u32[]{:S(2)}, u32[]{:S(2)}) collective-permute-start(bf16[384,256]{1,0:T(8,128)(2,1)S(1)} %collective-permute-done.4.rest_2_), channel_id=1, source_target_pairs={{8,0},{16,8},{24,16},{32,24},{40,32},{48,40},{56,48},{0,56},{72,64... | collective-permute-start | bytes 589832 | tf_op jit(solution)/shard_map/gather_keys_values/ppermute | solution.py:33
  63.0 2.4 %collective-permute-done.9.rest_6_ = bf16[384,256]{1,0:T(8,128)(2,1)S(1)} collective-permute-done((bf16[384,256]{1,0:T(8,128)(2,1)S(1)}, bf16[384,256]{1,0:T(8,128)(2,1)S(1)}, u32[]{:S(2)}, u32[]{:S(2)}) %collective-permute-start.9) | collective-permute-done | bytes 196640 | tf_op jit(solution)/shard_map/gather_keys_values/ppermute | solution.py:33
  66.3 2.9 %collective-permute-done.19.rest_10_ = bf16[1280,256]{1,0:T(8,128)(2,1)S(1)} collective-permute-done((bf16[1280,256]{1,0:T(8,128)(2,1)S(1)}, bf16[1280,256]{1,0:T(8,128)(2,1)S(1)}, u32[]{:S(2)}, u32[]{:S(2)}) %collective-permute-start.19) | collective-permute-done | bytes 655392 | tf_op jit(solution)/shard_map/gather_keys_values/ppermute | solution.py:33
  70.9 25.7 %attend_and_project.1 = (bf16[4,256,512]{2,1,0:T(8,128)(2,1)S(1)}, bf16[4,256,512]{2,1,0:T(8,128)(2,1)S(1)}) custom-call(s32[4]{0:T(128)S(1)} %copy-done.1, bf16[256,1024]{1,0:T(8,128)(2,1)S(1)} %copy-done, bf16[1024,4096]{1,0:T(8,128)(2,1)} %w_hbm.1, bf16[384,256]{1,0:T(8,128)(2,1)S(1)} %pad_maximum_fusion.rest_0_, ...), custom_call_target="tpu_custom_call" | custom-call | flops 6600000000 | bytes 15728640 | tf_op jit(solution)/shard_map/attend_and_project/pallas_call | solution.py:169
  96.7 2.6 %collective-permute-done.22 = bf16[4,256,512]{2,1,0:T(8,128)(2,1)S(1)} collective-permute-done((bf16[4,256,512]{2,1,0:T(8,128)(2,1)S(1)}, bf16[4,256,512]{2,1,0:T(8,128)(2,1)S(1)}, u32[]{:S(2)}, u32[]{:S(2)}) %collective-permute-start.22) | collective-permute-done | bytes 1048608 | tf_op jit(solution)/shard_map/sum_over_heads/ppermute | solution.py:189
  102.9 2.0 %collective-permute-start.24 = (bf16[256,512]{1,0:T(8,128)(2,1)S(1)}, bf16[256,512]{1,0:T(8,128)(2,1)S(1)}, u32[]{:S(2)}, u32[]{:S(2)}) collective-permute-start(bf16[256,512]{1,0:T(8,128)(2,1)S(1)} %get-tuple-element.11), channel_id=1, source_target_pairs={{4,0},{5,1},{6,2},{7,3},{0,4},{1,5},{2,6},{3,7},{12,8},{13,9},{14,... | collective-permute-start | bytes 786440 | tf_op jit(solution)/shard_map/sum_over_heads/ppermute | solution.py:196
  104.9 4.4 %collective-permute-done.23 = bf16[256,512]{1,0:T(8,128)(2,1)S(1)} collective-permute-done((bf16[256,512]{1,0:T(8,128)(2,1)S(1)}, bf16[256,512]{1,0:T(8,128)(2,1)S(1)}, u32[]{:S(2)}, u32[]{:S(2)}) %collective-permute-start.23) | collective-permute-done | bytes 262176 | tf_op jit(solution)/shard_map/sum_over_heads/ppermute | solution.py:196
  109.3 5.0 %collective-permute-done.25 = bf16[256,512]{1,0:T(8,128)(2,1)S(1)} collective-permute-done((bf16[256,512]{1,0:T(8,128)(2,1)S(1)}, bf16[256,512]{1,0:T(8,128)(2,1)S(1)}, u32[]{:S(2)}, u32[]{:S(2)}) %collective-permute-start.25) | collective-permute-done | bytes 262176 | tf_op jit(solution)/shard_map/sum_over_heads/ppermute | solution.py:196
  (52 shorter events, 23.2 us)
Async XLA Ops:
  1.7 8.3 %collective-permute-start.2 = (bf16[96,256]{1,0:T(8,128)(2,1)S(1)}, bf16[96,256]{1,0:T(8,128)(2,1)S(1)}, u32[]{:S(2)}, u32[]{:S(2)}) collective-permute-start(bf16[96,256]{1,0:T(8,128)(2,1)S(1)} %slice.56), channel_id=1, source_target_pairs={{192,0},{200,8},{208,16},{216,24},{224,32},{232,40},{240,48},{248,... | collective-permute-start | bytes 147464 | tf_op jit(solution)/shard_map/gather_keys_values/ppermute | solution.py:33
  4.0 8.2 %collective-permute-start.1 = (bf16[96,256]{1,0:T(8,128)(2,1)S(1)}, bf16[96,256]{1,0:T(8,128)(2,1)S(1)}, u32[]{:S(2)}, u32[]{:S(2)}) collective-permute-start(bf16[96,256]{1,0:T(8,128)(2,1)S(1)} %slice.56), channel_id=1, source_target_pairs={{128,0},{136,8},{144,16},{152,24},{160,32},{168,40},{176,48},{184,... | collective-permute-start | bytes 147464 | tf_op jit(solution)/shard_map/gather_keys_values/ppermute | solution.py:33
  4.7 9.2 %collective-permute-start = (bf16[96,256]{1,0:T(8,128)(2,1)S(1)}, bf16[96,256]{1,0:T(8,128)(2,1)S(1)}, u32[]{:S(2)}, u32[]{:S(2)}) collective-permute-start(bf16[96,256]{1,0:T(8,128)(2,1)S(1)} %slice.56), channel_id=1, source_target_pairs={{64,0},{72,8},{80,16},{88,24},{96,32},{104,40},{112,48},{120,56},{... | collective-permute-start | bytes 147464 | tf_op jit(solution)/shard_map/gather_keys_values/ppermute | solution.py:33
  5.0 34.0 %collective-permute-start.18 = (bf16[160,256]{1,0:T(8,128)(2,1)S(1)}, bf16[160,256]{1,0:T(8,128)(2,1)S(1)}, u32[]{:S(2)}, u32[]{:S(2)}) collective-permute-start(bf16[160,256]{1,0:T(8,128)(2,1)S(1)} %get-tuple-element.12), channel_id=1, source_target_pairs={{56,0},{0,8},{8,16},{16,24},{24,32},{32,40},{40,48},{48,56},{120,6... | collective-permute-start | bytes 245768 | tf_op jit(solution)/shard_map/gather_keys_values/ppermute | solution.py:33
  6.7 10.1 %collective-permute-start.15 = (bf16[160,256]{1,0:T(8,128)(2,1)S(1)}, bf16[160,256]{1,0:T(8,128)(2,1)S(1)}, u32[]{:S(2)}, u32[]{:S(2)}) collective-permute-start(bf16[160,256]{1,0:T(8,128)(2,1)S(1)} %get-tuple-element.12), channel_id=1, source_target_pairs={{48,0},{56,8},{0,16},{8,24},{16,32},{24,40},{32,48},{40,56},{112,6... | collective-permute-start | bytes 245768 | tf_op jit(solution)/shard_map/gather_keys_values/ppermute | solution.py:33
  10.0 8.1 %collective-permute-start.12 = (bf16[160,256]{1,0:T(8,128)(2,1)S(1)}, bf16[160,256]{1,0:T(8,128)(2,1)S(1)}, u32[]{:S(2)}, u32[]{:S(2)}) collective-permute-start(bf16[160,256]{1,0:T(8,128)(2,1)S(1)} %get-tuple-element.12), channel_id=1, source_target_pairs={{16,0},{24,8},{32,16},{40,24},{48,32},{56,40},{0,48},{8,56},{80,64... | collective-permute-start | bytes 245768 | tf_op jit(solution)/shard_map/gather_keys_values/ppermute | solution.py:33
  12.2 8.7 %collective-permute-start.11 = (bf16[160,256]{1,0:T(8,128)(2,1)S(1)}, bf16[160,256]{1,0:T(8,128)(2,1)S(1)}, u32[]{:S(2)}, u32[]{:S(2)}) collective-permute-start(bf16[160,256]{1,0:T(8,128)(2,1)S(1)} %get-tuple-element.12), channel_id=1, source_target_pairs={{8,0},{16,8},{24,16},{32,24},{40,32},{48,40},{56,48},{0,56},{72,64... | collective-permute-start | bytes 245768 | tf_op jit(solution)/shard_map/gather_keys_values/ppermute | solution.py:33
  13.9 29.5 %collective-permute-start.7 = (bf16[384,256]{1,0:T(8,128)(2,1)S(1)}, bf16[384,256]{1,0:T(8,128)(2,1)S(1)}, u32[]{:S(2)}, u32[]{:S(2)}) collective-permute-start(bf16[384,256]{1,0:T(8,128)(2,1)S(1)} %pad_maximum_fusion.rest_0_), channel_id=1, source_target_pairs={{48,0},{56,8},{0,16},{8,24},{16,32},{24,40},{32,48},{40,56},{112,6... | collective-permute-start | bytes 589832 | tf_op jit(solution)/shard_map/gather_keys_values/ppermute | solution.py:33
  16.8 27.2 %collective-permute-start.4 = (bf16[384,256]{1,0:T(8,128)(2,1)S(1)}, bf16[384,256]{1,0:T(8,128)(2,1)S(1)}, u32[]{:S(2)}, u32[]{:S(2)}) collective-permute-start(bf16[384,256]{1,0:T(8,128)(2,1)S(1)} %pad_maximum_fusion.rest_0_), channel_id=1, source_target_pairs={{16,0},{24,8},{32,16},{40,24},{48,32},{56,40},{0,48},{8,56},{80,64... | collective-permute-start | bytes 589832 | tf_op jit(solution)/shard_map/gather_keys_values/ppermute | solution.py:33
  18.1 16.9 %collective-permute-start.16 = (bf16[80,256]{1,0:T(8,128)(2,1)S(1)}, bf16[80,256]{1,0:T(8,128)(2,1)S(1)}, u32[]{:S(2)}, u32[]{:S(2)}) collective-permute-start(bf16[80,256]{1,0:T(8,128)(2,1)S(1)} %slice.61), channel_id=1, source_target_pairs={{48,0},{56,8},{0,16},{8,24},{16,32},{24,40},{32,48},{40,56},{112,6... | collective-permute-start | bytes 122888 | tf_op jit(solution)/shard_map/gather_keys_values/ppermute | solution.py:33
  20.9 7.3 %collective-permute-start.13 = (bf16[160,256]{1,0:T(8,128)(2,1)S(1)}, bf16[160,256]{1,0:T(8,128)(2,1)S(1)}, u32[]{:S(2)}, u32[]{:S(2)}) collective-permute-start(bf16[160,256]{1,0:T(8,128)(2,1)S(1)} %collective-permute-done.12), channel_id=1, source_target_pairs={{8,0},{16,8},{24,16},{32,24},{40,32},{48,40},{56,48},{0,56},{72,64... | collective-permute-start | bytes 245768 | tf_op jit(solution)/shard_map/gather_keys_values/ppermute | solution.py:33
  33.0 6.0 %collective-permute-start.17 = (bf16[160,256]{1,0:T(8,128)(2,1)S(1)}, bf16[160,256]{1,0:T(8,128)(2,1)S(1)}, u32[]{:S(2)}, u32[]{:S(2)}) collective-permute-start(bf16[160,256]{1,0:T(8,128)(2,1)S(1)} %collective-permute-done.15), channel_id=1, source_target_pairs={{56,0},{0,8},{8,16},{16,24},{24,32},{32,40},{40,48},{48,56},{120,6... | collective-permute-start | bytes 245768 | tf_op jit(solution)/shard_map/gather_keys_values/ppermute | solution.py:33
  39.1 27.2 %collective-permute-start.21 = (bf16[1280,256]{1,0:T(8,128)(2,1)S(1)}, bf16[1280,256]{1,0:T(8,128)(2,1)S(1)}, u32[]{:S(2)}, u32[]{:S(2)}) collective-permute-start(bf16[1280,256]{1,0:T(8,128)(2,1)S(1)} %constant_dynamic-update-slice_fusion.2.rest_9_), channel_id=1, source_target_pairs={{192,0},{200,8},{208,16},{216,24},{224,32},{232,40},{240,48},{248,... | collective-permute-start | bytes 1966088 | tf_op jit(solution)/shard_map/gather_keys_values/ppermute | solution.py:33
  42.0 24.3 %collective-permute-start.20 = (bf16[1280,256]{1,0:T(8,128)(2,1)S(1)}, bf16[1280,256]{1,0:T(8,128)(2,1)S(1)}, u32[]{:S(2)}, u32[]{:S(2)}) collective-permute-start(bf16[1280,256]{1,0:T(8,128)(2,1)S(1)} %constant_dynamic-update-slice_fusion.2.rest_9_), channel_id=1, source_target_pairs={{128,0},{136,8},{144,16},{152,24},{160,32},{168,40},{176,48},{184,... | collective-permute-start | bytes 1966088 | tf_op jit(solution)/shard_map/gather_keys_values/ppermute | solution.py:33
  42.2 27.0 %collective-permute-start.19 = (bf16[1280,256]{1,0:T(8,128)(2,1)S(1)}, bf16[1280,256]{1,0:T(8,128)(2,1)S(1)}, u32[]{:S(2)}, u32[]{:S(2)}) collective-permute-start(bf16[1280,256]{1,0:T(8,128)(2,1)S(1)} %constant_dynamic-update-slice_fusion.2.rest_9_), channel_id=1, source_target_pairs={{64,0},{72,8},{80,16},{88,24},{96,32},{104,40},{112,48},{120,56},{... | collective-permute-start | bytes 1966088 | tf_op jit(solution)/shard_map/gather_keys_values/ppermute | solution.py:33
  43.4 8.0 %collective-permute-start.10 = (bf16[384,256]{1,0:T(8,128)(2,1)S(1)}, bf16[384,256]{1,0:T(8,128)(2,1)S(1)}, u32[]{:S(2)}, u32[]{:S(2)}) collective-permute-start(bf16[384,256]{1,0:T(8,128)(2,1)S(1)} %pad_maximum_fusion.rest_0_), channel_id=1, source_target_pairs={{56,0},{0,8},{8,16},{16,24},{24,32},{32,40},{40,48},{48,56},{120,6... | collective-permute-start | bytes 589832 | tf_op jit(solution)/shard_map/gather_keys_values/ppermute | solution.py:33
  44.0 9.5 %collective-permute-start.3 = (bf16[384,256]{1,0:T(8,128)(2,1)S(1)}, bf16[384,256]{1,0:T(8,128)(2,1)S(1)}, u32[]{:S(2)}, u32[]{:S(2)}) collective-permute-start(bf16[384,256]{1,0:T(8,128)(2,1)S(1)} %pad_maximum_fusion.rest_0_), channel_id=1, source_target_pairs={{8,0},{16,8},{24,16},{32,24},{40,32},{48,40},{56,48},{0,56},{72,64... | collective-permute-start | bytes 589832 | tf_op jit(solution)/shard_map/gather_keys_values/ppermute | solution.py:33
  51.4 7.1 %collective-permute-start.8 = (bf16[192,256]{1,0:T(8,128)(2,1)S(1)}, bf16[192,256]{1,0:T(8,128)(2,1)S(1)}, u32[]{:S(2)}, u32[]{:S(2)}) collective-permute-start(bf16[192,256]{1,0:T(8,128)(2,1)S(1)} %slice.58), channel_id=1, source_target_pairs={{48,0},{56,8},{0,16},{8,24},{16,32},{24,40},{32,48},{40,56},{112,6... | collective-permute-start | bytes 294920 | tf_op jit(solution)/shard_map/gather_keys_values/ppermute | solution.py:33
  53.5 7.1 %collective-permute-start.6 = (bf16[192,256]{1,0:T(8,128)(2,1)S(1)}, bf16[192,256]{1,0:T(8,128)(2,1)S(1)}, u32[]{:S(2)}, u32[]{:S(2)}) collective-permute-start(bf16[192,256]{1,0:T(8,128)(2,1)S(1)} %slice.57), channel_id=1, source_target_pairs={{16,0},{24,8},{32,16},{40,24},{48,32},{56,40},{0,48},{8,56},{80,64... | collective-permute-start | bytes 294920 | tf_op jit(solution)/shard_map/gather_keys_values/ppermute | solution.py:33
  58.5 6.9 %collective-permute-start.9 = (bf16[384,256]{1,0:T(8,128)(2,1)S(1)}, bf16[384,256]{1,0:T(8,128)(2,1)S(1)}, u32[]{:S(2)}, u32[]{:S(2)}) collective-permute-start(bf16[384,256]{1,0:T(8,128)(2,1)S(1)} %collective-permute-done.7.rest_7_), channel_id=1, source_target_pairs={{56,0},{0,8},{8,16},{16,24},{24,32},{32,40},{40,48},{48,56},{120,6... | collective-permute-start | bytes 589832 | tf_op jit(solution)/shard_map/gather_keys_values/ppermute | solution.py:33
  60.6 5.7 %collective-permute-start.5 = (bf16[384,256]{1,0:T(8,128)(2,1)S(1)}, bf16[384,256]{1,0:T(8,128)(2,1)S(1)}, u32[]{:S(2)}, u32[]{:S(2)}) collective-permute-start(bf16[384,256]{1,0:T(8,128)(2,1)S(1)} %collective-permute-done.4.rest_2_), channel_id=1, source_target_pairs={{8,0},{16,8},{24,16},{32,24},{40,32},{48,40},{56,48},{0,56},{72,64... | collective-permute-start | bytes 589832 | tf_op jit(solution)/shard_map/gather_keys_values/ppermute | solution.py:33
  99.6 9.7 %collective-permute-start.23 = (bf16[256,512]{1,0:T(8,128)(2,1)S(1)}, bf16[256,512]{1,0:T(8,128)(2,1)S(1)}, u32[]{:S(2)}, u32[]{:S(2)}) collective-permute-start(bf16[256,512]{1,0:T(8,128)(2,1)S(1)} %get-tuple-element.9), channel_id=1, source_target_pairs={{6,0},{7,1},{0,2},{1,3},{2,4},{3,5},{4,6},{5,7},{14,8},{15,9},{8,1... | collective-permute-start | bytes 786440 | tf_op jit(solution)/shard_map/sum_over_heads/ppermute | solution.py:196
  101.3 13.0 %collective-permute-start.25 = (bf16[256,512]{1,0:T(8,128)(2,1)S(1)}, bf16[256,512]{1,0:T(8,128)(2,1)S(1)}, u32[]{:S(2)}, u32[]{:S(2)}) collective-permute-start(bf16[256,512]{1,0:T(8,128)(2,1)S(1)} %get-tuple-element.10), channel_id=1, source_target_pairs={{2,0},{3,1},{4,2},{5,3},{6,4},{7,5},{0,6},{1,7},{10,8},{11,9},{12,... | collective-permute-start | bytes 786440 | tf_op jit(solution)/shard_map/sum_over_heads/ppermute | solution.py:196
  102.9 13.2 %collective-permute-start.24 = (bf16[256,512]{1,0:T(8,128)(2,1)S(1)}, bf16[256,512]{1,0:T(8,128)(2,1)S(1)}, u32[]{:S(2)}, u32[]{:S(2)}) collective-permute-start(bf16[256,512]{1,0:T(8,128)(2,1)S(1)} %get-tuple-element.11), channel_id=1, source_target_pairs={{4,0},{5,1},{6,2},{7,3},{0,4},{1,5},{2,6},{3,7},{12,8},{13,9},{14,... | collective-permute-start | bytes 786440 | tf_op jit(solution)/shard_map/sum_over_heads/ppermute | solution.py:196
  (4 other events, 9.3 us)

commit v2 on v1

v2 whole, which is shorter than its diff:
```python
import functools

import jax
import jax.numpy as jnp
from jax import lax
from jax.experimental import pallas as pl
from jax.experimental.pallas import tpu as pltpu
from jax.sharding import PartitionSpec as P

HD = 128
GROUP = 8
NX, NZ, NY = 4, 8, 4
HALF = 128
BLOCKS = 2 * NX * NZ
CHUNK = 512
NEG = -1e30
SCALE2 = (HD ** -0.5) * 1.4426950408889634
FIRST_Z, LATER_Z = (0, 1, 7, 2), (6, 3, 4, 5)
VMEM = pl.BlockSpec(memory_space=pltpu.VMEM)
ANY = pl.BlockSpec(memory_space=pl.ANY)


def from_x(k):
    return [(((x + k) % NX) * NZ + z, x * NZ + z) for x in range(NX) for z in range(NZ)]


def from_z(k):
    return [(x * NZ + (z + k) % NZ, x * NZ + z) for x in range(NX) for z in range(NZ)]


def from_y(k):
    return [(((y + k) % NY) * 2 + c, y * 2 + c) for y in range(NY) for c in range(2)]


CORES = [(y * 2 + c, y * 2 + 1 - c) for y in range(NY) for c in range(2)]


def ctx(a, perm):
    return lax.ppermute(a, "ctx", perm)


def lay_beside(k_ref, v_ref, out):
    out[:, :HD] = k_ref[...]
    out[:, HD:] = v_ref[...]


def lay_together(*refs):
    at = 0
    for piece in refs[:-1]:
        refs[-1][at : at + piece.shape[0], :] = piece[...]
        at += piece.shape[0]


def together(parts):
    rows = sum(p.shape[0] for p in parts)
    return pl.pallas_call(
        lay_together,
        out_shape=jax.ShapeDtypeStruct((rows, parts[0].shape[1]), parts[0].dtype),
        in_specs=[VMEM] * len(parts),
        out_specs=VMEM,
        compiler_params=pltpu.CompilerParams(vmem_limit_bytes=8 * 2**20),
    )(*parts)


def attend(rows, first, last, *refs):
    refs = list(refs)
    take = lambda n: [refs.pop(0) for _ in range(n)]
    len_hbm, q_hbm = take(2)
    w_hbm = take(1)[0] if last else None
    pieces = take(2 * len(rows))
    state = [] if first else take(2)
    mine_ref, other_ref = take(2) if last else (None, None)
    acc, top, kv, q, lens, kv_sem, q_sem, len_sem = take(8)
    me = lax.axis_index("ctx")
    mx, mz = me // NZ, me % NZ
    span = NZ * HALF

    len_copy = pltpu.make_async_copy(len_hbm, lens, len_sem)
    len_copy.start()
    q_copy = pltpu.make_async_copy(q_hbm, q, q_sem)
    q_copy.start()
    for r in range(len(rows)):
        for ref, offsets in zip(pieces[2 * r : 2 * r + 2], (FIRST_Z, LATER_Z)):
            for i, kz in enumerate(offsets):
                z = (mz + kz) % NZ
                for part, at in ((0, z), (1, 2 * NZ - 1 - z)):
                    pltpu.make_async_copy(
                        ref.at[pl.ds((2 * i + part) * HALF, HALF), :],
                        kv.at[pl.ds(pl.multiple_of((2 * r * NZ + at) * HALF, HALF), HALF), :],
                        kv_sem,
                    ).start()
    if last:
        w, att, w_sem = take(3)
        w_copy = pltpu.make_async_copy(w_hbm, w, w_sem)
        w_copy.start()
    if first:
        acc[...] = jnp.zeros_like(acc)
        top[...] = jnp.full_like(top, NEG)
    else:
        acc[...] = state[0][...]
        top[...] = state[1][...]
    len_copy.wait()
    ends = []
    total = 0
    for i in range(4):
        total = total + lens[i]
        ends.append(total)

    def begins(p):
        start = jnp.zeros_like(p)
        for e in ends:
            start = jnp.maximum(start, jnp.where(p >= e, e, 0))
        return start

    q_copy.wait()
    pltpu.make_async_copy(kv, kv, kv_sem).wait()
    ones = jnp.ones((CHUNK, HD), jnp.bfloat16)
    per = span // CHUNK

    def rows_of(h, carry):
        q0 = jnp.where(h == 0, me, BLOCKS - 1 - me) * HALF
        first_start, last_start = begins(q0), begins(q0 + HALF - 1)
        q_rows = pl.ds(pl.multiple_of(h * HALF, HALF), HALF)

        def step(c, k0, masked):
            s0 = pl.multiple_of(c * CHUNK, CHUNK)
            k = kv[pl.ds(s0, CHUNK), :HD]
            v = jnp.concatenate([kv[pl.ds(s0, CHUNK), HD:], ones], axis=1)
            if masked:
                kp = k0 + lax.broadcasted_iota(jnp.int32, (HALF, CHUNK), 1)
                qp = q0 + lax.broadcasted_iota(jnp.int32, (HALF, CHUNK), 0)
                ok = (kp <= qp) & (kp >= begins(qp))
            for g in range(GROUP):
                at = slice(g * HALF, (g + 1) * HALF)
                s = lax.dot_general(
                    q[q_rows, g * HD : (g + 1) * HD],
                    k,
                    (((1,), (1,)), ((), ())),
                    preferred_element_type=jnp.float32,
                )
                if masked:
                    s = jnp.where(ok, s, NEG)
                old = top[h, at, :]
                new = jnp.maximum(old, jnp.max(s, axis=1, keepdims=True))
                p = jnp.exp2((s - jnp.tile(new, (1, CHUNK // HD))) * SCALE2)
                o = jnp.dot(p.astype(jnp.bfloat16), v, preferred_element_type=jnp.float32)
                alpha = jnp.exp2((old - new) * SCALE2)
                acc[h, at, :] = acc[h, at, :] * jnp.tile(alpha, (1, 2)) + o
                top[h, at, :] = new

        def one(c, carry):
            r, late, j = c // (2 * per), (c // per) % 2, c % per
            kx = rows[0]
            for i in range(1, len(rows)):
                kx = jnp.where(r == i, rows[i], kx)
            x = (mx + kx) % NX
            k0 = jnp.where(late == 0, x, 2 * NX - 1 - x) * span + j * CHUNK
            some = (k0 <= q0 + HALF - 1) & (k0 + CHUNK - 1 >= first_start)
            whole = (k0 >= last_start) & (k0 + CHUNK - 1 <= q0)
            pl.when(whole)(lambda: step(c, k0, False))
            pl.when(some & jnp.logical_not(whole))(lambda: step(c, k0, True))
            return carry

        lax.fori_loop(0, len(rows) * 2 * per, one, 0)
        if last:
            for g in range(GROUP):
                at = slice(g * HALF, (g + 1) * HALF)
                att[q_rows, g * HD : (g + 1) * HD] = (
                    acc[h, at, :HD] / acc[h, at, HD:]
                ).astype(jnp.bfloat16)
        return carry

    lax.fori_loop(0, 2, rows_of, 0)
    if last:
        w_copy.wait()
        tp = lax.axis_index("tp")
        my, mc = tp // 2, tp % 2
        width = mine_ref.shape[2]
        for k in range(NY):
            for ref, parity in ((mine_ref, mc), (other_ref, 1 - mc)):
                col = pl.multiple_of((((my + k) % NY) * 2 + parity) * width, width)
                ref[k] = jnp.dot(
                    att[...], w[:, pl.ds(col, width)], preferred_element_type=jnp.float32
                ).astype(jnp.bfloat16)


def attend_to(rows, lengths, queries, pieces, state=None, out_weight=None):
    first, last = state is None, out_weight is not None
    tokens = queries.shape[0]
    state_shape = [(2, GROUP * HALF, 2 * HD), (2, GROUP * HALF, HD)]
    outs = [jax.ShapeDtypeStruct(s, jnp.float32) for s in state_shape]
    operands = [lengths, queries] + ([out_weight] if last else []) + pieces
    specs = [ANY] * len(operands) + ([] if first else [VMEM] * 2)
    operands = operands + ([] if first else list(state))
    scratch = [
        pltpu.VMEM((len(rows) * 2 * NZ * HALF, 2 * HD), jnp.bfloat16),
        pltpu.VMEM(queries.shape, jnp.bfloat16),
        pltpu.SMEM(lengths.shape, jnp.int32),
    ] + [pltpu.SemaphoreType.DMA] * 3
    flops = 1_100_000_000 * len(rows)
    if last:
        width = out_weight.shape[1] // (2 * NY)
        scratch = [pltpu.VMEM(s, jnp.float32) for s in state_shape] + scratch
        scratch += [
            pltpu.VMEM(out_weight.shape, jnp.bfloat16),
            pltpu.VMEM(queries.shape, jnp.bfloat16),
            pltpu.SemaphoreType.DMA,
        ]
        outs = [jax.ShapeDtypeStruct((NY, tokens, width), jnp.bfloat16)] * 2
        flops += 2_150_000_000
    return pl.pallas_call(
        functools.partial(attend, rows, first, last),
        out_shape=outs,
        in_specs=specs,
        out_specs=[VMEM] * 2,
        scratch_shapes=scratch,
        compiler_params=pltpu.CompilerParams(vmem_limit_bytes=(36 if last else 20) * 2**20),
        cost_estimate=pl.CostEstimate(
            flops=flops, bytes_accessed=6 * 2**20, transcendentals=3_000_000 * len(rows)
        ),
    )(*operands)


def on_device(queries, keys, values, lengths, out_weight):
    tokens = queries.shape[0]
    with jax.named_scope("gather_keys_values"):
        kv = pl.pallas_call(
            lay_beside,
            out_shape=jax.ShapeDtypeStruct((tokens, 2 * HD), keys.dtype),
            in_specs=[VMEM] * 2,
            out_specs=VMEM,
        )(keys, values)
        up2, down2 = ctx(kv, from_z(2)), ctx(kv, from_z(-2))
        up1, down1 = ctx(kv, from_z(1)), ctx(kv, from_z(-1))
        early = together([kv, up1, down1, up2])
        right_a, left_a = ctx(early, from_x(1)), ctx(early, from_x(-1))
        up3, down3 = ctx(up2, from_z(1)), ctx(down2, from_z(-1))
        up4 = ctx(up2, from_z(2))
        later = together([down2, up3, up4, down3])
        right_b, left_b = ctx(later, from_x(1)), ctx(later, from_x(-1))
        far_a = ctx(right_a, from_x(1))
        far_b = ctx(left_b, from_x(-1))
    with jax.named_scope("attend_own_row"):
        state = attend_to((0,), lengths, queries, [early, later])
    with jax.named_scope("attend_next_rows"):
        state = attend_to((1, 3), lengths, queries, [right_a, right_b, left_a, left_b], state)
    with jax.named_scope("attend_far_row_and_project"):
        mine, other = attend_to((2,), lengths, queries, [far_a, far_b], state, out_weight)
    with jax.named_scope("sum_over_heads"):
        theirs = lax.ppermute(other, "tp", CORES)

        def pair(k):
            return (mine[k].astype(jnp.float32) + theirs[k].astype(jnp.float32)).astype(jnp.bfloat16)

        out = mine[0].astype(jnp.float32) + theirs[0].astype(jnp.float32)
        for k in (2, 1, 3):
            out = out + lax.ppermute(pair(k), "tp", from_y(-k)).astype(jnp.float32)
        return out.astype(jnp.bfloat16)


def solution(mesh):
    return jax.shard_map(
        on_device,
        mesh=mesh,
        in_specs=(P("ctx", "tp"), P("ctx", "tp"), P("ctx", "tp"), P(), P("tp", None)),
        out_specs=P("ctx", "tp"),
        check_vma=False,
    )
```

time: 116 us -> 91.6 us (0.79)
  the two profiles are of different devices: /device:TPU:6 before, /device:TPU:1 now
where the time goes in v2:
time: 91.6 us; the launch traced here: 91.3 us
  starting transfers between devices  36.4 us (40%)
  waiting for transfers between devices  27.4 us (30%)
  Pallas kernels  24.8 us (27%)
  local copies, waits for them, and re-layouts  1.57 us (2%)
  other arithmetic  1.08 us (1%)
    ppermute x13, starting transfers between devices, ctx(): return lax.ppermute(a, 'ctx', perm)  27.5 us
    pallas_call x3, Pallas kernels, attend_to(): pl.pallas_call(functools.partial(attend, rows, first, last), out_shape=ou...  23.1 us
    ppermute x13, waiting for transfers between devices, ctx(): return lax.ppermute(a, 'ctx', perm)  15.3 us
    ppermute x3, waiting for transfers between devices, on_device(): out = out + lax.ppermute(pair(k), 'tp', from_y(-k)).astype(jnp.float32)  9.76 us
    ppermute x3, starting transfers between devices, on_device(): out = out + lax.ppermute(pair(k), 'tp', from_y(-k)).astype(jnp.float32)  5.67 us
    ppermute x1, starting transfers between devices, on_device(): theirs = lax.ppermute(other, 'tp', CORES)  3.21 us
    ppermute x1, waiting for transfers between devices, on_device(): theirs = lax.ppermute(other, 'tp', CORES)  2.29 us
  transfers between devices with their start and end apart: 17, of which 10 were waited for; matrix products, arithmetic and copies ran while one was open for 0% of the time, Pallas kernels for 16%

profile of v2, /device:TPU:1, one launch (start us, length us, event | category | flops | bytes accessed | tf_op | source)
XLA Modules:
  0.0 91.3 jit_solution(14154188617320442946)
XLA Ops:
  0.0 1.6 %gather_keys_values.3.refs_0_ = bf16[256,256]{1,0:T(8,128)(2,1)} custom-call(bf16[256,128]{1,0:T(8,128)(2,1)} %k_ref.1, bf16[256,128]{1,0:T(8,128)(2,1)} %v_ref.1), custom_call_target="tpu_custom_call" | custom-call | tf_op jit(solution)/shard_map/gather_keys_values/pallas_call | solution.py:227
  1.6 6.8 %collective-permute-start.2 = (bf16[256,256]{1,0:T(8,128)(2,1)}, bf16[256,256]{1,0:T(8,128)(2,1)S(1)}, u32[]{:S(2)}, u32[]{:S(2)}) collective-permute-start(bf16[256,256]{1,0:T(8,128)(2,1)} %gather_keys_values.3.refs_0_), channel_id=1, source_target_pairs={{16,0},{24,8},{32,16},{40,24},{48,32},{56,40},{0,48},{8,56},{80,64... | collective-permute-start | bytes 393224 | tf_op jit(solution)/shard_map/gather_keys_values/ppermute | solution.py:39
  8.5 3.1 %collective-permute-start = (bf16[256,256]{1,0:T(8,128)(2,1)}, bf16[256,256]{1,0:T(8,128)(2,1)S(1)}, u32[]{:S(2)}, u32[]{:S(2)}) collective-permute-start(bf16[256,256]{1,0:T(8,128)(2,1)} %gather_keys_values.3.refs_0_), channel_id=1, source_target_pairs={{8,0},{16,8},{24,16},{32,24},{40,32},{48,40},{56,48},{0,56},{72,64... | collective-permute-start | bytes 393224 | tf_op jit(solution)/shard_map/gather_keys_values/ppermute | solution.py:39
  12.0 4.7 %collective-permute-start.6 = (bf16[256,256]{1,0:T(8,128)(2,1)S(1)}, bf16[256,256]{1,0:T(8,128)(2,1)S(1)}, u32[]{:S(2)}, u32[]{:S(2)}) collective-permute-start(bf16[256,256]{1,0:T(8,128)(2,1)S(1)} %collective-permute-done.2.refs_3_), channel_id=1, source_target_pairs={{8,0},{16,8},{24,16},{32,24},{40,32},{48,40},{56,48},{0,56},{72,64... | collective-permute-start | bytes 393224 | tf_op jit(solution)/shard_map/gather_keys_values/ppermute | solution.py:39
  16.8 1.4 %collective-permute-start.7 = (bf16[256,256]{1,0:T(8,128)(2,1)S(1)}, bf16[256,256]{1,0:T(8,128)(2,1)S(1)}, u32[]{:S(2)}, u32[]{:S(2)}) collective-permute-start(bf16[256,256]{1,0:T(8,128)(2,1)S(1)} %collective-permute-done.2.refs_3_), channel_id=1, source_target_pairs={{16,0},{24,8},{32,16},{40,24},{48,32},{56,40},{0,48},{8,56},{80,64... | collective-permute-start | bytes 393224 | tf_op jit(solution)/shard_map/gather_keys_values/ppermute | solution.py:39
  18.2 1.5 %collective-permute-start.8 = (bf16[256,256]{1,0:T(8,128)(2,1)S(1)}, bf16[256,256]{1,0:T(8,128)(2,1)S(1)}, u32[]{:S(2)}, u32[]{:S(2)}) collective-permute-start(bf16[256,256]{1,0:T(8,128)(2,1)S(1)} %collective-permute-done.5.refs_0_), channel_id=1, source_target_pairs={{56,0},{0,8},{8,16},{16,24},{24,32},{32,40},{40,48},{48,56},{120,6... | collective-permute-start | bytes 393224 | tf_op jit(solution)/shard_map/gather_keys_values/ppermute | solution.py:39
  19.7 1.1 %collective-permute-done.1.refs_2_ = bf16[256,256]{1,0:T(8,128)(2,1)S(1)} collective-permute-done((bf16[256,256]{1,0:T(8,128)(2,1)}, bf16[256,256]{1,0:T(8,128)(2,1)S(1)}, u32[]{:S(2)}, u32[]{:S(2)}) %collective-permute-start.1) | collective-permute-done | bytes 131104 | tf_op jit(solution)/shard_map/gather_keys_values/ppermute | solution.py:39
  21.7 2.6 %collective-permute-start.3 = (bf16[1024,256]{1,0:T(8,128)(2,1)S(1)}, bf16[1024,256]{1,0:T(8,128)(2,1)S(1)}, u32[]{:S(2)}, u32[]{:S(2)}) collective-permute-start(bf16[1024,256]{1,0:T(8,128)(2,1)S(1)} %gather_keys_values.4.refs_2_), channel_id=1, source_target_pairs={{64,0},{72,8},{80,16},{88,24},{96,32},{104,40},{112,48},{120,56},{... | collective-permute-start | bytes 1572872 | tf_op jit(solution)/shard_map/gather_keys_values/ppermute | solution.py:39
  25.1 1.3 %collective-permute-start.9 = (bf16[1024,256]{1,0:T(8,128)(2,1)S(1)}, bf16[1024,256]{1,0:T(8,128)(2,1)S(1)}, u32[]{:S(2)}, u32[]{:S(2)}) collective-permute-start(bf16[1024,256]{1,0:T(8,128)(2,1)S(1)} %gather_keys_values.5.refs_3_), channel_id=1, source_target_pairs={{192,0},{200,8},{208,16},{216,24},{224,32},{232,40},{240,48},{248,... | collective-permute-start | bytes 1572872 | tf_op jit(solution)/shard_map/gather_keys_values/ppermute | solution.py:39
  26.3 1.2 %collective-permute-start.12 = (bf16[1024,256]{1,0:T(8,128)(2,1)S(1)}, bf16[1024,256]{1,0:T(8,128)(2,1)S(1)}, u32[]{:S(2)}, u32[]{:S(2)}) collective-permute-start(bf16[1024,256]{1,0:T(8,128)(2,1)S(1)} %gather_keys_values.4.refs_2_), channel_id=1, source_target_pairs={{192,0},{200,8},{208,16},{216,24},{224,32},{232,40},{240,48},{248,... | collective-permute-start | bytes 1572872 | tf_op jit(solution)/shard_map/gather_keys_values/ppermute | solution.py:39
  27.6 1.5 %collective-permute-start.11 = (bf16[1024,256]{1,0:T(8,128)(2,1)S(1)}, bf16[1024,256]{1,0:T(8,128)(2,1)S(1)}, u32[]{:S(2)}, u32[]{:S(2)}) collective-permute-start(bf16[1024,256]{1,0:T(8,128)(2,1)S(1)} %gather_keys_values.5.refs_3_), channel_id=1, source_target_pairs={{64,0},{72,8},{80,16},{88,24},{96,32},{104,40},{112,48},{120,56},{... | collective-permute-start | bytes 1572872 | tf_op jit(solution)/shard_map/gather_keys_values/ppermute | solution.py:39
  29.0 4.7 %collective-permute-done.3.refs_2_ = bf16[1024,256]{1,0:T(8,128)(2,1)S(1)} collective-permute-done((bf16[1024,256]{1,0:T(8,128)(2,1)S(1)}, bf16[1024,256]{1,0:T(8,128)(2,1)S(1)}, u32[]{:S(2)}, u32[]{:S(2)}) %collective-permute-start.3) | collective-permute-done | bytes 524320 | tf_op jit(solution)/shard_map/gather_keys_values/ppermute | solution.py:39
  33.8 3.4 %collective-permute-start.4 = (bf16[1024,256]{1,0:T(8,128)(2,1)S(1)}, bf16[1024,256]{1,0:T(8,128)(2,1)S(1)}, u32[]{:S(2)}, u32[]{:S(2)}) collective-permute-start(bf16[1024,256]{1,0:T(8,128)(2,1)S(1)} %collective-permute-done.3.refs_2_), channel_id=1, source_target_pairs={{64,0},{72,8},{80,16},{88,24},{96,32},{104,40},{112,48},{120,56},{... | collective-permute-start | bytes 1572872 | tf_op jit(solution)/shard_map/gather_keys_values/ppermute | solution.py:39
  38.7 5.0 %attend_own_row.1 = (f32[2,1024,256]{2,1,0:T(8,128)S(1)}, f32[2,1024,128]{2,1,0:T(8,128)S(1)}) custom-call(s32[4]{0:T(128)S(1)} %copy-done.2, bf16[256,1024]{1,0:T(8,128)(2,1)S(1)} %copy-done, bf16[1024,256]{1,0:T(8,128)(2,1)S(1)} %gather_keys_values.4.refs_2_, bf16[1024,256]{1,0:T(8,128)(2,1)S(1)} %gather_keys_values.5.refs_3_), custom_call_target="tpu_custom_call" | custom-call | flops 1100000000 | bytes 6291456 | tf_op jit(solution)/shard_map/attend_own_row/pallas_call | solution.py:211
  43.6 5.6 %collective-permute-done.12.refs_4_ = bf16[1024,256]{1,0:T(8,128)(2,1)S(1)} collective-permute-done((bf16[1024,256]{1,0:T(8,128)(2,1)S(1)}, bf16[1024,256]{1,0:T(8,128)(2,1)S(1)}, u32[]{:S(2)}, u32[]{:S(2)}) %collective-permute-start.12) | collective-permute-done | bytes 524320 | tf_op jit(solution)/shard_map/gather_keys_values/ppermute | solution.py:39
  49.3 9.3 %attend_next_rows.1 = (f32[2,1024,256]{2,1,0:T(8,128)S(1)}, f32[2,1024,128]{2,1,0:T(8,128)S(1)}) custom-call(s32[4]{0:T(128)S(1)} %copy-done.3, bf16[256,1024]{1,0:T(8,128)(2,1)S(1)} %copy-done, bf16[1024,256]{1,0:T(8,128)(2,1)S(1)} %collective-permute-done.3.refs_2_, bf16[1024,256]{1,0:T(8,128)(2,1)S(1)} %collective-permute-done.11.refs_3_, ...), custom_call_target="tpu_custom_call" | custom-call | flops 2200000000 | bytes 6291456 | tf_op jit(solution)/shard_map/attend_next_rows/pallas_call | solution.py:211
  58.6 1.9 %collective-permute-done.10.refs_4_ = bf16[1024,256]{1,0:T(8,128)(2,1)S(1)} collective-permute-done((bf16[1024,256]{1,0:T(8,128)(2,1)S(1)}, bf16[1024,256]{1,0:T(8,128)(2,1)S(1)}, u32[]{:S(2)}, u32[]{:S(2)}) %collective-permute-start.10) | collective-permute-done | bytes 524320 | tf_op jit(solution)/shard_map/gather_keys_values/ppermute | solution.py:39
  60.5 8.8 %attend_far_row_and_project.1 = (bf16[4,256,512]{2,1,0:T(8,128)(2,1)S(1)}, bf16[4,256,512]{2,1,0:T(8,128)(2,1)S(1)}) custom-call(s32[4]{0:T(128)S(1)} %copy-done.3, bf16[256,1024]{1,0:T(8,128)(2,1)S(1)} %copy-done, bf16[1024,4096]{1,0:T(8,128)(2,1)S(1)} %bitcast.15, bf16[1024,256]{1,0:T(8,128)(2,1)S(1)} %collective-permute-done.4.refs_3_, ...), custom_call_target="tpu_custom_call" | custom-call | flops 3249999872 | bytes 6291456 | tf_op jit(solution)/shard_map/attend_far_row_and_project/pallas_call | solution.py:211
  69.3 3.2 %collective-permute-start.13 = (bf16[4,256,512]{2,1,0:T(8,128)(2,1)S(1)}, bf16[4,256,512]{2,1,0:T(8,128)(2,1)S(1)}, u32[]{:S(2)}, u32[]{:S(2)}) collective-permute-start(bf16[4,256,512]{2,1,0:T(8,128)(2,1)S(1)} %get-tuple-element.16), channel_id=1, source_target_pairs={{0,1},{1,0},{2,3},{3,2},{4,5},{5,4},{6,7},{7,6},{8,9},{9,8},{10,11... | collective-permute-start | bytes 3145736 | tf_op jit(solution)/shard_map/sum_over_heads/ppermute | solution.py:250
  72.5 2.3 %collective-permute-done.13 = bf16[4,256,512]{2,1,0:T(8,128)(2,1)S(1)} collective-permute-done((bf16[4,256,512]{2,1,0:T(8,128)(2,1)S(1)}, bf16[4,256,512]{2,1,0:T(8,128)(2,1)S(1)}, u32[]{:S(2)}, u32[]{:S(2)}) %collective-permute-start.13) | collective-permute-done | bytes 1048608 | tf_op jit(solution)/shard_map/sum_over_heads/ppermute | solution.py:250
  75.0 3.0 %collective-permute-start.14 = (bf16[256,512]{1,0:T(8,128)(2,1)S(1)}, bf16[256,512]{1,0:T(8,128)(2,1)S(1)}, u32[]{:S(2)}, u32[]{:S(2)}) collective-permute-start(bf16[256,512]{1,0:T(8,128)(2,1)S(1)} %get-tuple-element.17), channel_id=1, source_target_pairs={{4,0},{5,1},{6,2},{7,3},{0,4},{1,5},{2,6},{3,7},{12,8},{13,9},{14,... | collective-permute-start | bytes 786440 | tf_op jit(solution)/shard_map/sum_over_heads/ppermute | solution.py:257
  78.4 2.3 %collective-permute-start.16 = (bf16[256,512]{1,0:T(8,128)(2,1)S(1)}, bf16[256,512]{1,0:T(8,128)(2,1)S(1)}, u32[]{:S(2)}, u32[]{:S(2)}) collective-permute-start(bf16[256,512]{1,0:T(8,128)(2,1)S(1)} %get-tuple-element.18), channel_id=1, source_target_pairs={{2,0},{3,1},{4,2},{5,3},{6,4},{7,5},{0,6},{1,7},{10,8},{11,9},{12,... | collective-permute-start | bytes 786440 | tf_op jit(solution)/shard_map/sum_over_heads/ppermute | solution.py:257
  80.7 3.5 %collective-permute-done.14 = bf16[256,512]{1,0:T(8,128)(2,1)S(1)} collective-permute-done((bf16[256,512]{1,0:T(8,128)(2,1)S(1)}, bf16[256,512]{1,0:T(8,128)(2,1)S(1)}, u32[]{:S(2)}, u32[]{:S(2)}) %collective-permute-start.14) | collective-permute-done | bytes 262176 | tf_op jit(solution)/shard_map/sum_over_heads/ppermute | solution.py:257
  84.2 6.3 %collective-permute-done.15 = bf16[256,512]{1,0:T(8,128)(2,1)S(1)} collective-permute-done((bf16[256,512]{1,0:T(8,128)(2,1)S(1)}, bf16[256,512]{1,0:T(8,128)(2,1)S(1)}, u32[]{:S(2)}, u32[]{:S(2)}) %collective-permute-start.15) | collective-permute-done | bytes 262176 | tf_op jit(solution)/shard_map/sum_over_heads/ppermute | solution.py:257
  (31 shorter events, 5.1 us)
Async XLA Ops:
  0.0 38.0 %copy-start = (bf16[256,1024]{1,0:T(8,128)(2,1)S(1)}, bf16[256,1024]{1,0:T(8,128)(2,1)}, u32[]{:S(2)}) copy-start(bf16[256,1024]{1,0:T(8,128)(2,1)} %refs_1_.5) | copy-start | bytes 1572868
  1.6 10.4 %collective-permute-start.2 = (bf16[256,256]{1,0:T(8,128)(2,1)}, bf16[256,256]{1,0:T(8,128)(2,1)S(1)}, u32[]{:S(2)}, u32[]{:S(2)}) collective-permute-start(bf16[256,256]{1,0:T(8,128)(2,1)} %gather_keys_values.3.refs_0_), channel_id=1, source_target_pairs={{16,0},{24,8},{32,16},{40,24},{48,32},{56,40},{0,48},{8,56},{80,64... | collective-permute-start | bytes 393224 | tf_op jit(solution)/shard_map/gather_keys_values/ppermute | solution.py:39
  8.5 9.7 %collective-permute-start.5 = (bf16[256,256]{1,0:T(8,128)(2,1)}, bf16[256,256]{1,0:T(8,128)(2,1)S(1)}, u32[]{:S(2)}, u32[]{:S(2)}) collective-permute-start(bf16[256,256]{1,0:T(8,128)(2,1)} %gather_keys_values.3.refs_0_), channel_id=1, source_target_pairs={{48,0},{56,8},{0,16},{8,24},{16,32},{24,40},{32,48},{40,56},{112,6... | collective-permute-start | bytes 393224 | tf_op jit(solution)/shard_map/gather_keys_values/ppermute | solution.py:39
  8.5 11.2 %collective-permute-start = (bf16[256,256]{1,0:T(8,128)(2,1)}, bf16[256,256]{1,0:T(8,128)(2,1)S(1)}, u32[]{:S(2)}, u32[]{:S(2)}) collective-permute-start(bf16[256,256]{1,0:T(8,128)(2,1)} %gather_keys_values.3.refs_0_), channel_id=1, source_target_pairs={{8,0},{16,8},{24,16},{32,24},{40,32},{48,40},{56,48},{0,56},{72,64... | collective-permute-start | bytes 393224 | tf_op jit(solution)/shard_map/gather_keys_values/ppermute | solution.py:39
  11.6 9.2 %collective-permute-start.1 = (bf16[256,256]{1,0:T(8,128)(2,1)}, bf16[256,256]{1,0:T(8,128)(2,1)S(1)}, u32[]{:S(2)}, u32[]{:S(2)}) collective-permute-start(bf16[256,256]{1,0:T(8,128)(2,1)} %gather_keys_values.3.refs_0_), channel_id=1, source_target_pairs={{56,0},{0,8},{8,16},{16,24},{24,32},{32,40},{40,48},{48,56},{120,6... | collective-permute-start | bytes 393224 | tf_op jit(solution)/shard_map/gather_keys_values/ppermute | solution.py:39
  12.0 12.3 %collective-permute-start.6 = (bf16[256,256]{1,0:T(8,128)(2,1)S(1)}, bf16[256,256]{1,0:T(8,128)(2,1)S(1)}, u32[]{:S(2)}, u32[]{:S(2)}) collective-permute-start(bf16[256,256]{1,0:T(8,128)(2,1)S(1)} %collective-permute-done.2.refs_3_), channel_id=1, source_target_pairs={{8,0},{16,8},{24,16},{32,24},{40,32},{48,40},{56,48},{0,56},{72,64... | collective-permute-start | bytes 393224 | tf_op jit(solution)/shard_map/gather_keys_values/ppermute | solution.py:39
  16.8 8.2 %collective-permute-start.7 = (bf16[256,256]{1,0:T(8,128)(2,1)S(1)}, bf16[256,256]{1,0:T(8,128)(2,1)S(1)}, u32[]{:S(2)}, u32[]{:S(2)}) collective-permute-start(bf16[256,256]{1,0:T(8,128)(2,1)S(1)} %collective-permute-done.2.refs_3_), channel_id=1, source_target_pairs={{16,0},{24,8},{32,16},{40,24},{48,32},{56,40},{0,48},{8,56},{80,64... | collective-permute-start | bytes 393224 | tf_op jit(solution)/shard_map/gather_keys_values/ppermute | solution.py:39
  18.2 6.8 %collective-permute-start.8 = (bf16[256,256]{1,0:T(8,128)(2,1)S(1)}, bf16[256,256]{1,0:T(8,128)(2,1)S(1)}, u32[]{:S(2)}, u32[]{:S(2)}) collective-permute-start(bf16[256,256]{1,0:T(8,128)(2,1)S(1)} %collective-permute-done.5.refs_0_), channel_id=1, source_target_pairs={{56,0},{0,8},{8,16},{16,24},{24,32},{32,40},{40,48},{48,56},{120,6... | collective-permute-start | bytes 393224 | tf_op jit(solution)/shard_map/gather_keys_values/ppermute | solution.py:39
  20.8 0.9 copy-start.1
  21.7 12.0 %collective-permute-start.3 = (bf16[1024,256]{1,0:T(8,128)(2,1)S(1)}, bf16[1024,256]{1,0:T(8,128)(2,1)S(1)}, u32[]{:S(2)}, u32[]{:S(2)}) collective-permute-start(bf16[1024,256]{1,0:T(8,128)(2,1)S(1)} %gather_keys_values.4.refs_2_), channel_id=1, source_target_pairs={{64,0},{72,8},{80,16},{88,24},{96,32},{104,40},{112,48},{120,56},{... | collective-permute-start | bytes 1572872 | tf_op jit(solution)/shard_map/gather_keys_values/ppermute | solution.py:39
  25.0 24.2 %copy-start.3 = (s32[4]{0:T(128)S(1)}, s32[4]{0:T(128)}, u32[]{:S(2)}) copy-start(s32[4]{0:T(128)} %refs_0_.5) | copy-start | bytes 52
  25.1 13.0 %collective-permute-start.9 = (bf16[1024,256]{1,0:T(8,128)(2,1)S(1)}, bf16[1024,256]{1,0:T(8,128)(2,1)S(1)}, u32[]{:S(2)}, u32[]{:S(2)}) collective-permute-start(bf16[1024,256]{1,0:T(8,128)(2,1)S(1)} %gather_keys_values.5.refs_3_), channel_id=1, source_target_pairs={{192,0},{200,8},{208,16},{216,24},{224,32},{232,40},{240,48},{248,... | collective-permute-start | bytes 1572872 | tf_op jit(solution)/shard_map/gather_keys_values/ppermute | solution.py:39
  26.3 22.9 %collective-permute-start.12 = (bf16[1024,256]{1,0:T(8,128)(2,1)S(1)}, bf16[1024,256]{1,0:T(8,128)(2,1)S(1)}, u32[]{:S(2)}, u32[]{:S(2)}) collective-permute-start(bf16[1024,256]{1,0:T(8,128)(2,1)S(1)} %gather_keys_values.4.refs_2_), channel_id=1, source_target_pairs={{192,0},{200,8},{208,16},{216,24},{224,32},{232,40},{240,48},{248,... | collective-permute-start | bytes 1572872 | tf_op jit(solution)/shard_map/gather_keys_values/ppermute | solution.py:39
  27.6 21.7 %collective-permute-start.11 = (bf16[1024,256]{1,0:T(8,128)(2,1)S(1)}, bf16[1024,256]{1,0:T(8,128)(2,1)S(1)}, u32[]{:S(2)}, u32[]{:S(2)}) collective-permute-start(bf16[1024,256]{1,0:T(8,128)(2,1)S(1)} %gather_keys_values.5.refs_3_), channel_id=1, source_target_pairs={{64,0},{72,8},{80,16},{88,24},{96,32},{104,40},{112,48},{120,56},{... | collective-permute-start | bytes 1572872 | tf_op jit(solution)/shard_map/gather_keys_values/ppermute | solution.py:39
  33.8 24.9 %collective-permute-start.4 = (bf16[1024,256]{1,0:T(8,128)(2,1)S(1)}, bf16[1024,256]{1,0:T(8,128)(2,1)S(1)}, u32[]{:S(2)}, u32[]{:S(2)}) collective-permute-start(bf16[1024,256]{1,0:T(8,128)(2,1)S(1)} %collective-permute-done.3.refs_2_), channel_id=1, source_target_pairs={{64,0},{72,8},{80,16},{88,24},{96,32},{104,40},{112,48},{120,56},{... | collective-permute-start | bytes 1572872 | tf_op jit(solution)/shard_map/gather_keys_values/ppermute | solution.py:39
  38.0 22.5 %collective-permute-start.10 = (bf16[1024,256]{1,0:T(8,128)(2,1)S(1)}, bf16[1024,256]{1,0:T(8,128)(2,1)S(1)}, u32[]{:S(2)}, u32[]{:S(2)}) collective-permute-start(bf16[1024,256]{1,0:T(8,128)(2,1)S(1)} %collective-permute-done.9.refs_5_), channel_id=1, source_target_pairs={{192,0},{200,8},{208,16},{216,24},{224,32},{232,40},{240,48},{248,... | collective-permute-start | bytes 1572872 | tf_op jit(solution)/shard_map/gather_keys_values/ppermute | solution.py:39
  38.0 0.7 copy-start.2
  38.7 21.8 %slice-start = ((s8[8388608]{0:T(1024)(128)(4,1)}), s8[4194304]{0:T(1024)(128)(4,1)S(1)}, s32[]{:S(2)}) async-start(s8[8388608]{0:T(1024)(128)(4,1)} %bitcast.14), calls=%async_computation | async-start | bytes 8388608
  49.3 11.2 %slice-start.1 = ((s8[8388608]{0:T(1024)(128)(4,1)}), s8[4194304]{0:T(1024)(128)(4,1)S(1)}, s32[]{:S(2)}) async-start(s8[8388608]{0:T(1024)(128)(4,1)} %bitcast.14), calls=%async_computation.1 | async-start | bytes 8388608
  69.3 5.5 %collective-permute-start.13 = (bf16[4,256,512]{2,1,0:T(8,128)(2,1)S(1)}, bf16[4,256,512]{2,1,0:T(8,128)(2,1)S(1)}, u32[]{:S(2)}, u32[]{:S(2)}) collective-permute-start(bf16[4,256,512]{2,1,0:T(8,128)(2,1)S(1)} %get-tuple-element.16), channel_id=1, source_target_pairs={{0,1},{1,0},{2,3},{3,2},{4,5},{5,4},{6,7},{7,6},{8,9},{9,8},{10,11... | collective-permute-start | bytes 3145736 | tf_op jit(solution)/shard_map/sum_over_heads/ppermute | solution.py:250
  75.0 9.2 %collective-permute-start.14 = (bf16[256,512]{1,0:T(8,128)(2,1)S(1)}, bf16[256,512]{1,0:T(8,128)(2,1)S(1)}, u32[]{:S(2)}, u32[]{:S(2)}) collective-permute-start(bf16[256,512]{1,0:T(8,128)(2,1)S(1)} %get-tuple-element.17), channel_id=1, source_target_pairs={{4,0},{5,1},{6,2},{7,3},{0,4},{1,5},{2,6},{3,7},{12,8},{13,9},{14,... | collective-permute-start | bytes 786440 | tf_op jit(solution)/shard_map/sum_over_heads/ppermute | solution.py:257
  78.0 12.4 %collective-permute-start.15 = (bf16[256,512]{1,0:T(8,128)(2,1)S(1)}, bf16[256,512]{1,0:T(8,128)(2,1)S(1)}, u32[]{:S(2)}, u32[]{:S(2)}) collective-permute-start(bf16[256,512]{1,0:T(8,128)(2,1)S(1)} %get-tuple-element.19), channel_id=1, source_target_pairs={{6,0},{7,1},{0,2},{1,3},{2,4},{3,5},{4,6},{5,7},{14,8},{15,9},{8,1... | collective-permute-start | bytes 786440 | tf_op jit(solution)/shard_map/sum_over_heads/ppermute | solution.py:257
  78.4 12.0 %collective-permute-start.16 = (bf16[256,512]{1,0:T(8,128)(2,1)S(1)}, bf16[256,512]{1,0:T(8,128)(2,1)S(1)}, u32[]{:S(2)}, u32[]{:S(2)}) collective-permute-start(bf16[256,512]{1,0:T(8,128)(2,1)S(1)} %get-tuple-element.18), channel_id=1, source_target_pairs={{2,0},{3,1},{4,2},{5,3},{6,4},{7,5},{0,6},{1,7},{10,8},{11,9},{12,... | collective-permute-start | bytes 786440 | tf_op jit(solution)/shard_map/sum_over_heads/ppermute | solution.py:257

commit v3 on v2

v3 whole, which is shorter than its diff:
```python
import functools

import jax
import jax.numpy as jnp
from jax import lax
from jax.experimental import pallas as pl
from jax.experimental.pallas import tpu as pltpu
from jax.sharding import PartitionSpec as P

HD = 128
GROUP = 8
NX, NZ, NY = 4, 8, 4
HALF = 128
BLOCKS = 2 * NX * NZ
NEG = -1e30
SCALE2 = (HD ** -0.5) * 1.4426950408889634
FIRST_Z, LATER_Z = (0, 1, 7, 2, 6), (3, 4, 5)
VMEM = pl.BlockSpec(memory_space=pltpu.VMEM)
ANY = pl.BlockSpec(memory_space=pl.ANY)


def from_x(k):
    return [(((x + k) % NX) * NZ + z, x * NZ + z) for x in range(NX) for z in range(NZ)]


def from_z(k):
    return [(x * NZ + (z + k) % NZ, x * NZ + z) for x in range(NX) for z in range(NZ)]


def from_y(k):
    return [(((y + k) % NY) * 2 + c, y * 2 + c) for y in range(NY) for c in range(2)]


OVER = [(x * NZ + (z + (2 if z % 2 == 0 else -2)) % NZ, x * NZ + z) for x in range(NX) for z in range(NZ)]
CORES = [(y * 2 + c, y * 2 + 1 - c) for y in range(NY) for c in range(2)]


def ctx(a, perm):
    return lax.ppermute(a, "ctx", perm)


def lay_beside(k_hbm, v_hbm, out, k_sem, v_sem):
    copies = [
        pltpu.make_async_copy(k_hbm, out.at[:, pl.ds(0, HD)], k_sem),
        pltpu.make_async_copy(v_hbm, out.at[:, pl.ds(HD, HD)], v_sem),
    ]
    for copy in copies:
        copy.start()
    for copy in copies:
        copy.wait()


def lay_together(*refs):
    at = 0
    for piece in refs[:-1]:
        refs[-1][at : at + piece.shape[0], :] = piece[...]
        at += piece.shape[0]


def together(parts):
    rows = sum(p.shape[0] for p in parts)
    return pl.pallas_call(
        lay_together,
        out_shape=jax.ShapeDtypeStruct((rows, parts[0].shape[1]), parts[0].dtype),
        in_specs=[VMEM] * len(parts),
        out_specs=VMEM,
        compiler_params=pltpu.CompilerParams(vmem_limit_bytes=8 * 2**20),
    )(*parts)


def attend(rows, first, last, *refs):
    refs = list(refs)
    take = lambda n: [refs.pop(0) for _ in range(n)]
    len_hbm, q = take(2)
    w_hbm = take(1)[0] if last else None
    pieces = take(2 * len(rows))
    state = [] if first else take(2)
    mine_ref, other_ref = take(2) if last else (None, None)
    acc, top, lens, len_sem = take(4)
    me = lax.axis_index("ctx")
    mx, mz = me // NZ, me % NZ
    span = NZ * HALF

    len_copy = pltpu.make_async_copy(len_hbm, lens, len_sem)
    len_copy.start()
    if last:
        att, w, w_sem = take(3)
        w_copy = pltpu.make_async_copy(w_hbm, w, w_sem)
        w_copy.start()
    if first:
        acc[...] = jnp.zeros_like(acc)
        top[...] = jnp.full_like(top, NEG)
    else:
        acc[...] = state[0][...]
        top[...] = state[1][...]
    len_copy.wait()
    ends = []
    total = 0
    for i in range(4):
        total = total + lens[i]
        ends.append(total)

    def begins(p):
        start = jnp.zeros_like(p)
        for e in ends:
            start = jnp.maximum(start, jnp.where(p >= e, e, 0))
        return start

    ones = jnp.ones((span, HD), jnp.bfloat16)

    def step(blocks, h, q0, late, k0, masked):
        k, v, kp = [], [], []
        for ref, i, kz in blocks:
            at = pl.ds(pl.multiple_of((2 * i + late) * HALF, HALF), HALF)
            k.append(ref[at, :HD])
            v.append(ref[at, HD:])
            z = (mz + kz) % NZ
            if masked:
                base = k0 + jnp.where(late == 0, z, NZ - 1 - z) * HALF
                kp.append(base + lax.broadcasted_iota(jnp.int32, (HALF, HALF), 1))
        k = jnp.concatenate(k, axis=0)
        v = jnp.concatenate([jnp.concatenate(v, axis=0), ones], axis=1)
        if masked:
            kp = jnp.concatenate(kp, axis=1)
            qp = q0 + lax.broadcasted_iota(jnp.int32, (HALF, HD), 0)
            begin = jnp.tile(begins(qp), (1, NZ))
            ok = (kp <= jnp.tile(qp, (1, NZ))) & (kp >= begin)
        q_rows = pl.ds(pl.multiple_of(h * HALF, HALF), HALF)
        for g in range(GROUP):
            at = slice(g * HALF, (g + 1) * HALF)
            s = lax.dot_general(
                q[q_rows, g * HD : (g + 1) * HD],
                k,
                (((1,), (1,)), ((), ())),
                preferred_element_type=jnp.float32,
            )
            if masked:
                s = jnp.where(ok, s, NEG)
            old = top[h, at, :]
            new = jnp.maximum(old, jnp.max(s, axis=1, keepdims=True))
            p = jnp.exp2((s - jnp.tile(new, (1, NZ))) * SCALE2)
            o = jnp.dot(p.astype(jnp.bfloat16), v, preferred_element_type=jnp.float32)
            alpha = jnp.exp2((old - new) * SCALE2)
            acc[h, at, :] = acc[h, at, :] * jnp.tile(alpha, (1, 2)) + o
            top[h, at, :] = new

    for r, kx in enumerate(rows):
        x = (mx + kx) % NX
        blocks = [
            (ref, i, kz)
            for ref, offsets in zip(pieces[2 * r : 2 * r + 2], (FIRST_Z, LATER_Z))
            for i, kz in enumerate(offsets)
        ]

        def one(n, carry, x=x, blocks=blocks):
            h, late = jnp.where(n == 0, 0, 1), jnp.where(n == 2, 1, 0)
            q0 = jnp.where(h == 0, me, BLOCKS - 1 - me) * HALF
            first_start, last_start = begins(q0), begins(q0 + HALF - 1)
            k0 = jnp.where(late == 0, x, 2 * NX - 1 - x) * span
            some = (k0 <= q0 + HALF - 1) & (k0 + span - 1 >= first_start)
            whole = (k0 >= last_start) & (k0 + span - 1 <= q0)
            pl.when(whole)(lambda: step(blocks, h, q0, late, k0, False))
            pl.when(some & jnp.logical_not(whole))(lambda: step(blocks, h, q0, late, k0, True))
            return carry

        lax.fori_loop(0, 3, one, 0)

    if last:
        for h in range(2):
            for g in range(GROUP):
                at = slice(g * HALF, (g + 1) * HALF)
                att[h * HALF : (h + 1) * HALF, g * HD : (g + 1) * HD] = (
                    acc[h, at, :HD] / acc[h, at, HD:]
                ).astype(jnp.bfloat16)
        w_copy.wait()
        tp = lax.axis_index("tp")
        my, mc = tp // 2, tp % 2
        width = mine_ref.shape[2]
        for k in range(NY):
            for ref, parity in ((mine_ref, mc), (other_ref, 1 - mc)):
                col = pl.multiple_of((((my + k) % NY) * 2 + parity) * width, width)
                ref[k] = jnp.dot(
                    att[...], w[:, pl.ds(col, width)], preferred_element_type=jnp.float32
                ).astype(jnp.bfloat16)


def attend_to(rows, lengths, queries, pieces, state=None, out_weight=None):
    first, last = state is None, out_weight is not None
    tokens = queries.shape[0]
    state_shape = [(2, GROUP * HALF, 2 * HD), (2, GROUP * HALF, HD)]
    outs = [jax.ShapeDtypeStruct(s, jnp.float32) for s in state_shape]
    operands = [lengths, queries] + ([out_weight] if last else []) + pieces
    operands += [] if first else list(state)
    scratch = [pltpu.SMEM(lengths.shape, jnp.int32), pltpu.SemaphoreType.DMA]
    flops = 1_100_000_000 * len(rows)
    if last:
        width = out_weight.shape[1] // (2 * NY)
        scratch = [pltpu.VMEM(s, jnp.float32) for s in state_shape] + scratch
        scratch += [
            pltpu.VMEM(queries.shape, jnp.bfloat16),
            pltpu.VMEM(out_weight.shape, jnp.bfloat16),
            pltpu.SemaphoreType.DMA,
        ]
        outs = [jax.ShapeDtypeStruct((NY, tokens, width), jnp.bfloat16)] * 2
        flops += 2_150_000_000
    return pl.pallas_call(
        functools.partial(attend, rows, first, last),
        out_shape=outs,
        in_specs=[ANY, VMEM] + ([ANY] if last else []) + [VMEM] * (len(operands) - 2 - last),
        out_specs=[VMEM] * 2,
        scratch_shapes=scratch,
        compiler_params=pltpu.CompilerParams(vmem_limit_bytes=(22 if last else 14) * 2**20),
        cost_estimate=pl.CostEstimate(
            flops=flops, bytes_accessed=6 * 2**20, transcendentals=3_000_000 * len(rows)
        ),
    )(*operands)


def on_device(queries, keys, values, lengths, out_weight):
    tokens = queries.shape[0]
    with jax.named_scope("gather_keys_values"):
        kv = pl.pallas_call(
            lay_beside,
            out_shape=jax.ShapeDtypeStruct((tokens, 2 * HD), keys.dtype),
            in_specs=[ANY] * 2,
            out_specs=VMEM,
            scratch_shapes=[pltpu.SemaphoreType.DMA] * 2,
            compiler_params=pltpu.CompilerParams(vmem_limit_bytes=2 * 2**20),
        )(keys, values)
        up2, down2 = ctx(kv, from_z(2)), ctx(kv, from_z(-2))
        up1, down1 = ctx(kv, from_z(1)), ctx(kv, from_z(-1))
        early = together([kv, up1, down1, up2, down2])
        right_a, left_a = ctx(early, from_x(1)), ctx(early, from_x(-1))
        up3, down3 = ctx(up2, from_z(1)), ctx(down2, from_z(-1))
        even = lax.axis_index("ctx") % 2 == 0
        over = ctx(jnp.where(even, up2, down2), OVER)
        later = together([up3, over, down3])
        right_b, left_b = ctx(later, from_x(1)), ctx(later, from_x(-1))
    with jax.named_scope("attend_own_row"):
        state = attend_to((0,), lengths, queries, [early, later])
    with jax.named_scope("gather_keys_values"):
        right_a, left_a = lax.optimization_barrier((right_a, left_a))
        far_a = ctx(right_a, from_x(1))
        right_b, left_b, state = lax.optimization_barrier((right_b, left_b, state))
        far_b = ctx(left_b, from_x(-1))
    with jax.named_scope("attend_next_rows"):
        state = attend_to((1, 3), lengths, queries, [right_a, right_b, left_a, left_b], state)
    with jax.named_scope("attend_far_row_and_project"):
        mine, other = attend_to((2,), lengths, queries, [far_a, far_b], state, out_weight)
    with jax.named_scope("sum_over_heads"):
        theirs = lax.ppermute(other, "tp", CORES)

        def pair(k):
            return (mine[k].astype(jnp.float32) + theirs[k].astype(jnp.float32)).astype(jnp.bfloat16)

        out = mine[0].astype(jnp.float32) + theirs[0].astype(jnp.float32)
        for k in (2, 1, 3):
            out = out + lax.ppermute(pair(k), "tp", from_y(-k)).astype(jnp.float32)
        return out.astype(jnp.bfloat16)


def solution(mesh):
    return jax.shard_map(
        on_device,
        mesh=mesh,
        in_specs=(P("ctx", "tp"), P("ctx", "tp"), P("ctx", "tp"), P(), P("tp", None)),
        out_specs=P("ctx", "tp"),
        check_vma=False,
    )
```

time: 91.6 us -> 87.2 us (0.952)
  the two profiles are of different devices: /device:TPU:1 before, /device:TPU:6 now
where the time goes in v3:
time: 87.2 us; the launch traced here: 87.1 us
  waiting for transfers between devices  35.3 us (40%)
  starting transfers between devices  27.3 us (31%)
  Pallas kernels  21.5 us (25%)
  local copies, waits for them, and re-layouts  1.75 us (2%)
  other arithmetic  1.11 us (1%)
    ppermute x13, waiting for transfers between devices, ctx(): return lax.ppermute(a, 'ctx', perm)  23.3 us
    pallas_call x3, Pallas kernels, attend_to(): pl.pallas_call(functools.partial(attend, rows, first, last), out_shape=ou...  21.4 us
    ppermute x13, starting transfers between devices, ctx(): return lax.ppermute(a, 'ctx', perm)  20.5 us
    ppermute x3, waiting for transfers between devices, on_device(): out = out + lax.ppermute(pair(k), 'tp', from_y(-k)).astype(jnp.float32)  9.42 us
    ppermute x3, starting transfers between devices, on_device(): out = out + lax.ppermute(pair(k), 'tp', from_y(-k)).astype(jnp.float32)  6.52 us
    ppermute x1, waiting for transfers between devices, on_device(): theirs = lax.ppermute(other, 'tp', CORES)  2.65 us
    unnamed x12, local copies, waits for them, and re-layouts  1.75 us
  transfers between devices with their start and end apart: 17, of which 13 were waited for; matrix products, arithmetic and copies ran while one was open for 0% of the time, Pallas kernels for 17%

profile of v3, /device:TPU:6, one launch (start us, length us, event | category | flops | bytes accessed | tf_op | source)
XLA Modules:
  0.0 87.1 jit_solution(12864071199584038352)
XLA Ops:
  0.0 0.9 %copy-done.1 = bf16[256,128]{1,0:T(8,128)(2,1)S(1)} copy-done((bf16[256,128]{1,0:T(8,128)(2,1)S(1)}, bf16[256,128]{1,0:T(8,128)(2,1)}, u32[]{:S(2)}) %copy-start.1) | copy-done | bytes 65560
  1.8 6.4 %collective-permute-start.2 = (bf16[256,256]{1,0:T(8,128)(2,1)S(1)}, bf16[256,256]{1,0:T(8,128)(2,1)S(1)}, u32[]{:S(2)}, u32[]{:S(2)}) collective-permute-start(bf16[256,256]{1,0:T(8,128)(2,1)S(1)} %gather_keys_values.3.refs_0_), channel_id=1, source_target_pairs={{16,0},{24,8},{32,16},{40,24},{48,32},{56,40},{0,48},{8,56},{80,64... | collective-permute-start | bytes 393224 | tf_op jit(solution)/shard_map/gather_keys_values/ppermute | solution.py:39
  8.2 3.7 %collective-permute-start = (bf16[256,256]{1,0:T(8,128)(2,1)S(1)}, bf16[256,256]{1,0:T(8,128)(2,1)S(1)}, u32[]{:S(2)}, u32[]{:S(2)}) collective-permute-start(bf16[256,256]{1,0:T(8,128)(2,1)S(1)} %gather_keys_values.3.refs_0_), channel_id=1, source_target_pairs={{8,0},{16,8},{24,16},{32,24},{40,32},{48,40},{56,48},{0,56},{72,64... | collective-permute-start | bytes 393224 | tf_op jit(solution)/shard_map/gather_keys_values/ppermute | solution.py:39
  11.9 2.5 %collective-permute-done.2.refs_3_ = bf16[256,256]{1,0:T(8,128)(2,1)S(1)} collective-permute-done((bf16[256,256]{1,0:T(8,128)(2,1)S(1)}, bf16[256,256]{1,0:T(8,128)(2,1)S(1)}, u32[]{:S(2)}, u32[]{:S(2)}) %collective-permute-start.2) | collective-permute-done | bytes 131104 | tf_op jit(solution)/shard_map/gather_keys_values/ppermute | solution.py:39
  14.3 4.2 %collective-permute-done.3.refs_4_ = bf16[256,256]{1,0:T(8,128)(2,1)S(1)} collective-permute-done((bf16[256,256]{1,0:T(8,128)(2,1)S(1)}, bf16[256,256]{1,0:T(8,128)(2,1)S(1)}, u32[]{:S(2)}, u32[]{:S(2)}) %collective-permute-start.3) | collective-permute-done | bytes 131104 | tf_op jit(solution)/shard_map/gather_keys_values/ppermute | solution.py:39
  18.6 1.8 %collective-permute-done.1.refs_2_ = bf16[256,256]{1,0:T(8,128)(2,1)S(1)} collective-permute-done((bf16[256,256]{1,0:T(8,128)(2,1)S(1)}, bf16[256,256]{1,0:T(8,128)(2,1)S(1)}, u32[]{:S(2)}, u32[]{:S(2)}) %collective-permute-start.1) | collective-permute-done | bytes 131104 | tf_op jit(solution)/shard_map/gather_keys_values/ppermute | solution.py:39
  20.5 0.9 %collective-permute-start.4 = (bf16[1280,256]{1,0:T(8,128)(2,1)S(1)}, bf16[1280,256]{1,0:T(8,128)(2,1)S(1)}, u32[]{:S(2)}, u32[]{:S(2)}) collective-permute-start(bf16[1280,256]{1,0:T(8,128)(2,1)S(1)} %gather_keys_values.4.refs_2_), channel_id=1, source_target_pairs={{64,0},{72,8},{80,16},{88,24},{96,32},{104,40},{112,48},{120,56},{... | collective-permute-start | bytes 1966088 | tf_op jit(solution)/shard_map/gather_keys_values/ppermute | solution.py:39
  21.4 2.4 %collective-permute-start.5 = (bf16[1280,256]{1,0:T(8,128)(2,1)S(1)}, bf16[1280,256]{1,0:T(8,128)(2,1)S(1)}, u32[]{:S(2)}, u32[]{:S(2)}) collective-permute-start(bf16[1280,256]{1,0:T(8,128)(2,1)S(1)} %gather_keys_values.4.refs_2_), channel_id=1, source_target_pairs={{192,0},{200,8},{208,16},{216,24},{224,32},{232,40},{240,48},{248,... | collective-permute-start | bytes 1966088 | tf_op jit(solution)/shard_map/gather_keys_values/ppermute | solution.py:39
  24.1 1.6 %collective-permute-start.7 = (bf16[256,256]{1,0:T(8,128)(2,1)S(1)}, bf16[256,256]{1,0:T(8,128)(2,1)S(1)}, u32[]{:S(2)}, u32[]{:S(2)}) collective-permute-start(bf16[256,256]{1,0:T(8,128)(2,1)S(1)} %collective-permute-done.2.refs_3_), channel_id=1, source_target_pairs={{8,0},{16,8},{24,16},{32,24},{40,32},{48,40},{56,48},{0,56},{72,64... | collective-permute-start | bytes 393224 | tf_op jit(solution)/shard_map/gather_keys_values/ppermute | solution.py:39
  26.1 4.4 %collective-permute-done.8.refs_1_ = bf16[256,256]{1,0:T(8,128)(2,1)S(1)} collective-permute-done((bf16[256,256]{1,0:T(8,128)(2,1)S(1)}, bf16[256,256]{1,0:T(8,128)(2,1)S(1)}, u32[]{:S(2)}, u32[]{:S(2)}) %collective-permute-start.8) | collective-permute-done | bytes 131104 | tf_op jit(solution)/shard_map/gather_keys_values/ppermute | solution.py:39
  32.0 3.2 %collective-permute-start.11 = (bf16[768,256]{1,0:T(8,128)(2,1)S(1)}, bf16[768,256]{1,0:T(8,128)(2,1)S(1)}, u32[]{:S(2)}, u32[]{:S(2)}) collective-permute-start(bf16[768,256]{1,0:T(8,128)(2,1)S(1)} %gather_keys_values.5.refs_3_), channel_id=1, source_target_pairs={{192,0},{200,8},{208,16},{216,24},{224,32},{232,40},{240,48},{248,... | collective-permute-start | bytes 1179656 | tf_op jit(solution)/shard_map/gather_keys_values/ppermute | solution.py:39
  35.2 4.2 %collective-permute-done.4.refs_2_ = bf16[1280,256]{1,0:T(8,128)(2,1)S(1)} collective-permute-done((bf16[1280,256]{1,0:T(8,128)(2,1)S(1)}, bf16[1280,256]{1,0:T(8,128)(2,1)S(1)}, u32[]{:S(2)}, u32[]{:S(2)}) %collective-permute-start.4) | collective-permute-done | bytes 655392 | tf_op jit(solution)/shard_map/gather_keys_values/ppermute | solution.py:39
  39.6 6.3 %attend_own_row.1 = (f32[2,1024,256]{2,1,0:T(8,128)S(1)}, f32[2,1024,128]{2,1,0:T(8,128)S(1)}) custom-call(s32[4]{0:T(128)S(1)} %copy-done.3, bf16[256,1024]{1,0:T(8,128)(2,1)S(1)} %copy-done, bf16[1280,256]{1,0:T(8,128)(2,1)S(1)} %gather_keys_values.4.refs_2_, bf16[768,256]{1,0:T(8,128)(2,1)S(1)} %gather_keys_values.5.refs_3_), custom_call_target="tpu_custom_call" | custom-call | flops 1100000000 | bytes 6291456 | tf_op jit(solution)/shard_map/attend_own_row/pallas_call | solution.py:206
  45.9 1.9 %collective-permute-done.10.refs_3_ = bf16[768,256]{1,0:T(8,128)(2,1)S(1)} collective-permute-done((bf16[768,256]{1,0:T(8,128)(2,1)S(1)}, bf16[768,256]{1,0:T(8,128)(2,1)S(1)}, u32[]{:S(2)}, u32[]{:S(2)}) %collective-permute-start.10) | collective-permute-done | bytes 393248 | tf_op jit(solution)/shard_map/gather_keys_values/ppermute | solution.py:39
  47.9 1.3 %collective-permute-start.12 = (bf16[768,256]{1,0:T(8,128)(2,1)S(1)}, bf16[768,256]{1,0:T(8,128)(2,1)S(1)}, u32[]{:S(2)}, u32[]{:S(2)}) collective-permute-start(bf16[768,256]{1,0:T(8,128)(2,1)S(1)} %collective-permute-done.11.refs_5_), channel_id=1, source_target_pairs={{192,0},{200,8},{208,16},{216,24},{224,32},{232,40},{240,48},{248,... | collective-permute-start | bytes 1179656 | tf_op jit(solution)/shard_map/gather_keys_values/ppermute | solution.py:39
  49.2 8.2 %attend_next_rows.1 = (f32[2,1024,256]{2,1,0:T(8,128)S(1)}, f32[2,1024,128]{2,1,0:T(8,128)S(1)}) custom-call(s32[4]{0:T(128)S(1)} %copy-done.3, bf16[256,1024]{1,0:T(8,128)(2,1)S(1)} %copy-done, bf16[1280,256]{1,0:T(8,128)(2,1)S(1)} %collective-permute-done.4.refs_2_, bf16[768,256]{1,0:T(8,128)(2,1)S(1)} %collective-permute-done.10.refs_3_, ...), custom_call_target="tpu_custom_call" | custom-call | flops 2200000000 | bytes 6291456 | tf_op jit(solution)/shard_map/attend_next_rows/pallas_call | solution.py:206
  57.4 2.8 %collective-permute-done.6.refs_3_ = bf16[1280,256]{1,0:T(8,128)(2,1)S(1)} collective-permute-done((bf16[1280,256]{1,0:T(8,128)(2,1)S(1)}, bf16[1280,256]{1,0:T(8,128)(2,1)S(1)}, u32[]{:S(2)}, u32[]{:S(2)}) %collective-permute-start.6) | collective-permute-done | bytes 655392 | tf_op jit(solution)/shard_map/gather_keys_values/ppermute | solution.py:39
  60.2 6.8 %attend_far_row_and_project.1 = (bf16[4,256,512]{2,1,0:T(8,128)(2,1)S(1)}, bf16[4,256,512]{2,1,0:T(8,128)(2,1)S(1)}) custom-call(s32[4]{0:T(128)S(1)} %copy-done.3, bf16[256,1024]{1,0:T(8,128)(2,1)S(1)} %copy-done, bf16[1024,4096]{1,0:T(8,128)(2,1)S(1)} %bitcast.15, bf16[1280,256]{1,0:T(8,128)(2,1)S(1)} %collective-permute-done.6.refs_3_, ...), custom_call_target="tpu_custom_call" | custom-call | flops 3249999872 | bytes 6291456 | tf_op jit(solution)/shard_map/attend_far_row_and_project/pallas_call | solution.py:206
  67.4 2.6 %collective-permute-done.13 = bf16[4,256,512]{2,1,0:T(8,128)(2,1)S(1)} collective-permute-done((bf16[4,256,512]{2,1,0:T(8,128)(2,1)S(1)}, bf16[4,256,512]{2,1,0:T(8,128)(2,1)S(1)}, u32[]{:S(2)}, u32[]{:S(2)}) %collective-permute-start.13) | collective-permute-done | bytes 1048608 | tf_op jit(solution)/shard_map/sum_over_heads/ppermute | solution.py:251
  70.3 3.3 %collective-permute-start.14 = (bf16[256,512]{1,0:T(8,128)(2,1)S(1)}, bf16[256,512]{1,0:T(8,128)(2,1)S(1)}, u32[]{:S(2)}, u32[]{:S(2)}) collective-permute-start(bf16[256,512]{1,0:T(8,128)(2,1)S(1)} %get-tuple-element.29), channel_id=1, source_target_pairs={{4,0},{5,1},{6,2},{7,3},{0,4},{1,5},{2,6},{3,7},{12,8},{13,9},{14,... | collective-permute-start | bytes 786440 | tf_op jit(solution)/shard_map/sum_over_heads/ppermute | solution.py:258
  74.3 2.6 %collective-permute-start.16 = (bf16[256,512]{1,0:T(8,128)(2,1)S(1)}, bf16[256,512]{1,0:T(8,128)(2,1)S(1)}, u32[]{:S(2)}, u32[]{:S(2)}) collective-permute-start(bf16[256,512]{1,0:T(8,128)(2,1)S(1)} %get-tuple-element.30), channel_id=1, source_target_pairs={{2,0},{3,1},{4,2},{5,3},{6,4},{7,5},{0,6},{1,7},{10,8},{11,9},{12,... | collective-permute-start | bytes 786440 | tf_op jit(solution)/shard_map/sum_over_heads/ppermute | solution.py:258
  76.8 4.3 %collective-permute-done.14 = bf16[256,512]{1,0:T(8,128)(2,1)S(1)} collective-permute-done((bf16[256,512]{1,0:T(8,128)(2,1)S(1)}, bf16[256,512]{1,0:T(8,128)(2,1)S(1)}, u32[]{:S(2)}, u32[]{:S(2)}) %collective-permute-start.14) | collective-permute-done | bytes 262176 | tf_op jit(solution)/shard_map/sum_over_heads/ppermute | solution.py:258
  81.1 4.8 %collective-permute-done.15 = bf16[256,512]{1,0:T(8,128)(2,1)S(1)} collective-permute-done((bf16[256,512]{1,0:T(8,128)(2,1)S(1)}, bf16[256,512]{1,0:T(8,128)(2,1)S(1)}, u32[]{:S(2)}, u32[]{:S(2)}) %collective-permute-start.15) | collective-permute-done | bytes 262176 | tf_op jit(solution)/shard_map/sum_over_heads/ppermute | solution.py:258
  86.2 0.9 %fusion.2 = bf16[256,512]{1,0:T(8,128)(2,1)} fusion(bf16[256,512]{1,0:T(8,128)(2,1)S(1)} %collective-permute-done.16, bf16[256,512]{1,0:T(8,128)(2,1)S(1)} %collective-permute-done.15, bf16[256,512]{1,0:T(8,128)(2,1)S(1)} %collective-permute-done.14, bf16[4,256,512]{2,1,0:T(8,128)(2,1)S(1)} %collective-permute-done.13, ...), kind=kLoop, calls=%fused_computation.3 | loop fusion | flops 1310720 | bytes 1572864 | tf_op jit(solution)/shard_map/sum_over_heads/convert_element_type | solution.py:259
  (32 shorter events, 4.9 us)
Async XLA Ops:
  0.0 39.6 %copy-start = (bf16[256,1024]{1,0:T(8,128)(2,1)S(1)}, bf16[256,1024]{1,0:T(8,128)(2,1)}, u32[]{:S(2)}) copy-start(bf16[256,1024]{1,0:T(8,128)(2,1)} %refs_1_.5) | copy-start | bytes 1572868
  0.0 0.9 %copy-start.1 = (bf16[256,128]{1,0:T(8,128)(2,1)S(1)}, bf16[256,128]{1,0:T(8,128)(2,1)}, u32[]{:S(2)}) copy-start(bf16[256,128]{1,0:T(8,128)(2,1)} %k_hbm.1) | copy-start | bytes 196612
  0.9 0.8 copy-start.2
  1.7 37.8 %copy-start.3 = (s32[4]{0:T(128)S(1)}, s32[4]{0:T(128)}, u32[]{:S(2)}) copy-start(s32[4]{0:T(128)} %refs_0_.5) | copy-start | bytes 52
  1.8 12.5 %collective-permute-start.2 = (bf16[256,256]{1,0:T(8,128)(2,1)S(1)}, bf16[256,256]{1,0:T(8,128)(2,1)S(1)}, u32[]{:S(2)}, u32[]{:S(2)}) collective-permute-start(bf16[256,256]{1,0:T(8,128)(2,1)S(1)} %gather_keys_values.3.refs_0_), channel_id=1, source_target_pairs={{16,0},{24,8},{32,16},{40,24},{48,32},{56,40},{0,48},{8,56},{80,64... | collective-permute-start | bytes 393224 | tf_op jit(solution)/shard_map/gather_keys_values/ppermute | solution.py:39
  8.2 10.4 %collective-permute-start.3 = (bf16[256,256]{1,0:T(8,128)(2,1)S(1)}, bf16[256,256]{1,0:T(8,128)(2,1)S(1)}, u32[]{:S(2)}, u32[]{:S(2)}) collective-permute-start(bf16[256,256]{1,0:T(8,128)(2,1)S(1)} %gather_keys_values.3.refs_0_), channel_id=1, source_target_pairs={{48,0},{56,8},{0,16},{8,24},{16,32},{24,40},{32,48},{40,56},{112,6... | collective-permute-start | bytes 393224 | tf_op jit(solution)/shard_map/gather_keys_values/ppermute | solution.py:39
  8.2 10.4 %collective-permute-start = (bf16[256,256]{1,0:T(8,128)(2,1)S(1)}, bf16[256,256]{1,0:T(8,128)(2,1)S(1)}, u32[]{:S(2)}, u32[]{:S(2)}) collective-permute-start(bf16[256,256]{1,0:T(8,128)(2,1)S(1)} %gather_keys_values.3.refs_0_), channel_id=1, source_target_pairs={{8,0},{16,8},{24,16},{32,24},{40,32},{48,40},{56,48},{0,56},{72,64... | collective-permute-start | bytes 393224 | tf_op jit(solution)/shard_map/gather_keys_values/ppermute | solution.py:39
  11.9 8.5 %collective-permute-start.1 = (bf16[256,256]{1,0:T(8,128)(2,1)S(1)}, bf16[256,256]{1,0:T(8,128)(2,1)S(1)}, u32[]{:S(2)}, u32[]{:S(2)}) collective-permute-start(bf16[256,256]{1,0:T(8,128)(2,1)S(1)} %gather_keys_values.3.refs_0_), channel_id=1, source_target_pairs={{56,0},{0,8},{8,16},{16,24},{24,32},{32,40},{40,48},{48,56},{120,6... | collective-permute-start | bytes 393224 | tf_op jit(solution)/shard_map/gather_keys_values/ppermute | solution.py:39
  20.5 19.0 %collective-permute-start.4 = (bf16[1280,256]{1,0:T(8,128)(2,1)S(1)}, bf16[1280,256]{1,0:T(8,128)(2,1)S(1)}, u32[]{:S(2)}, u32[]{:S(2)}) collective-permute-start(bf16[1280,256]{1,0:T(8,128)(2,1)S(1)} %gather_keys_values.4.refs_2_), channel_id=1, source_target_pairs={{64,0},{72,8},{80,16},{88,24},{96,32},{104,40},{112,48},{120,56},{... | collective-permute-start | bytes 1966088 | tf_op jit(solution)/shard_map/gather_keys_values/ppermute | solution.py:39
  21.4 18.1 %collective-permute-start.5 = (bf16[1280,256]{1,0:T(8,128)(2,1)S(1)}, bf16[1280,256]{1,0:T(8,128)(2,1)S(1)}, u32[]{:S(2)}, u32[]{:S(2)}) collective-permute-start(bf16[1280,256]{1,0:T(8,128)(2,1)S(1)} %gather_keys_values.4.refs_2_), channel_id=1, source_target_pairs={{192,0},{200,8},{208,16},{216,24},{224,32},{232,40},{240,48},{248,... | collective-permute-start | bytes 1966088 | tf_op jit(solution)/shard_map/gather_keys_values/ppermute | solution.py:39
  23.8 6.8 %collective-permute-start.8 = (bf16[256,256]{1,0:T(8,128)(2,1)S(1)}, bf16[256,256]{1,0:T(8,128)(2,1)S(1)}, u32[]{:S(2)}, u32[]{:S(2)}) collective-permute-start(bf16[256,256]{1,0:T(8,128)(2,1)S(1)} %broadcast_select_fusion), channel_id=1, source_target_pairs={{16,0},{56,8},{32,16},{8,24},{48,32},{24,40},{0,48},{40,56},{80,64... | collective-permute-start | bytes 393224 | tf_op jit(solution)/shard_map/gather_keys_values/ppermute | solution.py:39
  24.1 6.9 %collective-permute-start.7 = (bf16[256,256]{1,0:T(8,128)(2,1)S(1)}, bf16[256,256]{1,0:T(8,128)(2,1)S(1)}, u32[]{:S(2)}, u32[]{:S(2)}) collective-permute-start(bf16[256,256]{1,0:T(8,128)(2,1)S(1)} %collective-permute-done.2.refs_3_), channel_id=1, source_target_pairs={{8,0},{16,8},{24,16},{32,24},{40,32},{48,40},{56,48},{0,56},{72,64... | collective-permute-start | bytes 393224 | tf_op jit(solution)/shard_map/gather_keys_values/ppermute | solution.py:39
  25.7 6.2 %collective-permute-start.9 = (bf16[256,256]{1,0:T(8,128)(2,1)S(1)}, bf16[256,256]{1,0:T(8,128)(2,1)S(1)}, u32[]{:S(2)}, u32[]{:S(2)}) collective-permute-start(bf16[256,256]{1,0:T(8,128)(2,1)S(1)} %collective-permute-done.3.refs_4_), channel_id=1, source_target_pairs={{56,0},{0,8},{8,16},{16,24},{24,32},{32,40},{40,48},{48,56},{120,6... | collective-permute-start | bytes 393224 | tf_op jit(solution)/shard_map/gather_keys_values/ppermute | solution.py:39
  31.9 16.0 %collective-permute-start.10 = (bf16[768,256]{1,0:T(8,128)(2,1)S(1)}, bf16[768,256]{1,0:T(8,128)(2,1)S(1)}, u32[]{:S(2)}, u32[]{:S(2)}) collective-permute-start(bf16[768,256]{1,0:T(8,128)(2,1)S(1)} %gather_keys_values.5.refs_3_), channel_id=1, source_target_pairs={{64,0},{72,8},{80,16},{88,24},{96,32},{104,40},{112,48},{120,56},{... | collective-permute-start | bytes 1179656 | tf_op jit(solution)/shard_map/gather_keys_values/ppermute | solution.py:39
  32.0 15.9 %collective-permute-start.11 = (bf16[768,256]{1,0:T(8,128)(2,1)S(1)}, bf16[768,256]{1,0:T(8,128)(2,1)S(1)}, u32[]{:S(2)}, u32[]{:S(2)}) collective-permute-start(bf16[768,256]{1,0:T(8,128)(2,1)S(1)} %gather_keys_values.5.refs_3_), channel_id=1, source_target_pairs={{192,0},{200,8},{208,16},{216,24},{224,32},{232,40},{240,48},{248,... | collective-permute-start | bytes 1179656 | tf_op jit(solution)/shard_map/gather_keys_values/ppermute | solution.py:39
  39.4 20.8 %collective-permute-start.6 = (bf16[1280,256]{1,0:T(8,128)(2,1)S(1)}, bf16[1280,256]{1,0:T(8,128)(2,1)S(1)}, u32[]{:S(2)}, u32[]{:S(2)}) collective-permute-start(bf16[1280,256]{1,0:T(8,128)(2,1)S(1)} %collective-permute-done.4.refs_2_), channel_id=1, source_target_pairs={{64,0},{72,8},{80,16},{88,24},{96,32},{104,40},{112,48},{120,56},{... | collective-permute-start | bytes 1966088 | tf_op jit(solution)/shard_map/gather_keys_values/ppermute | solution.py:39
  39.6 20.7 %slice-start = ((s8[8388608]{0:T(1024)(128)(4,1)}), s8[4194304]{0:T(1024)(128)(4,1)S(1)}, s32[]{:S(2)}) async-start(s8[8388608]{0:T(1024)(128)(4,1)} %bitcast.14), calls=%async_computation | async-start | bytes 8388608
  47.8 12.4 %slice-start.1 = ((s8[8388608]{0:T(1024)(128)(4,1)}), s8[4194304]{0:T(1024)(128)(4,1)S(1)}, s32[]{:S(2)}) async-start(s8[8388608]{0:T(1024)(128)(4,1)} %bitcast.14), calls=%async_computation.1 | async-start | bytes 8388608
  47.9 9.5 %collective-permute-start.12 = (bf16[768,256]{1,0:T(8,128)(2,1)S(1)}, bf16[768,256]{1,0:T(8,128)(2,1)S(1)}, u32[]{:S(2)}, u32[]{:S(2)}) collective-permute-start(bf16[768,256]{1,0:T(8,128)(2,1)S(1)} %collective-permute-done.11.refs_5_), channel_id=1, source_target_pairs={{192,0},{200,8},{208,16},{216,24},{224,32},{232,40},{240,48},{248,... | collective-permute-start | bytes 1179656 | tf_op jit(solution)/shard_map/gather_keys_values/ppermute | solution.py:39
  67.1 3.0 %collective-permute-start.13 = (bf16[4,256,512]{2,1,0:T(8,128)(2,1)S(1)}, bf16[4,256,512]{2,1,0:T(8,128)(2,1)S(1)}, u32[]{:S(2)}, u32[]{:S(2)}) collective-permute-start(bf16[4,256,512]{2,1,0:T(8,128)(2,1)S(1)} %get-tuple-element.28), channel_id=1, source_target_pairs={{0,1},{1,0},{2,3},{3,2},{4,5},{5,4},{6,7},{7,6},{8,9},{9,8},{10,11... | collective-permute-start | bytes 3145736 | tf_op jit(solution)/shard_map/sum_over_heads/ppermute | solution.py:251
  70.3 10.8 %collective-permute-start.14 = (bf16[256,512]{1,0:T(8,128)(2,1)S(1)}, bf16[256,512]{1,0:T(8,128)(2,1)S(1)}, u32[]{:S(2)}, u32[]{:S(2)}) collective-permute-start(bf16[256,512]{1,0:T(8,128)(2,1)S(1)} %get-tuple-element.29), channel_id=1, source_target_pairs={{4,0},{5,1},{6,2},{7,3},{0,4},{1,5},{2,6},{3,7},{12,8},{13,9},{14,... | collective-permute-start | bytes 786440 | tf_op jit(solution)/shard_map/sum_over_heads/ppermute | solution.py:258
  73.6 12.3 %collective-permute-start.15 = (bf16[256,512]{1,0:T(8,128)(2,1)S(1)}, bf16[256,512]{1,0:T(8,128)(2,1)S(1)}, u32[]{:S(2)}, u32[]{:S(2)}) collective-permute-start(bf16[256,512]{1,0:T(8,128)(2,1)S(1)} %get-tuple-element.31), channel_id=1, source_target_pairs={{6,0},{7,1},{0,2},{1,3},{2,4},{3,5},{4,6},{5,7},{14,8},{15,9},{8,1... | collective-permute-start | bytes 786440 | tf_op jit(solution)/shard_map/sum_over_heads/ppermute | solution.py:258
  74.3 12.0 %collective-permute-start.16 = (bf16[256,512]{1,0:T(8,128)(2,1)S(1)}, bf16[256,512]{1,0:T(8,128)(2,1)S(1)}, u32[]{:S(2)}, u32[]{:S(2)}) collective-permute-start(bf16[256,512]{1,0:T(8,128)(2,1)S(1)} %get-tuple-element.30), channel_id=1, source_target_pairs={{2,0},{3,1},{4,2},{5,3},{6,4},{7,5},{0,6},{1,7},{10,8},{11,9},{12,... | collective-permute-start | bytes 786440 | tf_op jit(solution)/shard_map/sum_over_heads/ppermute | solution.py:258

commit v4 on v3

--- a/solution.py
+++ b/solution.py
@@ -39,17 +39,6 @@
     return lax.ppermute(a, "ctx", perm)
 
 
-def lay_beside(k_hbm, v_hbm, out, k_sem, v_sem):
-    copies = [
-        pltpu.make_async_copy(k_hbm, out.at[:, pl.ds(0, HD)], k_sem),
-        pltpu.make_async_copy(v_hbm, out.at[:, pl.ds(HD, HD)], v_sem),
-    ]
-    for copy in copies:
-        copy.start()
-    for copy in copies:
-        copy.wait()
-
-
 def lay_together(*refs):
     at = 0
     for piece in refs[:-1]:
@@ -72,10 +61,10 @@
     refs = list(refs)
     take = lambda n: [refs.pop(0) for _ in range(n)]
     len_hbm, q = take(2)
-    w_hbm = take(1)[0] if last else None
+    w = take(1)[0] if last else None
     pieces = take(2 * len(rows))
     state = [] if first else take(2)
-    mine_ref, other_ref = take(2) if last else (None, None)
+    att, mine_ref, other_ref = take(3) if last else (None, None, None)
     acc, top, lens, len_sem = take(4)
     me = lax.axis_index("ctx")
     mx, mz = me // NZ, me % NZ
@@ -83,10 +72,6 @@
 
     len_copy = pltpu.make_async_copy(len_hbm, lens, len_sem)
     len_copy.start()
-    if last:
-        att, w, w_sem = take(3)
-        w_copy = pltpu.make_async_copy(w_hbm, w, w_sem)
-        w_copy.start()
     if first:
         acc[...] = jnp.zeros_like(acc)
         top[...] = jnp.full_like(top, NEG)
@@ -172,16 +157,37 @@
                 att[h * HALF : (h + 1) * HALF, g * HD : (g + 1) * HD] = (
                     acc[h, at, :HD] / acc[h, at, HD:]
                 ).astype(jnp.bfloat16)
-        w_copy.wait()
-        tp = lax.axis_index("tp")
-        my, mc = tp // 2, tp % 2
-        width = mine_ref.shape[2]
-        for k in range(NY):
-            for ref, parity in ((mine_ref, mc), (other_ref, 1 - mc)):
-                col = pl.multiple_of((((my + k) % NY) * 2 + parity) * width, width)
-                ref[k] = jnp.dot(
-                    att[...], w[:, pl.ds(col, width)], preferred_element_type=jnp.float32
-                ).astype(jnp.bfloat16)
+        for ref, same in ((other_ref, False), (mine_ref, True)):
+            ref[...] = projected(att, w, 2, same)
+
+
+def projected(att, w, k, same):
+    tp = lax.axis_index("tp")
+    width = w.shape[1] // (2 * NY)
+    core = tp % 2 if same else 1 - tp % 2
+    col = pl.multiple_of((((tp // 2 + k) % NY) * 2 + core) * width, width)
+    return jnp.dot(
+        att[...], w[:, pl.ds(col, width)], preferred_element_type=jnp.float32
+    ).astype(jnp.bfloat16)
+
+
+def project(ks, same, att, w, out):
+    for i, k in enumerate(ks):
+        out[i] = projected(att, w, k, same)
+
+
+def project_to(ks, same, att, out_weight):
+    shape = (len(ks), att.shape[0], out_weight.shape[1] // (2 * NY))
+    return pl.pallas_call(
+        functools.partial(project, ks, same),
+        out_shape=jax.ShapeDtypeStruct(shape, jnp.bfloat16),
+        in_specs=[VMEM] * 2,
+        out_specs=VMEM,
+        compiler_params=pltpu.CompilerParams(vmem_limit_bytes=14 * 2**20),
+        cost_estimate=pl.CostEstimate(
+            flops=270_000_000 * len(ks), bytes_accessed=2**20, transcendentals=0
+        ),
+    )(att, out_weight)
 
 
 def attend_to(rows, lengths, queries, pieces, state=None, out_weight=None):
@@ -196,18 +202,14 @@
     if last:
         width = out_weight.shape[1] // (2 * NY)
         scratch = [pltpu.VMEM(s, jnp.float32) for s in state_shape] + scratch
-        scratch += [
-            pltpu.VMEM(queries.shape, jnp.bfloat16),
-            pltpu.VMEM(out_weight.shape, jnp.bfloat16),
-            pltpu.SemaphoreType.DMA,
-        ]
-        outs = [jax.ShapeDtypeStruct((NY, tokens, width), jnp.bfloat16)] * 2
-        flops += 2_150_000_000
+        outs = [jax.ShapeDtypeStruct(queries.shape, jnp.bfloat16)]
+        outs += [jax.ShapeDtypeStruct((tokens, width), jnp.bfloat16)] * 2
+        flops += 540_000_000
     return pl.pallas_call(
         functools.partial(attend, rows, first, last),
         out_shape=outs,
-        in_specs=[ANY, VMEM] + ([ANY] if last else []) + [VMEM] * (len(operands) - 2 - last),
-        out_specs=[VMEM] * 2,
+        in_specs=[ANY] + [VMEM] * (len(operands) - 1),
+        out_specs=[VMEM] * len(outs),
         scratch_shapes=scratch,
         compiler_params=pltpu.CompilerParams(vmem_limit_bytes=(22 if last else 14) * 2**20),
         cost_estimate=pl.CostEstimate(
@@ -219,14 +221,12 @@
 def on_device(queries, keys, values, lengths, out_weight):
     tokens = queries.shape[0]
     with jax.named_scope("gather_keys_values"):
-        kv = pl.pallas_call(
-            lay_beside,
-            out_shape=jax.ShapeDtypeStruct((tokens, 2 * HD), keys.dtype),
-            in_specs=[ANY] * 2,
-            out_specs=VMEM,
-            scratch_shapes=[pltpu.SemaphoreType.DMA] * 2,
-            compiler_params=pltpu.CompilerParams(vmem_limit_bytes=2 * 2**20),
-        )(keys, values)
+        lane = lax.broadcasted_iota(jnp.int32, (tokens, 2 * HD), 1)
+        kv = jnp.where(
+            lane < HD,
+            jnp.pad(keys, ((0, 0), (0, HD))),
+            jnp.pad(values, ((0, 0), (HD, 0))),
+        )
         up2, down2 = ctx(kv, from_z(2)), ctx(kv, from_z(-2))
         up1, down1 = ctx(kv, from_z(1)), ctx(kv, from_z(-1))
         early = together([kv, up1, down1, up2, down2])
@@ -246,17 +246,23 @@
     with jax.named_scope("attend_next_rows"):
         state = attend_to((1, 3), lengths, queries, [right_a, right_b, left_a, left_b], state)
     with jax.named_scope("attend_far_row_and_project"):
-        mine, other = attend_to((2,), lengths, queries, [far_a, far_b], state, out_weight)
+        att, mine_2, other_2 = attend_to((2,), lengths, queries, [far_a, far_b], state, out_weight)
     with jax.named_scope("sum_over_heads"):
+
+        def pair(a, b):
+            return (a.astype(jnp.float32) + b.astype(jnp.float32)).astype(jnp.bfloat16)
+
+        near = (0, 1, 3)
+        theirs_2 = lax.ppermute(other_2, "tp", CORES)
+        other = project_to(near, False, att, out_weight)
+        theirs_2, other = lax.optimization_barrier((theirs_2, other))
         theirs = lax.ppermute(other, "tp", CORES)
-
-        def pair(k):
-            return (mine[k].astype(jnp.float32) + theirs[k].astype(jnp.float32)).astype(jnp.bfloat16)
-
-        out = mine[0].astype(jnp.float32) + theirs[0].astype(jnp.float32)
-        for k in (2, 1, 3):
-            out = out + lax.ppermute(pair(k), "tp", from_y(-k)).astype(jnp.float32)
-        return out.astype(jnp.bfloat16)
+        total = lax.ppermute(pair(mine_2, theirs_2), "tp", from_y(2)).astype(jnp.float32)
+        mine = project_to(near, True, att, out_weight)
+        for i, k in ((1, 1), (2, 3)):
+            total += lax.ppermute(pair(mine[i], theirs[i]), "tp", from_y(-k)).astype(jnp.float32)
+        total += mine[0].astype(jnp.float32) + theirs[0].astype(jnp.float32)
+        return total.astype(jnp.bfloat16)
 
 
 def solution(mesh):

time: 87.2 us -> 84.1 us (0.964)
  waiting for transfers between devices: 35.3 us -> 33.1 us
  local copies, waits for them, and re-layouts: 1.75 us -> 0.01 us
  other arithmetic: 1.11 us -> 2.05 us
    ppermute x1, waiting for transfers between devices: 2.65 us -> 0.01 us  [on_device(): theirs = lax.ppermute(other, 'tp', CORES)]
    pallas_call x3, Pallas kernels: 21.4 us -> 19.4 us  [attend_to(): pl.pallas_call(functools.partial(attend, rows, first, last), out_shape=ou...]
    pallas_call x1 -> x2, Pallas kernels: 0.04 us -> 1.99 us  [project_to(): pl.pallas_call(functools.partial(project, ks, same), out_shape=jax.ShapeD...]
    unnamed x12 -> x8, local copies, waits for them, and re-layouts: 1.75 us -> 0.01 us
    select_n x0 -> x1, other arithmetic: none -> 0.96 us  [on_device(): jnp.where(lane < HD, jnp.pad(keys, ((0, 0), (0, HD))), jnp.pad(values, ((...]
    ppermute x3 -> x4, waiting for transfers between devices: 9.42 us -> 9.82 us  [the longest x2 5.3 us: on_device(): lax.ppermute(pair(mine[i], theirs[i]), 'tp', from_y(-k)).astype(jnp.float32)]
    ppermute x3 -> x4, starting transfers between devices: 6.52 us -> 6.7 us  [the longest x2 3.31 us: on_device(): lax.ppermute(pair(mine[i], theirs[i]), 'tp', from_y(-k)).astype(jnp.float32)]
  transfers between devices with their start and end apart: 17 -> 18, of which waited for: 13 -> 13; matrix products, arithmetic and copies ran while one was open for 0% -> 0% of each run, Pallas kernels for 17% -> 20%
where the time goes in v4:
time: 84.1 us; the launch traced here: 84.2 us
  waiting for transfers between devices  33.1 us (39%)
  starting transfers between devices  27.5 us (33%)
  Pallas kernels  21.5 us (26%)
  other arithmetic  2.05 us (2%)
    ppermute x13, waiting for transfers between devices, ctx(): return lax.ppermute(a, 'ctx', perm)  23.3 us
    ppermute x13, starting transfers between devices, ctx(): return lax.ppermute(a, 'ctx', perm)  20.5 us
    pallas_call x3, Pallas kernels, attend_to(): pl.pallas_call(functools.partial(attend, rows, first, last), out_shape=ou...  19.4 us
    ppermute x2, waiting for transfers between devices, on_device(): lax.ppermute(pair(mine[i], theirs[i]), 'tp', from_y(-k)).astype(jnp.float32)  5.3 us
    ppermute x1, waiting for transfers between devices, on_device(): lax.ppermute(pair(mine_2, theirs_2), 'tp', from_y(2)).astype(jnp.float32)  4.02 us
    ppermute x2, starting transfers between devices, on_device(): lax.ppermute(pair(mine[i], theirs[i]), 'tp', from_y(-k)).astype(jnp.float32)  3.31 us
    ppermute x1, starting transfers between devices, on_device(): lax.ppermute(pair(mine_2, theirs_2), 'tp', from_y(2)).astype(jnp.float32)  3.29 us
    pallas_call x2, Pallas kernels, project_to(): pl.pallas_call(functools.partial(project, ks, same), out_shape=jax.ShapeD...  1.99 us
  transfers between devices with their start and end apart: 18, of which 13 were waited for; matrix products, arithmetic and copies ran while one was open for 0% of the time, Pallas kernels for 20%

profile of v4, /device:TPU:6, one launch (start us, length us, event | category | flops | bytes accessed | tf_op | source)
XLA Modules:
  0.0 84.2 jit_solution(398771404126462467)
XLA Ops:
  0.0 1.0 %pad_select_fusion.refs_0_ = bf16[256,256]{1,0:T(8,128)(2,1)S(1)} fusion(bf16[256,128]{1,0:T(8,128)(2,1)} %param.7, bf16[256,128]{1,0:T(8,128)(2,1)} %param.6, pred[256]{0:T(512)(128)(4,1)S(1)} %iota_compare_fusion), kind=kLoop, calls=%fused_computation.7 | loop fusion | flops 65536 | bytes 262400 | tf_op jit(solution)/shard_map/gather_keys_values/jit(_where)/select_n | solution.py:225
  1.0 6.4 %collective-permute-start.2 = (bf16[256,256]{1,0:T(8,128)(2,1)S(1)}, bf16[256,256]{1,0:T(8,128)(2,1)S(1)}, u32[]{:S(2)}, u32[]{:S(2)}) collective-permute-start(bf16[256,256]{1,0:T(8,128)(2,1)S(1)} %pad_select_fusion.refs_0_), channel_id=1, source_target_pairs={{16,0},{24,8},{32,16},{40,24},{48,32},{56,40},{0,48},{8,56},{80,64... | collective-permute-start | bytes 393224 | tf_op jit(solution)/shard_map/gather_keys_values/ppermute | solution.py:39
  7.4 3.7 %collective-permute-start = (bf16[256,256]{1,0:T(8,128)(2,1)S(1)}, bf16[256,256]{1,0:T(8,128)(2,1)S(1)}, u32[]{:S(2)}, u32[]{:S(2)}) collective-permute-start(bf16[256,256]{1,0:T(8,128)(2,1)S(1)} %pad_select_fusion.refs_0_), channel_id=1, source_target_pairs={{8,0},{16,8},{24,16},{32,24},{40,32},{48,40},{56,48},{0,56},{72,64... | collective-permute-start | bytes 393224 | tf_op jit(solution)/shard_map/gather_keys_values/ppermute | solution.py:39
  11.0 2.5 %collective-permute-done.2.refs_3_ = bf16[256,256]{1,0:T(8,128)(2,1)S(1)} collective-permute-done((bf16[256,256]{1,0:T(8,128)(2,1)S(1)}, bf16[256,256]{1,0:T(8,128)(2,1)S(1)}, u32[]{:S(2)}, u32[]{:S(2)}) %collective-permute-start.2) | collective-permute-done | bytes 131104 | tf_op jit(solution)/shard_map/gather_keys_values/ppermute | solution.py:39
  13.5 4.2 %collective-permute-done.3.refs_4_ = bf16[256,256]{1,0:T(8,128)(2,1)S(1)} collective-permute-done((bf16[256,256]{1,0:T(8,128)(2,1)S(1)}, bf16[256,256]{1,0:T(8,128)(2,1)S(1)}, u32[]{:S(2)}, u32[]{:S(2)}) %collective-permute-start.3) | collective-permute-done | bytes 131104 | tf_op jit(solution)/shard_map/gather_keys_values/ppermute | solution.py:39
  17.7 1.8 %collective-permute-done.1.refs_2_ = bf16[256,256]{1,0:T(8,128)(2,1)S(1)} collective-permute-done((bf16[256,256]{1,0:T(8,128)(2,1)S(1)}, bf16[256,256]{1,0:T(8,128)(2,1)S(1)}, u32[]{:S(2)}, u32[]{:S(2)}) %collective-permute-start.1) | collective-permute-done | bytes 131104 | tf_op jit(solution)/shard_map/gather_keys_values/ppermute | solution.py:39
  19.6 0.9 %collective-permute-start.4 = (bf16[1280,256]{1,0:T(8,128)(2,1)S(1)}, bf16[1280,256]{1,0:T(8,128)(2,1)S(1)}, u32[]{:S(2)}, u32[]{:S(2)}) collective-permute-start(bf16[1280,256]{1,0:T(8,128)(2,1)S(1)} %gather_keys_values.2.refs_2_), channel_id=1, source_target_pairs={{64,0},{72,8},{80,16},{88,24},{96,32},{104,40},{112,48},{120,56},{... | collective-permute-start | bytes 1966088 | tf_op jit(solution)/shard_map/gather_keys_values/ppermute | solution.py:39
  20.5 2.4 %collective-permute-start.5 = (bf16[1280,256]{1,0:T(8,128)(2,1)S(1)}, bf16[1280,256]{1,0:T(8,128)(2,1)S(1)}, u32[]{:S(2)}, u32[]{:S(2)}) collective-permute-start(bf16[1280,256]{1,0:T(8,128)(2,1)S(1)} %gather_keys_values.2.refs_2_), channel_id=1, source_target_pairs={{192,0},{200,8},{208,16},{216,24},{224,32},{232,40},{240,48},{248,... | collective-permute-start | bytes 1966088 | tf_op jit(solution)/shard_map/gather_keys_values/ppermute | solution.py:39
  23.3 1.6 %collective-permute-start.7 = (bf16[256,256]{1,0:T(8,128)(2,1)S(1)}, bf16[256,256]{1,0:T(8,128)(2,1)S(1)}, u32[]{:S(2)}, u32[]{:S(2)}) collective-permute-start(bf16[256,256]{1,0:T(8,128)(2,1)S(1)} %collective-permute-done.2.refs_3_), channel_id=1, source_target_pairs={{8,0},{16,8},{24,16},{32,24},{40,32},{48,40},{56,48},{0,56},{72,64... | collective-permute-start | bytes 393224 | tf_op jit(solution)/shard_map/gather_keys_values/ppermute | solution.py:39
  25.3 4.4 %collective-permute-done.8.refs_1_ = bf16[256,256]{1,0:T(8,128)(2,1)S(1)} collective-permute-done((bf16[256,256]{1,0:T(8,128)(2,1)S(1)}, bf16[256,256]{1,0:T(8,128)(2,1)S(1)}, u32[]{:S(2)}, u32[]{:S(2)}) %collective-permute-start.8) | collective-permute-done | bytes 131104 | tf_op jit(solution)/shard_map/gather_keys_values/ppermute | solution.py:39
  31.2 3.2 %collective-permute-start.11 = (bf16[768,256]{1,0:T(8,128)(2,1)S(1)}, bf16[768,256]{1,0:T(8,128)(2,1)S(1)}, u32[]{:S(2)}, u32[]{:S(2)}) collective-permute-start(bf16[768,256]{1,0:T(8,128)(2,1)S(1)} %gather_keys_values.3.refs_3_), channel_id=1, source_target_pairs={{192,0},{200,8},{208,16},{216,24},{224,32},{232,40},{240,48},{248,... | collective-permute-start | bytes 1179656 | tf_op jit(solution)/shard_map/gather_keys_values/ppermute | solution.py:39
  34.4 4.2 %collective-permute-done.4.refs_2_ = bf16[1280,256]{1,0:T(8,128)(2,1)S(1)} collective-permute-done((bf16[1280,256]{1,0:T(8,128)(2,1)S(1)}, bf16[1280,256]{1,0:T(8,128)(2,1)S(1)}, u32[]{:S(2)}, u32[]{:S(2)}) %collective-permute-start.4) | collective-permute-done | bytes 655392 | tf_op jit(solution)/shard_map/gather_keys_values/ppermute | solution.py:39
  38.8 6.3 %attend_own_row.1 = (f32[2,1024,256]{2,1,0:T(8,128)S(1)}, f32[2,1024,128]{2,1,0:T(8,128)S(1)}) custom-call(s32[4]{0:T(128)S(1)} %copy-done.1, bf16[256,1024]{1,0:T(8,128)(2,1)S(1)} %copy-done, bf16[1280,256]{1,0:T(8,128)(2,1)S(1)} %gather_keys_values.2.refs_2_, bf16[768,256]{1,0:T(8,128)(2,1)S(1)} %gather_keys_values.3.refs_3_), custom_call_target="tpu_custom_call" | custom-call | flops 1100000000 | bytes 6291456 | tf_op jit(solution)/shard_map/attend_own_row/pallas_call | solution.py:208
  45.1 1.9 %collective-permute-done.10.refs_3_ = bf16[768,256]{1,0:T(8,128)(2,1)S(1)} collective-permute-done((bf16[768,256]{1,0:T(8,128)(2,1)S(1)}, bf16[768,256]{1,0:T(8,128)(2,1)S(1)}, u32[]{:S(2)}, u32[]{:S(2)}) %collective-permute-start.10) | collective-permute-done | bytes 393248 | tf_op jit(solution)/shard_map/gather_keys_values/ppermute | solution.py:39
  47.0 1.3 %collective-permute-start.12 = (bf16[768,256]{1,0:T(8,128)(2,1)S(1)}, bf16[768,256]{1,0:T(8,128)(2,1)S(1)}, u32[]{:S(2)}, u32[]{:S(2)}) collective-permute-start(bf16[768,256]{1,0:T(8,128)(2,1)S(1)} %collective-permute-done.11.refs_5_), channel_id=1, source_target_pairs={{192,0},{200,8},{208,16},{216,24},{224,32},{232,40},{240,48},{248,... | collective-permute-start | bytes 1179656 | tf_op jit(solution)/shard_map/gather_keys_values/ppermute | solution.py:39
  48.3 8.2 %attend_next_rows.1 = (f32[2,1024,256]{2,1,0:T(8,128)S(1)}, f32[2,1024,128]{2,1,0:T(8,128)S(1)}) custom-call(s32[4]{0:T(128)S(1)} %copy-done.1, bf16[256,1024]{1,0:T(8,128)(2,1)S(1)} %copy-done, bf16[1280,256]{1,0:T(8,128)(2,1)S(1)} %collective-permute-done.4.refs_2_, bf16[768,256]{1,0:T(8,128)(2,1)S(1)} %collective-permute-done.10.refs_3_, ...), custom_call_target="tpu_custom_call" | custom-call | flops 2200000000 | bytes 6291456 | tf_op jit(solution)/shard_map/attend_next_rows/pallas_call | solution.py:208
  56.6 2.8 %collective-permute-done.6.refs_3_ = bf16[1280,256]{1,0:T(8,128)(2,1)S(1)} collective-permute-done((bf16[1280,256]{1,0:T(8,128)(2,1)S(1)}, bf16[1280,256]{1,0:T(8,128)(2,1)S(1)}, u32[]{:S(2)}, u32[]{:S(2)}) %collective-permute-start.6) | collective-permute-done | bytes 655392 | tf_op jit(solution)/shard_map/gather_keys_values/ppermute | solution.py:39
  59.4 4.9 %attend_far_row_and_project.1 = (bf16[256,1024]{1,0:T(8,128)(2,1)S(1)}, bf16[256,512]{1,0:T(8,128)(2,1)S(1)}, bf16[256,512]{1,0:T(8,128)(2,1)S(1)}) custom-call(s32[4]{0:T(128)S(1)} %copy-done.1, bf16[256,1024]{1,0:T(8,128)(2,1)S(1)} %copy-done, bf16[1024,4096]{1,0:T(8,128)(2,1)S(1)} %bitcast.9, bf16[1280,256]{1,0:T(8,128)(2,1)S(1)} %collective-permute-done.6.refs_3_, ...), custom_call_target="tpu_custom_call" | custom-call | flops 1640000000 | bytes 6291456 | tf_op jit(solution)/shard_map/attend_far_row_and_project/pallas_call | solution.py:208
  64.4 1.0 %sum_over_heads.2 = bf16[3,256,512]{2,1,0:T(8,128)(2,1)S(1)} custom-call(bf16[256,1024]{1,0:T(8,128)(2,1)S(1)} %get-tuple-element.32.att, bf16[1024,4096]{1,0:T(8,128)(2,1)S(1)} %bitcast.9), custom_call_target="tpu_custom_call" | custom-call | flops 810000000 | bytes 1048576 | tf_op jit(solution)/shard_map/sum_over_heads/pallas_call | solution.py:181
  66.2 1.0 %sum_over_heads.3 = bf16[3,256,512]{2,1,0:T(8,128)(2,1)S(1)} custom-call(bf16[256,1024]{1,0:T(8,128)(2,1)S(1)} %get-tuple-element.32.att, bf16[1024,4096]{1,0:T(8,128)(2,1)S(1)} %bitcast.9), custom_call_target="tpu_custom_call" | custom-call | flops 810000000 | bytes 1048576 | tf_op jit(solution)/shard_map/sum_over_heads/pallas_call | solution.py:181
  67.2 3.3 %collective-permute-start.14 = (bf16[256,512]{1,0:T(8,128)(2,1)S(1)}, bf16[256,512]{1,0:T(8,128)(2,1)S(1)}, u32[]{:S(2)}, u32[]{:S(2)}) collective-permute-start(bf16[256,512]{1,0:T(8,128)(2,1)S(1)} %add_convert_fusion.2), channel_id=1, source_target_pairs={{4,0},{5,1},{6,2},{7,3},{0,4},{1,5},{2,6},{3,7},{12,8},{13,9},{14,... | collective-permute-start | bytes 786440 | tf_op jit(solution)/shard_map/sum_over_heads/ppermute | solution.py:260
  71.4 2.6 %collective-permute-start.17 = (bf16[256,512]{1,0:T(8,128)(2,1)S(1)}, bf16[256,512]{1,0:T(8,128)(2,1)S(1)}, u32[]{:S(2)}, u32[]{:S(2)}) collective-permute-start(bf16[256,512]{1,0:T(8,128)(2,1)S(1)} %get-tuple-element.36), channel_id=1, source_target_pairs={{2,0},{3,1},{4,2},{5,3},{6,4},{7,5},{0,6},{1,7},{10,8},{11,9},{12,... | collective-permute-start | bytes 786440 | tf_op jit(solution)/shard_map/sum_over_heads/ppermute | solution.py:263
  74.0 4.0 %collective-permute-done.14 = bf16[256,512]{1,0:T(8,128)(2,1)S(1)} collective-permute-done((bf16[256,512]{1,0:T(8,128)(2,1)S(1)}, bf16[256,512]{1,0:T(8,128)(2,1)S(1)}, u32[]{:S(2)}, u32[]{:S(2)}) %collective-permute-start.14) | collective-permute-done | bytes 262176 | tf_op jit(solution)/shard_map/sum_over_heads/ppermute | solution.py:260
  78.0 4.9 %collective-permute-done.16 = bf16[256,512]{1,0:T(8,128)(2,1)S(1)} collective-permute-done((bf16[256,512]{1,0:T(8,128)(2,1)S(1)}, bf16[256,512]{1,0:T(8,128)(2,1)S(1)}, u32[]{:S(2)}, u32[]{:S(2)}) %collective-permute-start.16) | collective-permute-done | bytes 262176 | tf_op jit(solution)/shard_map/sum_over_heads/ppermute | solution.py:263
  (34 shorter events, 5.5 us)
Async XLA Ops:
  0.0 38.7 %copy-start = (bf16[256,1024]{1,0:T(8,128)(2,1)S(1)}, bf16[256,1024]{1,0:T(8,128)(2,1)}, u32[]{:S(2)}) copy-start(bf16[256,1024]{1,0:T(8,128)(2,1)} %refs_1_.5) | copy-start | bytes 1572868
  0.0 38.7 %copy-start.1 = (s32[4]{0:T(128)S(1)}, s32[4]{0:T(128)}, u32[]{:S(2)}) copy-start(s32[4]{0:T(128)} %refs_0_.5) | copy-start | bytes 52
  1.0 12.5 %collective-permute-start.2 = (bf16[256,256]{1,0:T(8,128)(2,1)S(1)}, bf16[256,256]{1,0:T(8,128)(2,1)S(1)}, u32[]{:S(2)}, u32[]{:S(2)}) collective-permute-start(bf16[256,256]{1,0:T(8,128)(2,1)S(1)} %pad_select_fusion.refs_0_), channel_id=1, source_target_pairs={{16,0},{24,8},{32,16},{40,24},{48,32},{56,40},{0,48},{8,56},{80,64... | collective-permute-start | bytes 393224 | tf_op jit(solution)/shard_map/gather_keys_values/ppermute | solution.py:39
  7.3 10.4 %collective-permute-start.3 = (bf16[256,256]{1,0:T(8,128)(2,1)S(1)}, bf16[256,256]{1,0:T(8,128)(2,1)S(1)}, u32[]{:S(2)}, u32[]{:S(2)}) collective-permute-start(bf16[256,256]{1,0:T(8,128)(2,1)S(1)} %pad_select_fusion.refs_0_), channel_id=1, source_target_pairs={{48,0},{56,8},{0,16},{8,24},{16,32},{24,40},{32,48},{40,56},{112,6... | collective-permute-start | bytes 393224 | tf_op jit(solution)/shard_map/gather_keys_values/ppermute | solution.py:39
  7.4 10.4 %collective-permute-start = (bf16[256,256]{1,0:T(8,128)(2,1)S(1)}, bf16[256,256]{1,0:T(8,128)(2,1)S(1)}, u32[]{:S(2)}, u32[]{:S(2)}) collective-permute-start(bf16[256,256]{1,0:T(8,128)(2,1)S(1)} %pad_select_fusion.refs_0_), channel_id=1, source_target_pairs={{8,0},{16,8},{24,16},{32,24},{40,32},{48,40},{56,48},{0,56},{72,64... | collective-permute-start | bytes 393224 | tf_op jit(solution)/shard_map/gather_keys_values/ppermute | solution.py:39
  11.0 8.5 %collective-permute-start.1 = (bf16[256,256]{1,0:T(8,128)(2,1)S(1)}, bf16[256,256]{1,0:T(8,128)(2,1)S(1)}, u32[]{:S(2)}, u32[]{:S(2)}) collective-permute-start(bf16[256,256]{1,0:T(8,128)(2,1)S(1)} %pad_select_fusion.refs_0_), channel_id=1, source_target_pairs={{56,0},{0,8},{8,16},{16,24},{24,32},{32,40},{40,48},{48,56},{120,6... | collective-permute-start | bytes 393224 | tf_op jit(solution)/shard_map/gather_keys_values/ppermute | solution.py:39
  19.6 19.0 %collective-permute-start.4 = (bf16[1280,256]{1,0:T(8,128)(2,1)S(1)}, bf16[1280,256]{1,0:T(8,128)(2,1)S(1)}, u32[]{:S(2)}, u32[]{:S(2)}) collective-permute-start(bf16[1280,256]{1,0:T(8,128)(2,1)S(1)} %gather_keys_values.2.refs_2_), channel_id=1, source_target_pairs={{64,0},{72,8},{80,16},{88,24},{96,32},{104,40},{112,48},{120,56},{... | collective-permute-start | bytes 1966088 | tf_op jit(solution)/shard_map/gather_keys_values/ppermute | solution.py:39
  20.5 18.1 %collective-permute-start.5 = (bf16[1280,256]{1,0:T(8,128)(2,1)S(1)}, bf16[1280,256]{1,0:T(8,128)(2,1)S(1)}, u32[]{:S(2)}, u32[]{:S(2)}) collective-permute-start(bf16[1280,256]{1,0:T(8,128)(2,1)S(1)} %gather_keys_values.2.refs_2_), channel_id=1, source_target_pairs={{192,0},{200,8},{208,16},{216,24},{224,32},{232,40},{240,48},{248,... | collective-permute-start | bytes 1966088 | tf_op jit(solution)/shard_map/gather_keys_values/ppermute | solution.py:39
  23.0 6.8 %collective-permute-start.8 = (bf16[256,256]{1,0:T(8,128)(2,1)S(1)}, bf16[256,256]{1,0:T(8,128)(2,1)S(1)}, u32[]{:S(2)}, u32[]{:S(2)}) collective-permute-start(bf16[256,256]{1,0:T(8,128)(2,1)S(1)} %broadcast_select_fusion), channel_id=1, source_target_pairs={{16,0},{56,8},{32,16},{8,24},{48,32},{24,40},{0,48},{40,56},{80,64... | collective-permute-start | bytes 393224 | tf_op jit(solution)/shard_map/gather_keys_values/ppermute | solution.py:39
  23.3 6.9 %collective-permute-start.7 = (bf16[256,256]{1,0:T(8,128)(2,1)S(1)}, bf16[256,256]{1,0:T(8,128)(2,1)S(1)}, u32[]{:S(2)}, u32[]{:S(2)}) collective-permute-start(bf16[256,256]{1,0:T(8,128)(2,1)S(1)} %collective-permute-done.2.refs_3_), channel_id=1, source_target_pairs={{8,0},{16,8},{24,16},{32,24},{40,32},{48,40},{56,48},{0,56},{72,64... | collective-permute-start | bytes 393224 | tf_op jit(solution)/shard_map/gather_keys_values/ppermute | solution.py:39
  24.9 6.2 %collective-permute-start.9 = (bf16[256,256]{1,0:T(8,128)(2,1)S(1)}, bf16[256,256]{1,0:T(8,128)(2,1)S(1)}, u32[]{:S(2)}, u32[]{:S(2)}) collective-permute-start(bf16[256,256]{1,0:T(8,128)(2,1)S(1)} %collective-permute-done.3.refs_4_), channel_id=1, source_target_pairs={{56,0},{0,8},{8,16},{16,24},{24,32},{32,40},{40,48},{48,56},{120,6... | collective-permute-start | bytes 393224 | tf_op jit(solution)/shard_map/gather_keys_values/ppermute | solution.py:39
  31.1 16.0 %collective-permute-start.10 = (bf16[768,256]{1,0:T(8,128)(2,1)S(1)}, bf16[768,256]{1,0:T(8,128)(2,1)S(1)}, u32[]{:S(2)}, u32[]{:S(2)}) collective-permute-start(bf16[768,256]{1,0:T(8,128)(2,1)S(1)} %gather_keys_values.3.refs_3_), channel_id=1, source_target_pairs={{64,0},{72,8},{80,16},{88,24},{96,32},{104,40},{112,48},{120,56},{... | collective-permute-start | bytes 1179656 | tf_op jit(solution)/shard_map/gather_keys_values/ppermute | solution.py:39
  31.2 15.9 %collective-permute-start.11 = (bf16[768,256]{1,0:T(8,128)(2,1)S(1)}, bf16[768,256]{1,0:T(8,128)(2,1)S(1)}, u32[]{:S(2)}, u32[]{:S(2)}) collective-permute-start(bf16[768,256]{1,0:T(8,128)(2,1)S(1)} %gather_keys_values.3.refs_3_), channel_id=1, source_target_pairs={{192,0},{200,8},{208,16},{216,24},{224,32},{232,40},{240,48},{248,... | collective-permute-start | bytes 1179656 | tf_op jit(solution)/shard_map/gather_keys_values/ppermute | solution.py:39
  38.6 20.8 %collective-permute-start.6 = (bf16[1280,256]{1,0:T(8,128)(2,1)S(1)}, bf16[1280,256]{1,0:T(8,128)(2,1)S(1)}, u32[]{:S(2)}, u32[]{:S(2)}) collective-permute-start(bf16[1280,256]{1,0:T(8,128)(2,1)S(1)} %collective-permute-done.4.refs_2_), channel_id=1, source_target_pairs={{64,0},{72,8},{80,16},{88,24},{96,32},{104,40},{112,48},{120,56},{... | collective-permute-start | bytes 1966088 | tf_op jit(solution)/shard_map/gather_keys_values/ppermute | solution.py:39
  38.8 20.7 %slice-start = ((s8[8388608]{0:T(1024)(128)(4,1)}), s8[4194304]{0:T(1024)(128)(4,1)S(1)}, s32[]{:S(2)}) async-start(s8[8388608]{0:T(1024)(128)(4,1)} %bitcast.8), calls=%async_computation | async-start | bytes 8388608
  47.0 12.4 %slice-start.1 = ((s8[8388608]{0:T(1024)(128)(4,1)}), s8[4194304]{0:T(1024)(128)(4,1)S(1)}, s32[]{:S(2)}) async-start(s8[8388608]{0:T(1024)(128)(4,1)} %bitcast.8), calls=%async_computation.1 | async-start | bytes 8388608
  47.0 9.5 %collective-permute-start.12 = (bf16[768,256]{1,0:T(8,128)(2,1)S(1)}, bf16[768,256]{1,0:T(8,128)(2,1)S(1)}, u32[]{:S(2)}, u32[]{:S(2)}) collective-permute-start(bf16[768,256]{1,0:T(8,128)(2,1)S(1)} %collective-permute-done.11.refs_5_), channel_id=1, source_target_pairs={{192,0},{200,8},{208,16},{216,24},{224,32},{232,40},{240,48},{248,... | collective-permute-start | bytes 1179656 | tf_op jit(solution)/shard_map/gather_keys_values/ppermute | solution.py:39
  64.3 1.6 %collective-permute-start.13 = (bf16[256,512]{1,0:T(8,128)(2,1)S(1)}, bf16[256,512]{1,0:T(8,128)(2,1)S(1)}, u32[]{:S(2)}, u32[]{:S(2)}) collective-permute-start(bf16[256,512]{1,0:T(8,128)(2,1)S(1)} %get-tuple-element.31), channel_id=1, source_target_pairs={{0,1},{1,0},{2,3},{3,2},{4,5},{5,4},{6,7},{7,6},{8,9},{9,8},{10,11... | collective-permute-start | bytes 786440 | tf_op jit(solution)/shard_map/sum_over_heads/ppermute | solution.py:256
  65.9 4.6 %collective-permute-start.15 = (bf16[3,256,512]{2,1,0:T(8,128)(2,1)S(1)}, bf16[3,256,512]{2,1,0:T(8,128)(2,1)S(1)}, u32[]{:S(2)}, u32[]{:S(2)}) collective-permute-start(bf16[3,256,512]{2,1,0:T(8,128)(2,1)S(1)} %sum_over_heads.2), channel_id=1, source_target_pairs={{0,1},{1,0},{2,3},{3,2},{4,5},{5,4},{6,7},{7,6},{8,9},{9,8},{10,11... | collective-permute-start | bytes 2359304 | tf_op jit(solution)/shard_map/sum_over_heads/ppermute | solution.py:259
  67.2 10.8 %collective-permute-start.14 = (bf16[256,512]{1,0:T(8,128)(2,1)S(1)}, bf16[256,512]{1,0:T(8,128)(2,1)S(1)}, u32[]{:S(2)}, u32[]{:S(2)}) collective-permute-start(bf16[256,512]{1,0:T(8,128)(2,1)S(1)} %add_convert_fusion.2), channel_id=1, source_target_pairs={{4,0},{5,1},{6,2},{7,3},{0,4},{1,5},{2,6},{3,7},{12,8},{13,9},{14,... | collective-permute-start | bytes 786440 | tf_op jit(solution)/shard_map/sum_over_heads/ppermute | solution.py:260
  70.7 12.2 %collective-permute-start.16 = (bf16[256,512]{1,0:T(8,128)(2,1)S(1)}, bf16[256,512]{1,0:T(8,128)(2,1)S(1)}, u32[]{:S(2)}, u32[]{:S(2)}) collective-permute-start(bf16[256,512]{1,0:T(8,128)(2,1)S(1)} %get-tuple-element.35), channel_id=1, source_target_pairs={{6,0},{7,1},{0,2},{1,3},{2,4},{3,5},{4,6},{5,7},{14,8},{15,9},{8,1... | collective-permute-start | bytes 786440 | tf_op jit(solution)/shard_map/sum_over_heads/ppermute | solution.py:263
  71.4 11.9 %collective-permute-start.17 = (bf16[256,512]{1,0:T(8,128)(2,1)S(1)}, bf16[256,512]{1,0:T(8,128)(2,1)S(1)}, u32[]{:S(2)}, u32[]{:S(2)}) collective-permute-start(bf16[256,512]{1,0:T(8,128)(2,1)S(1)} %get-tuple-element.36), channel_id=1, source_target_pairs={{2,0},{3,1},{4,2},{5,3},{6,4},{7,5},{0,6},{1,7},{10,8},{11,9},{12,... | collective-permute-start | bytes 786440 | tf_op jit(solution)/shard_map/sum_over_heads/ppermute | solution.py:263

commit v5 on v4

--- a/solution.py
+++ b/solution.py
@@ -14,7 +14,7 @@
 BLOCKS = 2 * NX * NZ
 NEG = -1e30
 SCALE2 = (HD ** -0.5) * 1.4426950408889634
-FIRST_Z, LATER_Z = (0, 1, 7, 2, 6), (3, 4, 5)
+OWN_Z, EARLY_Z, LATER_Z = (0,), (1, 7, 2, 6), (3, 4, 5)
 VMEM = pl.BlockSpec(memory_space=pltpu.VMEM)
 ANY = pl.BlockSpec(memory_space=pl.ANY)
 
@@ -57,12 +57,12 @@
     )(*parts)
 
 
-def attend(rows, first, last, *refs):
+def attend(jobs, first, last, *refs):
     refs = list(refs)
     take = lambda n: [refs.pop(0) for _ in range(n)]
-    len_hbm, q = take(2)
+    ends_hbm, q = take(2)
     w = take(1)[0] if last else None
-    pieces = take(2 * len(rows))
+    held = [(kx, [(take(1)[0], offsets) for offsets in pieces]) for kx, pieces in jobs]
     state = [] if first else take(2)
     att, mine_ref, other_ref = take(3) if last else (None, None, None)
     acc, top, lens, len_sem = take(4)
@@ -70,7 +70,7 @@
     mx, mz = me // NZ, me % NZ
     span = NZ * HALF
 
-    len_copy = pltpu.make_async_copy(len_hbm, lens, len_sem)
+    len_copy = pltpu.make_async_copy(ends_hbm, lens, len_sem)
     len_copy.start()
     if first:
         acc[...] = jnp.zeros_like(acc)
@@ -79,11 +79,7 @@
         acc[...] = state[0][...]
         top[...] = state[1][...]
     len_copy.wait()
-    ends = []
-    total = 0
-    for i in range(4):
-        total = total + lens[i]
-        ends.append(total)
+    ends = [lens[i] for i in range(lens.shape[0])]
 
     def begins(p):
         start = jnp.zeros_like(p)
@@ -91,9 +87,8 @@
             start = jnp.maximum(start, jnp.where(p >= e, e, 0))
         return start
 
-    ones = jnp.ones((span, HD), jnp.bfloat16)
-
     def step(blocks, h, q0, late, k0, masked):
+        n = len(blocks)
         k, v, kp = [], [], []
         for ref, i, kz in blocks:
             at = pl.ds(pl.multiple_of((2 * i + late) * HALF, HALF), HALF)
@@ -104,12 +99,13 @@
                 base = k0 + jnp.where(late == 0, z, NZ - 1 - z) * HALF
                 kp.append(base + lax.broadcasted_iota(jnp.int32, (HALF, HALF), 1))
         k = jnp.concatenate(k, axis=0)
+        ones = jnp.ones((n * HALF, HD), jnp.bfloat16)
         v = jnp.concatenate([jnp.concatenate(v, axis=0), ones], axis=1)
         if masked:
             kp = jnp.concatenate(kp, axis=1)
             qp = q0 + lax.broadcasted_iota(jnp.int32, (HALF, HD), 0)
-            begin = jnp.tile(begins(qp), (1, NZ))
-            ok = (kp <= jnp.tile(qp, (1, NZ))) & (kp >= begin)
+            begin = jnp.tile(begins(qp), (1, n))
+            ok = (kp <= jnp.tile(qp, (1, n))) & (kp >= begin)
         q_rows = pl.ds(pl.multiple_of(h * HALF, HALF), HALF)
         for g in range(GROUP):
             at = slice(g * HALF, (g + 1) * HALF)
@@ -123,19 +119,15 @@
                 s = jnp.where(ok, s, NEG)
             old = top[h, at, :]
             new = jnp.maximum(old, jnp.max(s, axis=1, keepdims=True))
-            p = jnp.exp2((s - jnp.tile(new, (1, NZ))) * SCALE2)
+            p = jnp.exp2((s - jnp.tile(new, (1, n))) * SCALE2)
             o = jnp.dot(p.astype(jnp.bfloat16), v, preferred_element_type=jnp.float32)
             alpha = jnp.exp2((old - new) * SCALE2)
             acc[h, at, :] = acc[h, at, :] * jnp.tile(alpha, (1, 2)) + o
             top[h, at, :] = new
 
-    for r, kx in enumerate(rows):
+    for kx, pieces in held:
         x = (mx + kx) % NX
-        blocks = [
-            (ref, i, kz)
-            for ref, offsets in zip(pieces[2 * r : 2 * r + 2], (FIRST_Z, LATER_Z))
-            for i, kz in enumerate(offsets)
-        ]
+        blocks = [(ref, i, kz) for ref, offsets in pieces for i, kz in enumerate(offsets)]
 
         def one(n, carry, x=x, blocks=blocks):
             h, late = jnp.where(n == 0, 0, 1), jnp.where(n == 2, 1, 0)
@@ -190,15 +182,18 @@
     )(att, out_weight)
 
 
-def attend_to(rows, lengths, queries, pieces, state=None, out_weight=None):
+def attend_to(jobs, ends, queries, state=None, out_weight=None):
     first, last = state is None, out_weight is not None
     tokens = queries.shape[0]
     state_shape = [(2, GROUP * HALF, 2 * HD), (2, GROUP * HALF, HD)]
     outs = [jax.ShapeDtypeStruct(s, jnp.float32) for s in state_shape]
-    operands = [lengths, queries] + ([out_weight] if last else []) + pieces
+    operands = [ends, queries] + ([out_weight] if last else [])
+    operands += [p for _, pieces in jobs for p, _ in pieces]
     operands += [] if first else list(state)
-    scratch = [pltpu.SMEM(lengths.shape, jnp.int32), pltpu.SemaphoreType.DMA]
-    flops = 1_100_000_000 * len(rows)
+    scratch = [pltpu.SMEM(ends.shape, jnp.int32), pltpu.SemaphoreType.DMA]
+    jobs = tuple((kx, tuple(offsets for _, offsets in pieces)) for kx, pieces in jobs)
+    blocks = sum(len(offsets) for _, pieces in jobs for offsets in pieces)
+    flops = 140_000_000 * blocks
     if last:
         width = out_weight.shape[1] // (2 * NY)
         scratch = [pltpu.VMEM(s, jnp.float32) for s in state_shape] + scratch
@@ -206,14 +201,14 @@
         outs += [jax.ShapeDtypeStruct((tokens, width), jnp.bfloat16)] * 2
         flops += 540_000_000
     return pl.pallas_call(
-        functools.partial(attend, rows, first, last),
+        functools.partial(attend, jobs, first, last),
         out_shape=outs,
         in_specs=[ANY] + [VMEM] * (len(operands) - 1),
         out_specs=[VMEM] * len(outs),
         scratch_shapes=scratch,
         compiler_params=pltpu.CompilerParams(vmem_limit_bytes=(22 if last else 14) * 2**20),
         cost_estimate=pl.CostEstimate(
-            flops=flops, bytes_accessed=6 * 2**20, transcendentals=3_000_000 * len(rows)
+            flops=flops, bytes_accessed=6 * 2**20, transcendentals=400_000 * blocks
         ),
     )(*operands)
 
@@ -229,36 +224,55 @@
         )
         up2, down2 = ctx(kv, from_z(2)), ctx(kv, from_z(-2))
         up1, down1 = ctx(kv, from_z(1)), ctx(kv, from_z(-1))
-        early = together([kv, up1, down1, up2, down2])
+        right_0, left_0 = ctx(kv, from_x(1)), ctx(kv, from_x(-1))
+        early = together([up1, down1, up2, down2])
+        before = jnp.tril(jnp.ones((lengths.shape[0],) * 2, bool))
+        ends = jnp.sum(jnp.where(before, lengths[None, :], 0), axis=1)
+        q = jnp.where(lax.axis_index("ctx") >= 0, queries, 0)
+        early, right_0, left_0, q, ends = lax.optimization_barrier(
+            (early, right_0, left_0, q, ends)
+        )
         right_a, left_a = ctx(early, from_x(1)), ctx(early, from_x(-1))
         up3, down3 = ctx(up2, from_z(1)), ctx(down2, from_z(-1))
         even = lax.axis_index("ctx") % 2 == 0
         over = ctx(jnp.where(even, up2, down2), OVER)
         later = together([up3, over, down3])
+    with jax.named_scope("attend_own_row_early"):
+        jobs = [(0, [(kv, OWN_Z), (early, EARLY_Z)])]
+        state = attend_to(jobs, ends, q)
+    with jax.named_scope("gather_keys_values"):
+        later, state = lax.optimization_barrier((later, state))
         right_b, left_b = ctx(later, from_x(1)), ctx(later, from_x(-1))
-    with jax.named_scope("attend_own_row"):
-        state = attend_to((0,), lengths, queries, [early, later])
-    with jax.named_scope("gather_keys_values"):
         right_a, left_a = lax.optimization_barrier((right_a, left_a))
         far_a = ctx(right_a, from_x(1))
-        right_b, left_b, state = lax.optimization_barrier((right_b, left_b, state))
+        far_0 = ctx(left_0, from_x(-1))
+    with jax.named_scope("attend_right_row_early"):
+        jobs = [(0, [(later, LATER_Z)]), (1, [(right_0, OWN_Z), (right_a, EARLY_Z)])]
+        state = attend_to(jobs, ends, q, state)
+    with jax.named_scope("gather_keys_values"):
+        right_b, left_b, state, far_0 = lax.optimization_barrier((right_b, left_b, state, far_0))
         far_b = ctx(left_b, from_x(-1))
-    with jax.named_scope("attend_next_rows"):
-        state = attend_to((1, 3), lengths, queries, [right_a, right_b, left_a, left_b], state)
+    with jax.named_scope("attend_left_row"):
+        jobs = [
+            (3, [(left_0, OWN_Z), (left_a, EARLY_Z), (left_b, LATER_Z)]),
+            (1, [(right_b, LATER_Z)]),
+        ]
+        state = attend_to(jobs, ends, q, state)
     with jax.named_scope("attend_far_row_and_project"):
-        att, mine_2, other_2 = attend_to((2,), lengths, queries, [far_a, far_b], state, out_weight)
+        jobs = [(2, [(far_0, OWN_Z), (far_a, EARLY_Z), (far_b, LATER_Z)])]
+        att, mine_2, other_2 = attend_to(jobs, ends, q, state, out_weight)
     with jax.named_scope("sum_over_heads"):
 
         def pair(a, b):
             return (a.astype(jnp.float32) + b.astype(jnp.float32)).astype(jnp.bfloat16)
 
-        near = (0, 1, 3)
+        rest = (0, 1, 3)
         theirs_2 = lax.ppermute(other_2, "tp", CORES)
-        other = project_to(near, False, att, out_weight)
+        other = project_to(rest, False, att, out_weight)
         theirs_2, other = lax.optimization_barrier((theirs_2, other))
         theirs = lax.ppermute(other, "tp", CORES)
         total = lax.ppermute(pair(mine_2, theirs_2), "tp", from_y(2)).astype(jnp.float32)
-        mine = project_to(near, True, att, out_weight)
+        mine = project_to(rest, True, att, out_weight)
         for i, k in ((1, 1), (2, 3)):
             total += lax.ppermute(pair(mine[i], theirs[i]), "tp", from_y(-k)).astype(jnp.float32)
         total += mine[0].astype(jnp.float32) + theirs[0].astype(jnp.float32)

time: 84.1 us -> 80.7 us (0.960)
  waiting for transfers between devices: 33.1 us -> 23.3 us
  starting transfers between devices: 27.5 us -> 32.5 us
  other arithmetic: 2.05 us -> 3.84 us
    ppermute x13 -> x16, waiting for transfers between devices: 23.3 us -> 13.3 us  [ctx(): return lax.ppermute(a, 'ctx', perm)]
    ppermute x13 -> x16, starting transfers between devices: 20.5 us -> 25.6 us  [ctx(): return lax.ppermute(a, 'ctx', perm)]
    select_n x0 -> x1, other arithmetic: none -> 1.08 us  [on_device(): q = jnp.where(lax.axis_index('ctx') >= 0, queries, 0)]
    pallas_call x3 -> x4, Pallas kernels: 19.4 us -> 18.7 us  [attend_to(): pl.pallas_call(functools.partial(attend, jobs, first, last), out_shape=ou...]
  transfers between devices with their start and end apart: 18 -> 21, of which waited for: 13 -> 10; matrix products, arithmetic and copies ran while one was open for 0% -> 3% of each run, Pallas kernels for 20% -> 19%
where the time goes in v5:
time: 80.7 us; the launch traced here: 80.5 us
  starting transfers between devices  32.5 us (40%)
  waiting for transfers between devices  23.3 us (29%)
  Pallas kernels  20.8 us (26%)
  other arithmetic  3.84 us (5%)
    ppermute x16, starting transfers between devices, ctx(): return lax.ppermute(a, 'ctx', perm)  25.6 us
    pallas_call x4, Pallas kernels, attend_to(): pl.pallas_call(functools.partial(attend, jobs, first, last), out_shape=ou...  18.7 us
    ppermute x16, waiting for transfers between devices, ctx(): return lax.ppermute(a, 'ctx', perm)  13.3 us
    ppermute x2, waiting for transfers between devices, on_device(): lax.ppermute(pair(mine[i], theirs[i]), 'tp', from_y(-k)).astype(jnp.float32)  5.41 us
    ppermute x1, waiting for transfers between devices, on_device(): lax.ppermute(pair(mine_2, theirs_2), 'tp', from_y(2)).astype(jnp.float32)  4.01 us
    ppermute x1, starting transfers between devices, on_device(): lax.ppermute(pair(mine_2, theirs_2), 'tp', from_y(2)).astype(jnp.float32)  3.32 us
    ppermute x2, starting transfers between devices, on_device(): lax.ppermute(pair(mine[i], theirs[i]), 'tp', from_y(-k)).astype(jnp.float32)  3.31 us
    pallas_call x2, Pallas kernels, project_to(): pl.pallas_call(functools.partial(project, ks, same), out_shape=jax.ShapeD...  1.99 us
  transfers between devices with their start and end apart: 21, of which 10 were waited for; matrix products, arithmetic and copies ran while one was open for 3% of the time, Pallas kernels for 19%

profile of v5, /device:TPU:6, one launch (start us, length us, event | category | flops | bytes accessed | tf_op | source)
XLA Modules:
  0.0 80.5 jit_solution(5241956286992322886)
XLA Ops:
  0.9 6.4 %collective-permute-start.2 = (bf16[256,256]{1,0:T(8,128)(2,1)S(1)}, bf16[256,256]{1,0:T(8,128)(2,1)S(1)}, u32[]{:S(2)}, u32[]{:S(2)}) collective-permute-start(bf16[256,256]{1,0:T(8,128)(2,1)S(1)} %pad_select_fusion.refs_2_), channel_id=1, source_target_pairs={{16,0},{24,8},{32,16},{40,24},{48,32},{56,40},{0,48},{8,56},{80,64... | collective-permute-start | bytes 393224 | tf_op jit(solution)/shard_map/gather_keys_values/ppermute | solution.py:39
  7.3 3.7 %collective-permute-start = (bf16[256,256]{1,0:T(8,128)(2,1)S(1)}, bf16[256,256]{1,0:T(8,128)(2,1)S(1)}, u32[]{:S(2)}, u32[]{:S(2)}) collective-permute-start(bf16[256,256]{1,0:T(8,128)(2,1)S(1)} %pad_select_fusion.refs_2_), channel_id=1, source_target_pairs={{8,0},{16,8},{24,16},{32,24},{40,32},{48,40},{56,48},{0,56},{72,64... | collective-permute-start | bytes 393224 | tf_op jit(solution)/shard_map/gather_keys_values/ppermute | solution.py:39
  11.8 1.6 %collective-permute-done.2.refs_2_ = bf16[256,256]{1,0:T(8,128)(2,1)S(1)} collective-permute-done((bf16[256,256]{1,0:T(8,128)(2,1)S(1)}, bf16[256,256]{1,0:T(8,128)(2,1)S(1)}, u32[]{:S(2)}, u32[]{:S(2)}) %collective-permute-start.2) | collective-permute-done | bytes 131104 | tf_op jit(solution)/shard_map/gather_keys_values/ppermute | solution.py:39
  14.2 1.1 %broadcast_select_fusion.refs_1_ = bf16[256,1024]{1,0:T(8,128)(2,1)S(1)} fusion(bf16[256,1024]{1,0:T(8,128)(2,1)} %param.5, pred[]{:T(512)S(6)} %ge.7), kind=kLoop, calls=%fused_computation.5 | loop fusion | flops 262144 | bytes 1048577 | tf_op jit(solution)/shard_map/gather_keys_values/jit(_where)/select_n | solution.py:231
  16.1 1.6 %collective-permute-done.3.refs_3_ = bf16[256,256]{1,0:T(8,128)(2,1)S(1)} collective-permute-done((bf16[256,256]{1,0:T(8,128)(2,1)S(1)}, bf16[256,256]{1,0:T(8,128)(2,1)S(1)}, u32[]{:S(2)}, u32[]{:S(2)}) %collective-permute-start.3) | collective-permute-done | bytes 131104 | tf_op jit(solution)/shard_map/gather_keys_values/ppermute | solution.py:39
  17.7 1.8 %collective-permute-done.1.refs_1_ = bf16[256,256]{1,0:T(8,128)(2,1)S(1)} collective-permute-done((bf16[256,256]{1,0:T(8,128)(2,1)S(1)}, bf16[256,256]{1,0:T(8,128)(2,1)S(1)}, u32[]{:S(2)}, u32[]{:S(2)}) %collective-permute-start.1) | collective-permute-done | bytes 131104 | tf_op jit(solution)/shard_map/gather_keys_values/ppermute | solution.py:39
  20.5 2.4 %collective-permute-start.12 = (bf16[1024,256]{1,0:T(8,128)(2,1)S(1)}, bf16[1024,256]{1,0:T(8,128)(2,1)S(1)}, u32[]{:S(2)}, u32[]{:S(2)}) collective-permute-start(bf16[1024,256]{1,0:T(8,128)(2,1)S(1)} %gather_keys_values.2.refs_3_), channel_id=1, source_target_pairs={{192,0},{200,8},{208,16},{216,24},{224,32},{232,40},{240,48},{248,... | collective-permute-start | bytes 1572872 | tf_op jit(solution)/shard_map/gather_keys_values/ppermute | solution.py:39
  22.9 3.6 %collective-permute-start.7 = (bf16[256,256]{1,0:T(8,128)(2,1)S(1)}, bf16[256,256]{1,0:T(8,128)(2,1)S(1)}, u32[]{:S(2)}, u32[]{:S(2)}) collective-permute-start(bf16[256,256]{1,0:T(8,128)(2,1)S(1)} %broadcast_select_fusion.1), channel_id=1, source_target_pairs={{16,0},{56,8},{32,16},{8,24},{48,32},{24,40},{0,48},{40,56},{80,64... | collective-permute-start | bytes 393224 | tf_op jit(solution)/shard_map/gather_keys_values/ppermute | solution.py:39
  26.5 2.0 %collective-permute-start.8 = (bf16[256,256]{1,0:T(8,128)(2,1)S(1)}, bf16[256,256]{1,0:T(8,128)(2,1)S(1)}, u32[]{:S(2)}, u32[]{:S(2)}) collective-permute-start(bf16[256,256]{1,0:T(8,128)(2,1)S(1)} %collective-permute-done.3.refs_3_), channel_id=1, source_target_pairs={{56,0},{0,8},{8,16},{16,24},{24,32},{32,40},{40,48},{48,56},{120,6... | collective-permute-start | bytes 393224 | tf_op jit(solution)/shard_map/gather_keys_values/ppermute | solution.py:39
  28.5 5.3 %attend_own_row_early.1 = (f32[2,1024,256]{2,1,0:T(8,128)S(1)}, f32[2,1024,128]{2,1,0:T(8,128)S(1)}) custom-call(s32[4]{0:T(128)S(1)} %select_reduce_fusion.refs_0_, bf16[256,1024]{1,0:T(8,128)(2,1)S(1)} %broadcast_select_fusion.refs_1_, bf16[256,256]{1,0:T(8,128)(2,1)S(1)} %pad_select_fusion.refs_2_, bf16[1024,256]{1,0:T(8,128)(2,1)S(1)} %gather_keys_values.2.refs_3_), custom_call_target="tpu_custom_call" | custom-call | flops 700000000 | bytes 6291456 | tf_op jit(solution)/shard_map/attend_own_row_early/pallas_call | solution.py:203
  33.9 2.0 %collective-permute-start.9 = (bf16[768,256]{1,0:T(8,128)(2,1)S(1)}, bf16[768,256]{1,0:T(8,128)(2,1)S(1)}, u32[]{:S(2)}, u32[]{:S(2)}) collective-permute-start(bf16[768,256]{1,0:T(8,128)(2,1)S(1)} %gather_keys_values.3.refs_2_), channel_id=1, source_target_pairs={{64,0},{72,8},{80,16},{88,24},{96,32},{104,40},{112,48},{120,56},{... | collective-permute-start | bytes 1179656 | tf_op jit(solution)/shard_map/gather_keys_values/ppermute | solution.py:39
  35.9 1.5 %collective-permute-start.13 = (bf16[256,256]{1,0:T(8,128)(2,1)S(1)}, bf16[256,256]{1,0:T(8,128)(2,1)S(1)}, u32[]{:S(2)}, u32[]{:S(2)}) collective-permute-start(bf16[256,256]{1,0:T(8,128)(2,1)S(1)} %collective-permute-done.5.refs_2_), channel_id=1, source_target_pairs={{192,0},{200,8},{208,16},{216,24},{224,32},{232,40},{240,48},{248,... | collective-permute-start | bytes 393224 | tf_op jit(solution)/shard_map/gather_keys_values/ppermute | solution.py:39
  38.0 3.9 %attend_right_row_early.1 = (f32[2,1024,256]{2,1,0:T(8,128)S(1)}, f32[2,1024,128]{2,1,0:T(8,128)S(1)}) custom-call(s32[4]{0:T(128)S(1)} %select_reduce_fusion.refs_0_, bf16[256,1024]{1,0:T(8,128)(2,1)S(1)} %broadcast_select_fusion.refs_1_, bf16[768,256]{1,0:T(8,128)(2,1)S(1)} %gather_keys_values.3.refs_2_, ...), custom_call_target="tpu_custom_call" | custom-call | flops 1120000000 | bytes 6291456 | tf_op jit(solution)/shard_map/attend_right_row_early/pallas_call | solution.py:203
  41.8 2.8 %collective-permute-done.13.refs_3_ = bf16[256,256]{1,0:T(8,128)(2,1)S(1)} collective-permute-done((bf16[256,256]{1,0:T(8,128)(2,1)S(1)}, bf16[256,256]{1,0:T(8,128)(2,1)S(1)}, u32[]{:S(2)}, u32[]{:S(2)}) %collective-permute-start.13) | collective-permute-done | bytes 131104 | tf_op jit(solution)/shard_map/gather_keys_values/ppermute | solution.py:39
  44.7 2.8 %collective-permute-done.9.refs_5_ = bf16[768,256]{1,0:T(8,128)(2,1)S(1)} collective-permute-done((bf16[768,256]{1,0:T(8,128)(2,1)S(1)}, bf16[768,256]{1,0:T(8,128)(2,1)S(1)}, u32[]{:S(2)}, u32[]{:S(2)}) %collective-permute-start.9) | collective-permute-done | bytes 393248 | tf_op jit(solution)/shard_map/gather_keys_values/ppermute | solution.py:39
  48.4 4.2 %attend_left_row.1 = (f32[2,1024,256]{2,1,0:T(8,128)S(1)}, f32[2,1024,128]{2,1,0:T(8,128)S(1)}) custom-call(s32[4]{0:T(128)S(1)} %select_reduce_fusion.refs_0_, bf16[256,1024]{1,0:T(8,128)(2,1)S(1)} %broadcast_select_fusion.refs_1_, bf16[256,256]{1,0:T(8,128)(2,1)S(1)} %collective-permute-done.5.refs_2_, ...), custom_call_target="tpu_custom_call" | custom-call | flops 1540000000 | bytes 6291456 | tf_op jit(solution)/shard_map/attend_left_row/pallas_call | solution.py:203
  52.6 2.7 %collective-permute-done.15.refs_5_ = bf16[768,256]{1,0:T(8,128)(2,1)S(1)} collective-permute-done((bf16[768,256]{1,0:T(8,128)(2,1)S(1)}, bf16[768,256]{1,0:T(8,128)(2,1)S(1)}, u32[]{:S(2)}, u32[]{:S(2)}) %collective-permute-start.15) | collective-permute-done | bytes 393248 | tf_op jit(solution)/shard_map/gather_keys_values/ppermute | solution.py:39
  55.2 5.4 %attend_far_row_and_project.1 = (bf16[256,1024]{1,0:T(8,128)(2,1)S(1)}, bf16[256,512]{1,0:T(8,128)(2,1)S(1)}, bf16[256,512]{1,0:T(8,128)(2,1)S(1)}) custom-call(s32[4]{0:T(128)S(1)} %select_reduce_fusion.refs_0_, bf16[256,1024]{1,0:T(8,128)(2,1)S(1)} %broadcast_select_fusion.refs_1_, bf16[1024,4096]{1,0:T(8,128)(2,1)S(1)} %bitcast.9, ...), custom_call_target="tpu_custom_call" | custom-call | flops 1660000000 | bytes 6291456 | tf_op jit(solution)/shard_map/attend_far_row_and_project/pallas_call | solution.py:203
  60.8 1.0 %sum_over_heads.2 = bf16[3,256,512]{2,1,0:T(8,128)(2,1)S(1)} custom-call(bf16[256,1024]{1,0:T(8,128)(2,1)S(1)} %get-tuple-element.54.att, bf16[1024,4096]{1,0:T(8,128)(2,1)S(1)} %bitcast.9), custom_call_target="tpu_custom_call" | custom-call | flops 810000000 | bytes 1048576 | tf_op jit(solution)/shard_map/sum_over_heads/pallas_call | solution.py:173
  62.4 1.0 %sum_over_heads.3 = bf16[3,256,512]{2,1,0:T(8,128)(2,1)S(1)} custom-call(bf16[256,1024]{1,0:T(8,128)(2,1)S(1)} %get-tuple-element.54.att, bf16[1024,4096]{1,0:T(8,128)(2,1)S(1)} %bitcast.9), custom_call_target="tpu_custom_call" | custom-call | flops 810000000 | bytes 1048576 | tf_op jit(solution)/shard_map/sum_over_heads/pallas_call | solution.py:173
  63.5 3.3 %collective-permute-start.17 = (bf16[256,512]{1,0:T(8,128)(2,1)S(1)}, bf16[256,512]{1,0:T(8,128)(2,1)S(1)}, u32[]{:S(2)}, u32[]{:S(2)}) collective-permute-start(bf16[256,512]{1,0:T(8,128)(2,1)S(1)} %add_convert_fusion.2), channel_id=1, source_target_pairs={{4,0},{5,1},{6,2},{7,3},{0,4},{1,5},{2,6},{3,7},{12,8},{13,9},{14,... | collective-permute-start | bytes 786440 | tf_op jit(solution)/shard_map/sum_over_heads/ppermute | solution.py:274
  67.7 2.6 %collective-permute-start.20 = (bf16[256,512]{1,0:T(8,128)(2,1)S(1)}, bf16[256,512]{1,0:T(8,128)(2,1)S(1)}, u32[]{:S(2)}, u32[]{:S(2)}) collective-permute-start(bf16[256,512]{1,0:T(8,128)(2,1)S(1)} %get-tuple-element.58), channel_id=1, source_target_pairs={{2,0},{3,1},{4,2},{5,3},{6,4},{7,5},{0,6},{1,7},{10,8},{11,9},{12,... | collective-permute-start | bytes 786440 | tf_op jit(solution)/shard_map/sum_over_heads/ppermute | solution.py:277
  70.2 4.0 %collective-permute-done.17 = bf16[256,512]{1,0:T(8,128)(2,1)S(1)} collective-permute-done((bf16[256,512]{1,0:T(8,128)(2,1)S(1)}, bf16[256,512]{1,0:T(8,128)(2,1)S(1)}, u32[]{:S(2)}, u32[]{:S(2)}) %collective-permute-start.17) | collective-permute-done | bytes 262176 | tf_op jit(solution)/shard_map/sum_over_heads/ppermute | solution.py:274
  74.3 5.0 %collective-permute-done.19 = bf16[256,512]{1,0:T(8,128)(2,1)S(1)} collective-permute-done((bf16[256,512]{1,0:T(8,128)(2,1)S(1)}, bf16[256,512]{1,0:T(8,128)(2,1)S(1)}, u32[]{:S(2)}, u32[]{:S(2)}) %collective-permute-start.19) | collective-permute-done | bytes 262176 | tf_op jit(solution)/shard_map/sum_over_heads/ppermute | solution.py:277
  (39 shorter events, 8.8 us)
Async XLA Ops:
  0.9 12.5 %collective-permute-start.2 = (bf16[256,256]{1,0:T(8,128)(2,1)S(1)}, bf16[256,256]{1,0:T(8,128)(2,1)S(1)}, u32[]{:S(2)}, u32[]{:S(2)}) collective-permute-start(bf16[256,256]{1,0:T(8,128)(2,1)S(1)} %pad_select_fusion.refs_2_), channel_id=1, source_target_pairs={{16,0},{24,8},{32,16},{40,24},{48,32},{56,40},{0,48},{8,56},{80,64... | collective-permute-start | bytes 393224 | tf_op jit(solution)/shard_map/gather_keys_values/ppermute | solution.py:39
  7.3 10.4 %collective-permute-start.3 = (bf16[256,256]{1,0:T(8,128)(2,1)S(1)}, bf16[256,256]{1,0:T(8,128)(2,1)S(1)}, u32[]{:S(2)}, u32[]{:S(2)}) collective-permute-start(bf16[256,256]{1,0:T(8,128)(2,1)S(1)} %pad_select_fusion.refs_2_), channel_id=1, source_target_pairs={{48,0},{56,8},{0,16},{8,24},{16,32},{24,40},{32,48},{40,56},{112,6... | collective-permute-start | bytes 393224 | tf_op jit(solution)/shard_map/gather_keys_values/ppermute | solution.py:39
  7.3 10.4 %collective-permute-start = (bf16[256,256]{1,0:T(8,128)(2,1)S(1)}, bf16[256,256]{1,0:T(8,128)(2,1)S(1)}, u32[]{:S(2)}, u32[]{:S(2)}) collective-permute-start(bf16[256,256]{1,0:T(8,128)(2,1)S(1)} %pad_select_fusion.refs_2_), channel_id=1, source_target_pairs={{8,0},{16,8},{24,16},{32,24},{40,32},{48,40},{56,48},{0,56},{72,64... | collective-permute-start | bytes 393224 | tf_op jit(solution)/shard_map/gather_keys_values/ppermute | solution.py:39
  11.0 8.5 %collective-permute-start.1 = (bf16[256,256]{1,0:T(8,128)(2,1)S(1)}, bf16[256,256]{1,0:T(8,128)(2,1)S(1)}, u32[]{:S(2)}, u32[]{:S(2)}) collective-permute-start(bf16[256,256]{1,0:T(8,128)(2,1)S(1)} %pad_select_fusion.refs_2_), channel_id=1, source_target_pairs={{56,0},{0,8},{8,16},{16,24},{24,32},{32,40},{40,48},{48,56},{120,6... | collective-permute-start | bytes 393224 | tf_op jit(solution)/shard_map/gather_keys_values/ppermute | solution.py:39
  11.0 8.6 %collective-permute-start.4 = (bf16[256,256]{1,0:T(8,128)(2,1)S(1)}, bf16[256,256]{1,0:T(8,128)(2,1)S(1)}, u32[]{:S(2)}, u32[]{:S(2)}) collective-permute-start(bf16[256,256]{1,0:T(8,128)(2,1)S(1)} %pad_select_fusion.refs_2_), channel_id=1, source_target_pairs={{64,0},{72,8},{80,16},{88,24},{96,32},{104,40},{112,48},{120,56},{... | collective-permute-start | bytes 393224 | tf_op jit(solution)/shard_map/gather_keys_values/ppermute | solution.py:39
  13.4 6.1 %collective-permute-start.5 = (bf16[256,256]{1,0:T(8,128)(2,1)S(1)}, bf16[256,256]{1,0:T(8,128)(2,1)S(1)}, u32[]{:S(2)}, u32[]{:S(2)}) collective-permute-start(bf16[256,256]{1,0:T(8,128)(2,1)S(1)} %pad_select_fusion.refs_2_), channel_id=1, source_target_pairs={{192,0},{200,8},{208,16},{216,24},{224,32},{232,40},{240,48},{248,... | collective-permute-start | bytes 393224 | tf_op jit(solution)/shard_map/gather_keys_values/ppermute | solution.py:39
  19.6 17.8 %collective-permute-start.11 = (bf16[1024,256]{1,0:T(8,128)(2,1)S(1)}, bf16[1024,256]{1,0:T(8,128)(2,1)S(1)}, u32[]{:S(2)}, u32[]{:S(2)}) collective-permute-start(bf16[1024,256]{1,0:T(8,128)(2,1)S(1)} %gather_keys_values.2.refs_3_), channel_id=1, source_target_pairs={{64,0},{72,8},{80,16},{88,24},{96,32},{104,40},{112,48},{120,56},{... | collective-permute-start | bytes 1572872 | tf_op jit(solution)/shard_map/gather_keys_values/ppermute | solution.py:39
  20.5 16.9 %collective-permute-start.12 = (bf16[1024,256]{1,0:T(8,128)(2,1)S(1)}, bf16[1024,256]{1,0:T(8,128)(2,1)S(1)}, u32[]{:S(2)}, u32[]{:S(2)}) collective-permute-start(bf16[1024,256]{1,0:T(8,128)(2,1)S(1)} %gather_keys_values.2.refs_3_), channel_id=1, source_target_pairs={{192,0},{200,8},{208,16},{216,24},{224,32},{232,40},{240,48},{248,... | collective-permute-start | bytes 1572872 | tf_op jit(solution)/shard_map/gather_keys_values/ppermute | solution.py:39
  22.9 10.8 %collective-permute-start.7 = (bf16[256,256]{1,0:T(8,128)(2,1)S(1)}, bf16[256,256]{1,0:T(8,128)(2,1)S(1)}, u32[]{:S(2)}, u32[]{:S(2)}) collective-permute-start(bf16[256,256]{1,0:T(8,128)(2,1)S(1)} %broadcast_select_fusion.1), channel_id=1, source_target_pairs={{16,0},{56,8},{32,16},{8,24},{48,32},{24,40},{0,48},{40,56},{80,64... | collective-permute-start | bytes 393224 | tf_op jit(solution)/shard_map/gather_keys_values/ppermute | solution.py:39
  26.5 7.3 %collective-permute-start.6 = (bf16[256,256]{1,0:T(8,128)(2,1)S(1)}, bf16[256,256]{1,0:T(8,128)(2,1)S(1)}, u32[]{:S(2)}, u32[]{:S(2)}) collective-permute-start(bf16[256,256]{1,0:T(8,128)(2,1)S(1)} %collective-permute-done.2.refs_2_), channel_id=1, source_target_pairs={{8,0},{16,8},{24,16},{32,24},{40,32},{48,40},{56,48},{0,56},{72,64... | collective-permute-start | bytes 393224 | tf_op jit(solution)/shard_map/gather_keys_values/ppermute | solution.py:39
  26.5 7.3 %collective-permute-start.8 = (bf16[256,256]{1,0:T(8,128)(2,1)S(1)}, bf16[256,256]{1,0:T(8,128)(2,1)S(1)}, u32[]{:S(2)}, u32[]{:S(2)}) collective-permute-start(bf16[256,256]{1,0:T(8,128)(2,1)S(1)} %collective-permute-done.3.refs_3_), channel_id=1, source_target_pairs={{56,0},{0,8},{8,16},{16,24},{24,32},{32,40},{40,48},{48,56},{120,6... | collective-permute-start | bytes 393224 | tf_op jit(solution)/shard_map/gather_keys_values/ppermute | solution.py:39
  33.8 21.4 %slice-start = ((s8[8388608]{0:T(1024)(128)(4,1)}), s8[4194304]{0:T(1024)(128)(4,1)S(1)}, s32[]{:S(2)}) async-start(s8[8388608]{0:T(1024)(128)(4,1)} %bitcast.8), calls=%async_computation | async-start | bytes 8388608
  33.8 10.8 %collective-permute-start.10 = (bf16[768,256]{1,0:T(8,128)(2,1)S(1)}, bf16[768,256]{1,0:T(8,128)(2,1)S(1)}, u32[]{:S(2)}, u32[]{:S(2)}) collective-permute-start(bf16[768,256]{1,0:T(8,128)(2,1)S(1)} %gather_keys_values.3.refs_2_), channel_id=1, source_target_pairs={{192,0},{200,8},{208,16},{216,24},{224,32},{232,40},{240,48},{248,... | collective-permute-start | bytes 1179656 | tf_op jit(solution)/shard_map/gather_keys_values/ppermute | solution.py:39
  33.9 13.5 %collective-permute-start.9 = (bf16[768,256]{1,0:T(8,128)(2,1)S(1)}, bf16[768,256]{1,0:T(8,128)(2,1)S(1)}, u32[]{:S(2)}, u32[]{:S(2)}) collective-permute-start(bf16[768,256]{1,0:T(8,128)(2,1)S(1)} %gather_keys_values.3.refs_2_), channel_id=1, source_target_pairs={{64,0},{72,8},{80,16},{88,24},{96,32},{104,40},{112,48},{120,56},{... | collective-permute-start | bytes 1179656 | tf_op jit(solution)/shard_map/gather_keys_values/ppermute | solution.py:39
  35.9 8.7 %collective-permute-start.13 = (bf16[256,256]{1,0:T(8,128)(2,1)S(1)}, bf16[256,256]{1,0:T(8,128)(2,1)S(1)}, u32[]{:S(2)}, u32[]{:S(2)}) collective-permute-start(bf16[256,256]{1,0:T(8,128)(2,1)S(1)} %collective-permute-done.5.refs_2_), channel_id=1, source_target_pairs={{192,0},{200,8},{208,16},{216,24},{224,32},{232,40},{240,48},{248,... | collective-permute-start | bytes 393224 | tf_op jit(solution)/shard_map/gather_keys_values/ppermute | solution.py:39
  37.4 17.8 %collective-permute-start.14 = (bf16[1024,256]{1,0:T(8,128)(2,1)S(1)}, bf16[1024,256]{1,0:T(8,128)(2,1)S(1)}, u32[]{:S(2)}, u32[]{:S(2)}) collective-permute-start(bf16[1024,256]{1,0:T(8,128)(2,1)S(1)} %collective-permute-done.11.refs_4_), channel_id=1, source_target_pairs={{64,0},{72,8},{80,16},{88,24},{96,32},{104,40},{112,48},{120,56},{... | collective-permute-start | bytes 1572872 | tf_op jit(solution)/shard_map/gather_keys_values/ppermute | solution.py:39
  47.5 7.8 %slice-start.1 = ((s8[8388608]{0:T(1024)(128)(4,1)}), s8[4194304]{0:T(1024)(128)(4,1)S(1)}, s32[]{:S(2)}) async-start(s8[8388608]{0:T(1024)(128)(4,1)} %bitcast.8), calls=%async_computation.1 | async-start | bytes 8388608
  47.5 7.8 %collective-permute-start.15 = (bf16[768,256]{1,0:T(8,128)(2,1)S(1)}, bf16[768,256]{1,0:T(8,128)(2,1)S(1)}, u32[]{:S(2)}, u32[]{:S(2)}) collective-permute-start(bf16[768,256]{1,0:T(8,128)(2,1)S(1)} %collective-permute-done.10.refs_4_), channel_id=1, source_target_pairs={{192,0},{200,8},{208,16},{216,24},{224,32},{232,40},{240,48},{248,... | collective-permute-start | bytes 1179656 | tf_op jit(solution)/shard_map/gather_keys_values/ppermute | solution.py:39
  60.7 1.6 %collective-permute-start.16 = (bf16[256,512]{1,0:T(8,128)(2,1)S(1)}, bf16[256,512]{1,0:T(8,128)(2,1)S(1)}, u32[]{:S(2)}, u32[]{:S(2)}) collective-permute-start(bf16[256,512]{1,0:T(8,128)(2,1)S(1)} %get-tuple-element.53), channel_id=1, source_target_pairs={{0,1},{1,0},{2,3},{3,2},{4,5},{5,4},{6,7},{7,6},{8,9},{9,8},{10,11... | collective-permute-start | bytes 786440 | tf_op jit(solution)/shard_map/sum_over_heads/ppermute | solution.py:270
  62.3 4.5 %collective-permute-start.18 = (bf16[3,256,512]{2,1,0:T(8,128)(2,1)S(1)}, bf16[3,256,512]{2,1,0:T(8,128)(2,1)S(1)}, u32[]{:S(2)}, u32[]{:S(2)}) collective-permute-start(bf16[3,256,512]{2,1,0:T(8,128)(2,1)S(1)} %sum_over_heads.2), channel_id=1, source_target_pairs={{0,1},{1,0},{2,3},{3,2},{4,5},{5,4},{6,7},{7,6},{8,9},{9,8},{10,11... | collective-permute-start | bytes 2359304 | tf_op jit(solution)/shard_map/sum_over_heads/ppermute | solution.py:273
  63.5 10.8 %collective-permute-start.17 = (bf16[256,512]{1,0:T(8,128)(2,1)S(1)}, bf16[256,512]{1,0:T(8,128)(2,1)S(1)}, u32[]{:S(2)}, u32[]{:S(2)}) collective-permute-start(bf16[256,512]{1,0:T(8,128)(2,1)S(1)} %add_convert_fusion.2), channel_id=1, source_target_pairs={{4,0},{5,1},{6,2},{7,3},{0,4},{1,5},{2,6},{3,7},{12,8},{13,9},{14,... | collective-permute-start | bytes 786440 | tf_op jit(solution)/shard_map/sum_over_heads/ppermute | solution.py:274
  66.9 12.4 %collective-permute-start.19 = (bf16[256,512]{1,0:T(8,128)(2,1)S(1)}, bf16[256,512]{1,0:T(8,128)(2,1)S(1)}, u32[]{:S(2)}, u32[]{:S(2)}) collective-permute-start(bf16[256,512]{1,0:T(8,128)(2,1)S(1)} %get-tuple-element.57), channel_id=1, source_target_pairs={{6,0},{7,1},{0,2},{1,3},{2,4},{3,5},{4,6},{5,7},{14,8},{15,9},{8,1... | collective-permute-start | bytes 786440 | tf_op jit(solution)/shard_map/sum_over_heads/ppermute | solution.py:277
  67.7 12.0 %collective-permute-start.20 = (bf16[256,512]{1,0:T(8,128)(2,1)S(1)}, bf16[256,512]{1,0:T(8,128)(2,1)S(1)}, u32[]{:S(2)}, u32[]{:S(2)}) collective-permute-start(bf16[256,512]{1,0:T(8,128)(2,1)S(1)} %get-tuple-element.58), channel_id=1, source_target_pairs={{2,0},{3,1},{4,2},{5,3},{6,4},{7,5},{0,6},{1,7},{10,8},{11,9},{12,... | collective-permute-start | bytes 786440 | tf_op jit(solution)/shard_map/sum_over_heads/ppermute | solution.py:277

commit v6 on v5

--- a/solution.py
+++ b/solution.py
@@ -250,7 +250,7 @@
         jobs = [(0, [(later, LATER_Z)]), (1, [(right_0, OWN_Z), (right_a, EARLY_Z)])]
         state = attend_to(jobs, ends, q, state)
     with jax.named_scope("gather_keys_values"):
-        right_b, left_b, state, far_0 = lax.optimization_barrier((right_b, left_b, state, far_0))
+        left_b, state, far_0 = lax.optimization_barrier((left_b, state, far_0))
         far_b = ctx(left_b, from_x(-1))
     with jax.named_scope("attend_left_row"):
         jobs = [

time: 80.7 us -> 82.1 us (1.017)
  the two profiles are of different devices: /device:TPU:6 before, /device:TPU:1 now
where the time goes in v6:
time: 82.1 us; the launch traced here: 83.6 us
  starting transfers between devices  30.9 us (38%)
  waiting for transfers between devices  28.6 us (35%)
  Pallas kernels  20.2 us (25%)
  other arithmetic  3.84 us (5%)
    ppermute x16, starting transfers between devices, ctx(): return lax.ppermute(a, 'ctx', perm)  21.4 us
    ppermute x16, waiting for transfers between devices, ctx(): return lax.ppermute(a, 'ctx', perm)  18.8 us
    pallas_call x4, Pallas kernels, attend_to(): pl.pallas_call(functools.partial(attend, jobs, first, last), out_shape=ou...  18.2 us
    ppermute x2, waiting for transfers between devices, on_device(): lax.ppermute(pair(mine[i], theirs[i]), 'tp', from_y(-k)).astype(jnp.float32)  6.04 us
    ppermute x1, waiting for transfers between devices, on_device(): lax.ppermute(pair(mine_2, theirs_2), 'tp', from_y(2)).astype(jnp.float32)  3.52 us
    ppermute x1, starting transfers between devices, on_device(): theirs_2 = lax.ppermute(other_2, 'tp', CORES)  3.34 us
    ppermute x1, starting transfers between devices, on_device(): lax.ppermute(pair(mine_2, theirs_2), 'tp', from_y(2)).astype(jnp.float32)  2.99 us
    ppermute x2, starting transfers between devices, on_device(): lax.ppermute(pair(mine[i], theirs[i]), 'tp', from_y(-k)).astype(jnp.float32)  2.75 us
  transfers between devices with their start and end apart: 21, of which 10 were waited for; matrix products, arithmetic and copies ran while one was open for 2% of the time, Pallas kernels for 18%

profile of v6, /device:TPU:1, one launch (start us, length us, event | category | flops | bytes accessed | tf_op | source)
XLA Modules:
  0.0 83.6 jit_solution(11862806708677707712)
XLA Ops:
  0.9 6.9 %collective-permute-start.2 = (bf16[256,256]{1,0:T(8,128)(2,1)S(1)}, bf16[256,256]{1,0:T(8,128)(2,1)S(1)}, u32[]{:S(2)}, u32[]{:S(2)}) collective-permute-start(bf16[256,256]{1,0:T(8,128)(2,1)S(1)} %pad_select_fusion.refs_2_), channel_id=1, source_target_pairs={{16,0},{24,8},{32,16},{40,24},{48,32},{56,40},{0,48},{8,56},{80,64... | collective-permute-start | bytes 393224 | tf_op jit(solution)/shard_map/gather_keys_values/ppermute | solution.py:39
  7.8 3.1 %collective-permute-start = (bf16[256,256]{1,0:T(8,128)(2,1)S(1)}, bf16[256,256]{1,0:T(8,128)(2,1)S(1)}, u32[]{:S(2)}, u32[]{:S(2)}) collective-permute-start(bf16[256,256]{1,0:T(8,128)(2,1)S(1)} %pad_select_fusion.refs_2_), channel_id=1, source_target_pairs={{8,0},{16,8},{24,16},{32,24},{40,32},{48,40},{56,48},{0,56},{72,64... | collective-permute-start | bytes 393224 | tf_op jit(solution)/shard_map/gather_keys_values/ppermute | solution.py:39
  11.0 2.5 %collective-permute-start.4 = (bf16[256,256]{1,0:T(8,128)(2,1)S(1)}, bf16[256,256]{1,0:T(8,128)(2,1)S(1)}, u32[]{:S(2)}, u32[]{:S(2)}) collective-permute-start(bf16[256,256]{1,0:T(8,128)(2,1)S(1)} %pad_select_fusion.refs_2_), channel_id=1, source_target_pairs={{64,0},{72,8},{80,16},{88,24},{96,32},{104,40},{112,48},{120,56},{... | collective-permute-start | bytes 393224 | tf_op jit(solution)/shard_map/gather_keys_values/ppermute | solution.py:39
  13.5 1.1 %broadcast_select_fusion.refs_1_ = bf16[256,1024]{1,0:T(8,128)(2,1)S(1)} fusion(bf16[256,1024]{1,0:T(8,128)(2,1)} %param.5, pred[]{:T(512)S(6)} %ge.7), kind=kLoop, calls=%fused_computation.5 | loop fusion | flops 262144 | bytes 1048577 | tf_op jit(solution)/shard_map/gather_keys_values/jit(_where)/select_n | solution.py:231
  15.3 1.0 %collective-permute-done.refs_0_ = bf16[256,256]{1,0:T(8,128)(2,1)S(1)} collective-permute-done((bf16[256,256]{1,0:T(8,128)(2,1)S(1)}, bf16[256,256]{1,0:T(8,128)(2,1)S(1)}, u32[]{:S(2)}, u32[]{:S(2)}) %collective-permute-start) | collective-permute-done | bytes 131104 | tf_op jit(solution)/shard_map/gather_keys_values/ppermute | solution.py:39
  16.4 3.6 %collective-permute-done.1.refs_1_ = bf16[256,256]{1,0:T(8,128)(2,1)S(1)} collective-permute-done((bf16[256,256]{1,0:T(8,128)(2,1)S(1)}, bf16[256,256]{1,0:T(8,128)(2,1)S(1)}, u32[]{:S(2)}, u32[]{:S(2)}) %collective-permute-start.1) | collective-permute-done | bytes 131104 | tf_op jit(solution)/shard_map/gather_keys_values/ppermute | solution.py:39
  20.0 2.6 %collective-permute-start.10 = (bf16[1024,256]{1,0:T(8,128)(2,1)S(1)}, bf16[1024,256]{1,0:T(8,128)(2,1)S(1)}, u32[]{:S(2)}, u32[]{:S(2)}) collective-permute-start(bf16[1024,256]{1,0:T(8,128)(2,1)S(1)} %gather_keys_values.2.refs_3_), channel_id=1, source_target_pairs={{64,0},{72,8},{80,16},{88,24},{96,32},{104,40},{112,48},{120,56},{... | collective-permute-start | bytes 1572872 | tf_op jit(solution)/shard_map/gather_keys_values/ppermute | solution.py:39
  22.5 1.4 %collective-permute-start.7 = (bf16[256,256]{1,0:T(8,128)(2,1)S(1)}, bf16[256,256]{1,0:T(8,128)(2,1)S(1)}, u32[]{:S(2)}, u32[]{:S(2)}) collective-permute-start(bf16[256,256]{1,0:T(8,128)(2,1)S(1)} %broadcast_select_fusion.1), channel_id=1, source_target_pairs={{16,0},{56,8},{32,16},{8,24},{48,32},{24,40},{0,48},{40,56},{80,64... | collective-permute-start | bytes 393224 | tf_op jit(solution)/shard_map/gather_keys_values/ppermute | solution.py:39
  24.0 1.5 %collective-permute-start.8 = (bf16[256,256]{1,0:T(8,128)(2,1)S(1)}, bf16[256,256]{1,0:T(8,128)(2,1)S(1)}, u32[]{:S(2)}, u32[]{:S(2)}) collective-permute-start(bf16[256,256]{1,0:T(8,128)(2,1)S(1)} %collective-permute-done.3.refs_3_), channel_id=1, source_target_pairs={{56,0},{0,8},{8,16},{16,24},{24,32},{32,40},{40,48},{48,56},{120,6... | collective-permute-start | bytes 393224 | tf_op jit(solution)/shard_map/gather_keys_values/ppermute | solution.py:39
  25.4 3.9 %attend_own_row_early.1 = (f32[2,1024,256]{2,1,0:T(8,128)S(1)}, f32[2,1024,128]{2,1,0:T(8,128)S(1)}) custom-call(s32[4]{0:T(128)S(1)} %select_reduce_fusion.refs_0_, bf16[256,1024]{1,0:T(8,128)(2,1)S(1)} %broadcast_select_fusion.refs_1_, bf16[256,256]{1,0:T(8,128)(2,1)S(1)} %pad_select_fusion.refs_2_, bf16[1024,256]{1,0:T(8,128)(2,1)S(1)} %gather_keys_values.2.refs_3_), custom_call_target="tpu_custom_call" | custom-call | flops 700000000 | bytes 6291456 | tf_op jit(solution)/shard_map/attend_own_row_early/pallas_call | solution.py:203
  30.8 2.8 %collective-permute-start.15 = (bf16[768,256]{1,0:T(8,128)(2,1)S(1)}, bf16[768,256]{1,0:T(8,128)(2,1)S(1)}, u32[]{:S(2)}, u32[]{:S(2)}) collective-permute-start(bf16[768,256]{1,0:T(8,128)(2,1)S(1)} %gather_keys_values.3.refs_2_), channel_id=1, source_target_pairs={{64,0},{72,8},{80,16},{88,24},{96,32},{104,40},{112,48},{120,56},{... | collective-permute-start | bytes 1179656 | tf_op jit(solution)/shard_map/gather_keys_values/ppermute | solution.py:39
  33.6 2.2 %collective-permute-done.11.refs_3_ = bf16[1024,256]{1,0:T(8,128)(2,1)S(1)} collective-permute-done((bf16[1024,256]{1,0:T(8,128)(2,1)S(1)}, bf16[1024,256]{1,0:T(8,128)(2,1)S(1)}, u32[]{:S(2)}, u32[]{:S(2)}) %collective-permute-start.11) | collective-permute-done | bytes 524320 | tf_op jit(solution)/shard_map/gather_keys_values/ppermute | solution.py:39
  36.3 4.2 %attend_right_row_early.1 = (f32[2,1024,256]{2,1,0:T(8,128)S(1)}, f32[2,1024,128]{2,1,0:T(8,128)S(1)}) custom-call(s32[4]{0:T(128)S(1)} %select_reduce_fusion.refs_0_, bf16[256,1024]{1,0:T(8,128)(2,1)S(1)} %broadcast_select_fusion.refs_1_, bf16[768,256]{1,0:T(8,128)(2,1)S(1)} %gather_keys_values.3.refs_2_, ...), custom_call_target="tpu_custom_call" | custom-call | flops 1120000000 | bytes 6291456 | tf_op jit(solution)/shard_map/attend_right_row_early/pallas_call | solution.py:203
  40.5 6.5 %collective-permute-done.12.refs_3_ = bf16[256,256]{1,0:T(8,128)(2,1)S(1)} collective-permute-done((bf16[256,256]{1,0:T(8,128)(2,1)S(1)}, bf16[256,256]{1,0:T(8,128)(2,1)S(1)}, u32[]{:S(2)}, u32[]{:S(2)}) %collective-permute-start.12) | collective-permute-done | bytes 131104 | tf_op jit(solution)/shard_map/gather_keys_values/ppermute | solution.py:39
  47.0 5.2 %attend_left_row.1 = (f32[2,1024,256]{2,1,0:T(8,128)S(1)}, f32[2,1024,128]{2,1,0:T(8,128)S(1)}) custom-call(s32[4]{0:T(128)S(1)} %select_reduce_fusion.refs_0_, bf16[256,1024]{1,0:T(8,128)(2,1)S(1)} %broadcast_select_fusion.refs_1_, bf16[256,256]{1,0:T(8,128)(2,1)S(1)} %collective-permute-done.5.refs_2_, ...), custom_call_target="tpu_custom_call" | custom-call | flops 1540000000 | bytes 6291456 | tf_op jit(solution)/shard_map/attend_left_row/pallas_call | solution.py:203
  52.2 4.3 %collective-permute-done.14.refs_5_ = bf16[768,256]{1,0:T(8,128)(2,1)S(1)} collective-permute-done((bf16[768,256]{1,0:T(8,128)(2,1)S(1)}, bf16[768,256]{1,0:T(8,128)(2,1)S(1)}, u32[]{:S(2)}, u32[]{:S(2)}) %collective-permute-start.14) | collective-permute-done | bytes 393248 | tf_op jit(solution)/shard_map/gather_keys_values/ppermute | solution.py:39
  56.5 4.9 %attend_far_row_and_project.1 = (bf16[256,1024]{1,0:T(8,128)(2,1)S(1)}, bf16[256,512]{1,0:T(8,128)(2,1)S(1)}, bf16[256,512]{1,0:T(8,128)(2,1)S(1)}) custom-call(s32[4]{0:T(128)S(1)} %select_reduce_fusion.refs_0_, bf16[256,1024]{1,0:T(8,128)(2,1)S(1)} %broadcast_select_fusion.refs_1_, bf16[1024,4096]{1,0:T(8,128)(2,1)S(1)} %bitcast.9, ...), custom_call_target="tpu_custom_call" | custom-call | flops 1660000000 | bytes 6291456 | tf_op jit(solution)/shard_map/attend_far_row_and_project/pallas_call | solution.py:203
  61.4 3.3 %collective-permute-start.16 = (bf16[256,512]{1,0:T(8,128)(2,1)S(1)}, bf16[256,512]{1,0:T(8,128)(2,1)S(1)}, u32[]{:S(2)}, u32[]{:S(2)}) collective-permute-start(bf16[256,512]{1,0:T(8,128)(2,1)S(1)} %get-tuple-element.51), channel_id=1, source_target_pairs={{0,1},{1,0},{2,3},{3,2},{4,5},{5,4},{6,7},{7,6},{8,9},{9,8},{10,11... | collective-permute-start | bytes 786440 | tf_op jit(solution)/shard_map/sum_over_heads/ppermute | solution.py:270
  64.7 1.0 %sum_over_heads.2 = bf16[3,256,512]{2,1,0:T(8,128)(2,1)S(1)} custom-call(bf16[256,1024]{1,0:T(8,128)(2,1)S(1)} %get-tuple-element.52.att, bf16[1024,4096]{1,0:T(8,128)(2,1)S(1)} %bitcast.9), custom_call_target="tpu_custom_call" | custom-call | flops 810000000 | bytes 1048576 | tf_op jit(solution)/shard_map/sum_over_heads/pallas_call | solution.py:173
  66.2 1.0 %sum_over_heads.3 = bf16[3,256,512]{2,1,0:T(8,128)(2,1)S(1)} custom-call(bf16[256,1024]{1,0:T(8,128)(2,1)S(1)} %get-tuple-element.52.att, bf16[1024,4096]{1,0:T(8,128)(2,1)S(1)} %bitcast.9), custom_call_target="tpu_custom_call" | custom-call | flops 810000000 | bytes 1048576 | tf_op jit(solution)/shard_map/sum_over_heads/pallas_call | solution.py:173
  67.3 3.0 %collective-permute-start.17 = (bf16[256,512]{1,0:T(8,128)(2,1)S(1)}, bf16[256,512]{1,0:T(8,128)(2,1)S(1)}, u32[]{:S(2)}, u32[]{:S(2)}) collective-permute-start(bf16[256,512]{1,0:T(8,128)(2,1)S(1)} %add_convert_fusion.2), channel_id=1, source_target_pairs={{4,0},{5,1},{6,2},{7,3},{0,4},{1,5},{2,6},{3,7},{12,8},{13,9},{14,... | collective-permute-start | bytes 786440 | tf_op jit(solution)/shard_map/sum_over_heads/ppermute | solution.py:274
  70.9 2.3 %collective-permute-start.20 = (bf16[256,512]{1,0:T(8,128)(2,1)S(1)}, bf16[256,512]{1,0:T(8,128)(2,1)S(1)}, u32[]{:S(2)}, u32[]{:S(2)}) collective-permute-start(bf16[256,512]{1,0:T(8,128)(2,1)S(1)} %get-tuple-element.56), channel_id=1, source_target_pairs={{2,0},{3,1},{4,2},{5,3},{6,4},{7,5},{0,6},{1,7},{10,8},{11,9},{12,... | collective-permute-start | bytes 786440 | tf_op jit(solution)/shard_map/sum_over_heads/ppermute | solution.py:277
  73.2 3.5 %collective-permute-done.17 = bf16[256,512]{1,0:T(8,128)(2,1)S(1)} collective-permute-done((bf16[256,512]{1,0:T(8,128)(2,1)S(1)}, bf16[256,512]{1,0:T(8,128)(2,1)S(1)}, u32[]{:S(2)}, u32[]{:S(2)}) %collective-permute-start.17) | collective-permute-done | bytes 262176 | tf_op jit(solution)/shard_map/sum_over_heads/ppermute | solution.py:274
  76.7 6.0 %collective-permute-done.19 = bf16[256,512]{1,0:T(8,128)(2,1)S(1)} collective-permute-done((bf16[256,512]{1,0:T(8,128)(2,1)S(1)}, bf16[256,512]{1,0:T(8,128)(2,1)S(1)}, u32[]{:S(2)}, u32[]{:S(2)}) %collective-permute-start.19) | collective-permute-done | bytes 262176 | tf_op jit(solution)/shard_map/sum_over_heads/ppermute | solution.py:277
  (39 shorter events, 5.8 us)
Async XLA Ops:
  0.9 12.5 %collective-permute-start.2 = (bf16[256,256]{1,0:T(8,128)(2,1)S(1)}, bf16[256,256]{1,0:T(8,128)(2,1)S(1)}, u32[]{:S(2)}, u32[]{:S(2)}) collective-permute-start(bf16[256,256]{1,0:T(8,128)(2,1)S(1)} %pad_select_fusion.refs_2_), channel_id=1, source_target_pairs={{16,0},{24,8},{32,16},{40,24},{48,32},{56,40},{0,48},{8,56},{80,64... | collective-permute-start | bytes 393224 | tf_op jit(solution)/shard_map/gather_keys_values/ppermute | solution.py:39
  7.8 7.5 %collective-permute-start.3 = (bf16[256,256]{1,0:T(8,128)(2,1)S(1)}, bf16[256,256]{1,0:T(8,128)(2,1)S(1)}, u32[]{:S(2)}, u32[]{:S(2)}) collective-permute-start(bf16[256,256]{1,0:T(8,128)(2,1)S(1)} %pad_select_fusion.refs_2_), channel_id=1, source_target_pairs={{48,0},{56,8},{0,16},{8,24},{16,32},{24,40},{32,48},{40,56},{112,6... | collective-permute-start | bytes 393224 | tf_op jit(solution)/shard_map/gather_keys_values/ppermute | solution.py:39
  7.8 8.5 %collective-permute-start = (bf16[256,256]{1,0:T(8,128)(2,1)S(1)}, bf16[256,256]{1,0:T(8,128)(2,1)S(1)}, u32[]{:S(2)}, u32[]{:S(2)}) collective-permute-start(bf16[256,256]{1,0:T(8,128)(2,1)S(1)} %pad_select_fusion.refs_2_), channel_id=1, source_target_pairs={{8,0},{16,8},{24,16},{32,24},{40,32},{48,40},{56,48},{0,56},{72,64... | collective-permute-start | bytes 393224 | tf_op jit(solution)/shard_map/gather_keys_values/ppermute | solution.py:39
  11.0 8.9 %collective-permute-start.1 = (bf16[256,256]{1,0:T(8,128)(2,1)S(1)}, bf16[256,256]{1,0:T(8,128)(2,1)S(1)}, u32[]{:S(2)}, u32[]{:S(2)}) collective-permute-start(bf16[256,256]{1,0:T(8,128)(2,1)S(1)} %pad_select_fusion.refs_2_), channel_id=1, source_target_pairs={{56,0},{0,8},{8,16},{16,24},{24,32},{32,40},{40,48},{48,56},{120,6... | collective-permute-start | bytes 393224 | tf_op jit(solution)/shard_map/gather_keys_values/ppermute | solution.py:39
  11.0 9.0 %collective-permute-start.4 = (bf16[256,256]{1,0:T(8,128)(2,1)S(1)}, bf16[256,256]{1,0:T(8,128)(2,1)S(1)}, u32[]{:S(2)}, u32[]{:S(2)}) collective-permute-start(bf16[256,256]{1,0:T(8,128)(2,1)S(1)} %pad_select_fusion.refs_2_), channel_id=1, source_target_pairs={{64,0},{72,8},{80,16},{88,24},{96,32},{104,40},{112,48},{120,56},{... | collective-permute-start | bytes 393224 | tf_op jit(solution)/shard_map/gather_keys_values/ppermute | solution.py:39
  13.4 6.5 %collective-permute-start.5 = (bf16[256,256]{1,0:T(8,128)(2,1)S(1)}, bf16[256,256]{1,0:T(8,128)(2,1)S(1)}, u32[]{:S(2)}, u32[]{:S(2)}) collective-permute-start(bf16[256,256]{1,0:T(8,128)(2,1)S(1)} %pad_select_fusion.refs_2_), channel_id=1, source_target_pairs={{192,0},{200,8},{208,16},{216,24},{224,32},{232,40},{240,48},{248,... | collective-permute-start | bytes 393224 | tf_op jit(solution)/shard_map/gather_keys_values/ppermute | solution.py:39
  20.0 13.6 %collective-permute-start.10 = (bf16[1024,256]{1,0:T(8,128)(2,1)S(1)}, bf16[1024,256]{1,0:T(8,128)(2,1)S(1)}, u32[]{:S(2)}, u32[]{:S(2)}) collective-permute-start(bf16[1024,256]{1,0:T(8,128)(2,1)S(1)} %gather_keys_values.2.refs_3_), channel_id=1, source_target_pairs={{64,0},{72,8},{80,16},{88,24},{96,32},{104,40},{112,48},{120,56},{... | collective-permute-start | bytes 1572872 | tf_op jit(solution)/shard_map/gather_keys_values/ppermute | solution.py:39
  22.5 13.2 %collective-permute-start.11 = (bf16[1024,256]{1,0:T(8,128)(2,1)S(1)}, bf16[1024,256]{1,0:T(8,128)(2,1)S(1)}, u32[]{:S(2)}, u32[]{:S(2)}) collective-permute-start(bf16[1024,256]{1,0:T(8,128)(2,1)S(1)} %gather_keys_values.2.refs_3_), channel_id=1, source_target_pairs={{192,0},{200,8},{208,16},{216,24},{224,32},{232,40},{240,48},{248,... | collective-permute-start | bytes 1572872 | tf_op jit(solution)/shard_map/gather_keys_values/ppermute | solution.py:39
  22.5 6.8 %collective-permute-start.7 = (bf16[256,256]{1,0:T(8,128)(2,1)S(1)}, bf16[256,256]{1,0:T(8,128)(2,1)S(1)}, u32[]{:S(2)}, u32[]{:S(2)}) collective-permute-start(bf16[256,256]{1,0:T(8,128)(2,1)S(1)} %broadcast_select_fusion.1), channel_id=1, source_target_pairs={{16,0},{56,8},{32,16},{8,24},{48,32},{24,40},{0,48},{40,56},{80,64... | collective-permute-start | bytes 393224 | tf_op jit(solution)/shard_map/gather_keys_values/ppermute | solution.py:39
  24.0 6.0 %collective-permute-start.6 = (bf16[256,256]{1,0:T(8,128)(2,1)S(1)}, bf16[256,256]{1,0:T(8,128)(2,1)S(1)}, u32[]{:S(2)}, u32[]{:S(2)}) collective-permute-start(bf16[256,256]{1,0:T(8,128)(2,1)S(1)} %collective-permute-done.2.refs_2_), channel_id=1, source_target_pairs={{8,0},{16,8},{24,16},{32,24},{40,32},{48,40},{56,48},{0,56},{72,64... | collective-permute-start | bytes 393224 | tf_op jit(solution)/shard_map/gather_keys_values/ppermute | solution.py:39
  24.0 6.7 %collective-permute-start.8 = (bf16[256,256]{1,0:T(8,128)(2,1)S(1)}, bf16[256,256]{1,0:T(8,128)(2,1)S(1)}, u32[]{:S(2)}, u32[]{:S(2)}) collective-permute-start(bf16[256,256]{1,0:T(8,128)(2,1)S(1)} %collective-permute-done.3.refs_3_), channel_id=1, source_target_pairs={{56,0},{0,8},{8,16},{16,24},{24,32},{32,40},{40,48},{48,56},{120,6... | collective-permute-start | bytes 393224 | tf_op jit(solution)/shard_map/gather_keys_values/ppermute | solution.py:39
  30.6 25.9 %slice-start = ((s8[8388608]{0:T(1024)(128)(4,1)}), s8[4194304]{0:T(1024)(128)(4,1)S(1)}, s32[]{:S(2)}) async-start(s8[8388608]{0:T(1024)(128)(4,1)} %bitcast.8), calls=%async_computation | async-start | bytes 8388608
  30.7 16.3 %collective-permute-start.9 = (bf16[768,256]{1,0:T(8,128)(2,1)S(1)}, bf16[768,256]{1,0:T(8,128)(2,1)S(1)}, u32[]{:S(2)}, u32[]{:S(2)}) collective-permute-start(bf16[768,256]{1,0:T(8,128)(2,1)S(1)} %gather_keys_values.3.refs_2_), channel_id=1, source_target_pairs={{192,0},{200,8},{208,16},{216,24},{224,32},{232,40},{240,48},{248,... | collective-permute-start | bytes 1179656 | tf_op jit(solution)/shard_map/gather_keys_values/ppermute | solution.py:39
  30.8 16.2 %collective-permute-start.15 = (bf16[768,256]{1,0:T(8,128)(2,1)S(1)}, bf16[768,256]{1,0:T(8,128)(2,1)S(1)}, u32[]{:S(2)}, u32[]{:S(2)}) collective-permute-start(bf16[768,256]{1,0:T(8,128)(2,1)S(1)} %gather_keys_values.3.refs_2_), channel_id=1, source_target_pairs={{64,0},{72,8},{80,16},{88,24},{96,32},{104,40},{112,48},{120,56},{... | collective-permute-start | bytes 1179656 | tf_op jit(solution)/shard_map/gather_keys_values/ppermute | solution.py:39
  33.6 13.4 %collective-permute-start.12 = (bf16[256,256]{1,0:T(8,128)(2,1)S(1)}, bf16[256,256]{1,0:T(8,128)(2,1)S(1)}, u32[]{:S(2)}, u32[]{:S(2)}) collective-permute-start(bf16[256,256]{1,0:T(8,128)(2,1)S(1)} %collective-permute-done.5.refs_2_), channel_id=1, source_target_pairs={{192,0},{200,8},{208,16},{216,24},{224,32},{232,40},{240,48},{248,... | collective-permute-start | bytes 393224 | tf_op jit(solution)/shard_map/gather_keys_values/ppermute | solution.py:39
  35.7 20.7 %collective-permute-start.13 = (bf16[1024,256]{1,0:T(8,128)(2,1)S(1)}, bf16[1024,256]{1,0:T(8,128)(2,1)S(1)}, u32[]{:S(2)}, u32[]{:S(2)}) collective-permute-start(bf16[1024,256]{1,0:T(8,128)(2,1)S(1)} %collective-permute-done.10.refs_4_), channel_id=1, source_target_pairs={{64,0},{72,8},{80,16},{88,24},{96,32},{104,40},{112,48},{120,56},{... | collective-permute-start | bytes 1572872 | tf_op jit(solution)/shard_map/gather_keys_values/ppermute | solution.py:39
  47.0 9.5 %slice-start.1 = ((s8[8388608]{0:T(1024)(128)(4,1)}), s8[4194304]{0:T(1024)(128)(4,1)S(1)}, s32[]{:S(2)}) async-start(s8[8388608]{0:T(1024)(128)(4,1)} %bitcast.8), calls=%async_computation.1 | async-start | bytes 8388608
  47.0 9.5 %collective-permute-start.14 = (bf16[768,256]{1,0:T(8,128)(2,1)S(1)}, bf16[768,256]{1,0:T(8,128)(2,1)S(1)}, u32[]{:S(2)}, u32[]{:S(2)}) collective-permute-start(bf16[768,256]{1,0:T(8,128)(2,1)S(1)} %collective-permute-done.9.refs_4_), channel_id=1, source_target_pairs={{192,0},{200,8},{208,16},{216,24},{224,32},{232,40},{240,48},{248,... | collective-permute-start | bytes 1179656 | tf_op jit(solution)/shard_map/gather_keys_values/ppermute | solution.py:39
  61.4 4.5 %collective-permute-start.16 = (bf16[256,512]{1,0:T(8,128)(2,1)S(1)}, bf16[256,512]{1,0:T(8,128)(2,1)S(1)}, u32[]{:S(2)}, u32[]{:S(2)}) collective-permute-start(bf16[256,512]{1,0:T(8,128)(2,1)S(1)} %get-tuple-element.51), channel_id=1, source_target_pairs={{0,1},{1,0},{2,3},{3,2},{4,5},{5,4},{6,7},{7,6},{8,9},{9,8},{10,11... | collective-permute-start | bytes 786440 | tf_op jit(solution)/shard_map/sum_over_heads/ppermute | solution.py:270
  65.9 4.4 %collective-permute-start.18 = (bf16[3,256,512]{2,1,0:T(8,128)(2,1)S(1)}, bf16[3,256,512]{2,1,0:T(8,128)(2,1)S(1)}, u32[]{:S(2)}, u32[]{:S(2)}) collective-permute-start(bf16[3,256,512]{2,1,0:T(8,128)(2,1)S(1)} %sum_over_heads.2), channel_id=1, source_target_pairs={{0,1},{1,0},{2,3},{3,2},{4,5},{5,4},{6,7},{7,6},{8,9},{9,8},{10,11... | collective-permute-start | bytes 2359304 | tf_op jit(solution)/shard_map/sum_over_heads/ppermute | solution.py:273
  67.3 9.4 %collective-permute-start.17 = (bf16[256,512]{1,0:T(8,128)(2,1)S(1)}, bf16[256,512]{1,0:T(8,128)(2,1)S(1)}, u32[]{:S(2)}, u32[]{:S(2)}) collective-permute-start(bf16[256,512]{1,0:T(8,128)(2,1)S(1)} %add_convert_fusion.2), channel_id=1, source_target_pairs={{4,0},{5,1},{6,2},{7,3},{0,4},{1,5},{2,6},{3,7},{12,8},{13,9},{14,... | collective-permute-start | bytes 786440 | tf_op jit(solution)/shard_map/sum_over_heads/ppermute | solution.py:274
  70.4 12.3 %collective-permute-start.19 = (bf16[256,512]{1,0:T(8,128)(2,1)S(1)}, bf16[256,512]{1,0:T(8,128)(2,1)S(1)}, u32[]{:S(2)}, u32[]{:S(2)}) collective-permute-start(bf16[256,512]{1,0:T(8,128)(2,1)S(1)} %get-tuple-element.55), channel_id=1, source_target_pairs={{6,0},{7,1},{0,2},{1,3},{2,4},{3,5},{4,6},{5,7},{14,8},{15,9},{8,1... | collective-permute-start | bytes 786440 | tf_op jit(solution)/shard_map/sum_over_heads/ppermute | solution.py:277
  70.9 11.8 %collective-permute-start.20 = (bf16[256,512]{1,0:T(8,128)(2,1)S(1)}, bf16[256,512]{1,0:T(8,128)(2,1)S(1)}, u32[]{:S(2)}, u32[]{:S(2)}) collective-permute-start(bf16[256,512]{1,0:T(8,128)(2,1)S(1)} %get-tuple-element.56), channel_id=1, source_target_pairs={{2,0},{3,1},{4,2},{5,3},{6,4},{7,5},{0,6},{1,7},{10,8},{11,9},{12,... | collective-permute-start | bytes 786440 | tf_op jit(solution)/shard_map/sum_over_heads/ppermute | solution.py:277
